TPU v7x, 512 devices: a whole 4x8x8 slice. The times are simulated.
512 devices in a mesh: seq: 64 (over x, z_lo, y), tensor: 8 (over z_hi, core).
Axes of the slice: x: 4, y: 8, z: 8 (z_hi: 4, z_lo: 2; z = z_hi * 2 + z_lo), core: 2. Of those that a mesh axis runs over, the one named last changes fastest.
Arguments:
- tokens: bfloat16 [2, 8192, 4096], P(None, 'seq', 'tensor'), may hold values from -6 to 6
- in_weight: bfloat16 [4096, 3, 4096], P('seq', None, 'tensor'), may hold values from -0.09375 to 0.09375
- adapter_down_factors: bfloat16 [8, 4096, 16], P(None, 'tensor'), may hold values from -0.09375 to 0.09375
- adapter_up_factors: bfloat16 [8, 16, 3, 4096], P(None, None, None, 'tensor'), may hold values from -1.5 to 1.5
- filters: bfloat16 [4096, 128], P('tensor'), may hold values from -6 to 6
- task_ids: int32 [2], replicated, may hold values from 0 to 7
- window_lengths: int32 [2, 32], replicated, may hold values from 1 to 512, 8192 in all within a row
- out_weight: bfloat16 [4096, 4096], P('tensor', 'seq'), may hold values from -0.75 to 0.75
Outputs:
- embeddings: bfloat16 [2, 32, 4096], P(None, 'tensor', 'seq')
Inputs may be any that keep to these rules, and one draw needn't show every extreme that they name: `window_lengths`: each segment's window lengths sum to 8192, and the longest window of each segment has exactly 512 tokens.
All inputs are finite; a program needn't handle non-finite values.
Results may differ from a plain program's by a relative error of at most 0.014.
Values may be sent and summed in bfloat16 or wider, within the bound.
No kernel may reach another device: no remote copies, remote signals or barrier semaphores. Data moves between devices by JAX's collectives and lax.ppermute only.
A program may use at most 128 MiB of HBM per device.

v0:
```python
import jax
import jax.numpy as jnp
from jax import lax
from jax.sharding import PartitionSpec as P

adapter_scale = 0.5


def shifted(value, axis, steps):
    count = lax.axis_size(axis)
    leading, last = (max(0, -steps), min(count, count - steps))
    return lax.ppermute(value, axis, [(source, source + steps) for source in range(leading, last)])


def tap_conv(extended, filters, out_rows):
    tap_count = filters.shape[1]
    filter_cols = filters.astype(jnp.float32).T
    result = None
    for tap in range(tap_count):
        begin = tap_count - 1 - tap
        term = (
            extended[:, begin : begin + out_rows].astype(jnp.float32)
            * filter_cols[tap][None, None, :]
        )
        result = term if result is None else result + term
    return result


def local(
    tokens,
    in_weight,
    adapter_down_factors,
    adapter_up_factors,
    filters,
    task_ids,
    window_lengths,
    out_weight,
):
    seg_count, row_count = (tokens.shape[0], tokens.shape[1])
    channels = in_weight.shape[2]
    tap_count = filters.shape[1]
    gathered_rows = lax.all_gather(tokens, "tensor", axis=2, tiled=True)
    flat_tokens = gathered_rows.reshape(seg_count * row_count, gathered_rows.shape[2])
    full_weight = lax.all_gather(in_weight, "seq", axis=0, tiled=True)
    base_projection_output = jnp.dot(
        flat_tokens,
        full_weight.reshape(full_weight.shape[0], 3 * channels),
        preferred_element_type=jnp.float32,
    )
    base_projection_output = base_projection_output.reshape(seg_count, row_count, 3, channels)
    down_sel = jnp.stack(
        [
            lax.dynamic_index_in_dim(adapter_down_factors, task_ids[segment], 0, keepdims=False)
            for segment in range(seg_count)
        ]
    )
    selected_up_factor = jnp.stack(
        [
            lax.dynamic_index_in_dim(adapter_up_factors, task_ids[segment], 0, keepdims=False)
            for segment in range(seg_count)
        ]
    )
    down_factor_full = lax.all_gather(down_sel, "tensor", axis=1, tiled=True)
    low_rank_rows = jnp.einsum(
        "oan,onj->oaj", gathered_rows, down_factor_full, preferred_element_type=jnp.float32
    )
    low_rank_rows = low_rank_rows.astype(jnp.bfloat16)
    lifted_rows = jnp.einsum(
        "slr,srkc->slkc", low_rank_rows, selected_up_factor, preferred_element_type=jnp.float32
    )
    projected_output = base_projection_output + adapter_scale * lifted_rows
    queries = projected_output[:, :, 0]
    kv_product = (projected_output[:, :, 1] * projected_output[:, :, 2]).astype(jnp.bfloat16)
    tail_rows = kv_product[:, row_count - (tap_count - 1) :]
    previous = shifted(tail_rows, "seq", 1)
    extended = jnp.concatenate([previous, kv_product], axis=1)
    conv = tap_conv(extended, filters, row_count)
    gated = (queries * conv).astype(jnp.bfloat16)
    positions = lax.axis_index("seq") * row_count + jnp.arange(row_count, dtype=jnp.int32)
    window_ends = jnp.cumsum(window_lengths, axis=1, dtype=jnp.int32)
    window_starts = window_ends - window_lengths
    membership = (
        (positions[None, None, :] >= window_starts[:, :, None])
        & (positions[None, None, :] < window_ends[:, :, None])
    ).astype(jnp.bfloat16)
    local_total = jnp.einsum("swl,slc->swc", membership, gated, preferred_element_type=jnp.float32)
    window_total = lax.psum(local_total, "seq")
    averages = (window_total / window_lengths[:, :, None].astype(jnp.float32)).astype(jnp.bfloat16)
    embedding_terms = jnp.einsum(
        "swc,cd->swd", averages, out_weight, preferred_element_type=jnp.float32
    )
    return lax.psum_scatter(embedding_terms, "tensor", scatter_dimension=1, tiled=True).astype(
        jnp.bfloat16
    )


def solution(mesh):
    in_specs = (
        P(None, "seq", "tensor"),
        P("seq", None, "tensor"),
        P(None, "tensor", None),
        P(None, None, None, "tensor"),
        P("tensor", None),
        P(),
        P(),
        P("tensor", "seq"),
    )
    out_specs = P(None, "tensor", "seq")
    return jax.shard_map(local, mesh=mesh, in_specs=in_specs, out_specs=out_specs, check_vma=False)
```

profile of v0, /device:TPU:1, one launch (start us, length us, event | category | flops | bytes accessed | tf_op | source)
XLA Modules:
  0.0 1015.9 jit_solution(686923856574689766)
XLA Ops:
  8.1 1.3 fusion.154
  13.2 0.7 constant_dynamic-slice_fusion.3
  13.9 0.8 constant_dynamic-slice_fusion.1
  14.7 21.6 %all_gather.11 = bf16[2,4096,16]{1,2,0:T(8,128)(2,1)S(1)} all-gather(bf16[2,512,16]{1,2,0:T(8,128)(2,1)S(1)} %pad_maximum_fusion.1), channel_id=1, replica_groups=mesh['seq'=64,'tensor'=8] {'tensor'}, dimensions={1}, use_global_device_ids=true | all-gather | bytes 294912 | tf_op jit(solution)/shard_map/all_gather | solution.py:63
  36.3 0.9 convert_bitcast_fusion
  37.3 1.9 slice_reduce_fusion.119
  39.2 3.3 slice_reduce_fusion.125
  42.5 3.3 slice_reduce_fusion.120
  45.8 3.3 slice_reduce_fusion.124
  49.0 3.3 slice_reduce_fusion.123
  52.3 3.7 slice_reduce_fusion.122
  56.1 3.3 slice_reduce_fusion.121
  59.3 3.8 fusion.8
  63.1 277.6 %all-gather.5.cloned.1.call-done = bf16[4096,3,512]{2,0,1:T(8,128)(2,1)} async-done(((bf16[64,3,512]{2,0,1:T(8,128)(2,1)}), bf16[4096,3,512]{2,0,1:T(8,128)(2,1)}) %all-gather.5.cloned.1.call-update) | async-done | bytes 12582928 | tf_op jit(solution)/shard_map/all_gather | solution.py:44
  340.8 17.0 %copy.12 = bf16[4096,3,512]{0,2,1:T(8,128)(2,1)} copy(bf16[4096,3,512]{2,0,1:T(8,128)(2,1)} %all-gather.5.cloned.1.call-done) | data formatting | bytes 25165824 | tf_op jit(solution)/shard_map/all_gather | solution.py:44
  357.7 7.1 multiply_add_fusion
  365.0 1.0 copy-done.2
  366.0 1.5 collective-permute-start
  368.9 2.0 collective-permute-done
  374.1 1.3 fusion.78
  375.4 1.5 fusion.87
  376.9 1.5 fusion.96
  378.5 1.5 fusion.105
  380.0 1.5 fusion.114
  381.5 1.5 fusion.123
  383.3 1.5 fusion.132
  385.2 19.2 %fusion.11 = bf16[2,128,512]{2,1,0:T(8,128)(2,1)S(1)} fusion(f32[2,128,3,512]{3,1,2,0:T(8,128)} %copy-done.2, bf16[2,128,512]{2,1,0:T(8,128)(2,1)} %get-tuple-element.259, bf16[2,128,512]{2,1,0:T(8,128)(2,1)} %get-tuple-element.260, bf16[2,128,512]{2,1,0:T(8,128)(2,1)} %get-tuple-element.258, bf16[2,128,512]{2,1,0:T(8,128)(2,1)} %get-tuple-element.257, ...), kind=kLoop, calls=%fused_computation.263 | loop fusion | flops 50593792 | bytes 35123200 | tf_op jit(solution)/shard_map/convert_element_type | solution.py:78
  404.4 1.5 fusion.144
  406.0 1.3 dynamic-slice
  407.9 546.7 %all-reduce.3.cloned.1.call-done = f32[2,32,512]{2,1,0:T(8,128)} async-done(((f32[2,32,512]{2,1,0:T(8,128)}), f32[2,32,512]{2,1,0:T(8,128)}) %all-reduce.3.cloned.1.call-update) | async-done | bytes 131088 | tf_op jit(solution)/shard_map/psum | solution.py:87
  954.5 1.1 fusion.142
  955.7 52.9 %all-reduce = bf16[2,32,64]{2,1,0:T(8,128)(2,1)S(1)} all-reduce(f32[2,32,64]{2,1,0:T(8,128)S(1)} %fusion.142), channel_id=2, replica_groups=mesh['seq'=64,'tensor'=8] {'tensor'}, use_global_device_ids=true, to_apply=%region_2.3.clone | all-reduce | flops 4096 | bytes 24576
  (96 shorter events, 6.9 us)
Async XLA Ops:
  6.5 948.0 %copy-start = (bf16[512,64]{0,1:T(8,128)(2,1)S(1)}, bf16[512,64]{0,1:T(8,128)(2,1)}, u32[]{:S(2)}) copy-start(bf16[512,64]{0,1:T(8,128)(2,1)} %param.15) | copy-start | bytes 196612
  6.5 52.8 %all-gather.3.cloned.1.call-start = ((), (), s32[]{:S(2)}) async-start(), calls=%async_computation | async-start | bytes 2359296 | tf_op jit(solution)/shard_map/all_gather | solution.py:42
  7.3 333.5 %all-gather.5.cloned.1.call-start = ((), (), s32[]{:S(2)}) async-start(), calls=%async_computation.1 | async-start | bytes 12779520 | tf_op jit(solution)/shard_map/all_gather | solution.py:44
  8.0 946.5 %all-reduce.3.cloned.1.call-start = ((), (), s32[]{:S(2)}) async-start(), calls=%async_computation.2 | async-start | bytes 262144 | tf_op jit(solution)/shard_map/psum | solution.py:87
  63.1 294.6 %copy-start.1 = (bf16[2,128,4096]{2,1,0:T(8,128)(2,1)S(1)}, bf16[2,128,4096]{2,1,0:T(8,128)(2,1)}, u32[]{:S(2)}) copy-start(bf16[2,128,4096]{2,1,0:T(8,128)(2,1)} %all-gather.3.cloned.1.call-done) | copy-start | bytes 6291460
  364.8 3.3 copy-start.37
  366.0 4.9 collective-permute-start
  383.0 1.8 copy-start.4
  383.0 1.8 copy-start.5
  383.0 1.8 copy-start.6
  383.0 1.8 copy-start.7
  383.0 1.8 copy-start.8
  383.1 1.8 copy-start.9
  383.1 1.8 copy-start.10
  383.1 1.8 copy-start.11
  383.1 1.8 copy-start.12
  383.1 1.8 copy-start.13
  383.1 1.8 copy-start.14
  383.1 1.8 copy-start.15
  383.1 1.8 copy-start.16
  383.1 1.8 copy-start.17
  383.1 1.8 copy-start.18
  383.2 1.8 copy-start.19
  383.2 1.8 copy-start.20
  383.2 1.8 copy-start.21
  383.2 1.8 copy-start.22
  383.2 1.8 copy-start.23
  383.2 1.8 copy-start.24
  383.2 1.8 copy-start.25
  383.2 1.8 copy-start.26
  383.2 1.8 copy-start.27
  383.2 1.8 copy-start.28
  (10 other events, 17.7 us)
Sparse Core Ops, SparseCore 0:
  9.5 46.1 all-gather.2
  57.8 282.9 all-gather.4
  406.1 548.4 all-reduce.2
where the time goes:
time: 1030 us; the launch traced here: 1020 us
  waiting for transfers between devices  828 us (80%)
  blocking collectives  74.5 us (7%)
  local copies, waits for them, and re-layouts  45 us (4%)
  other arithmetic  35.2 us (3%)
  between operations  18.4 us (2%)
  matrix products  13.5 us (1%)
    psum x1, waiting for transfers between devices, local(): window_total = lax.psum(local_total, 'seq')  547 us
    all_gather x1, waiting for transfers between devices, local(): full_weight = lax.all_gather(in_weight, 'seq', axis=0, tiled=True)  278 us
    unnamed x1, blocking collectives  52.9 us
    slice x7, local copies, waits for them, and re-layouts, tap_conv(): filter_cols[tap][None, None, :]  22.1 us
    all_gather x1, blocking collectives, local(): down_factor_full = lax.all_gather(down_sel, 'tensor', axis=1, tiled=True)  21.6 us
  transfers between devices with their start and end apart: 4, of which 3 were waited for; matrix products, arithmetic and copies ran while one was open for 3% of the time, Pallas kernels for 0%

commit v1 on v0

v1 whole, which is shorter than its diff:
```python
import functools
import jax
import jax.numpy as jnp
from jax import lax
from jax.experimental import pallas as pl
from jax.experimental.pallas import tpu as pltpu
from jax.sharding import Mesh, PartitionSpec as P

AXES = ("xhi", "xlo", "zlo", "y", "zhi", "core")
SIZES = (2, 2, 2, 8, 4, 2)
SEQ = ("xhi", "xlo", "zlo", "y")
TENSOR = ("zhi", "core")
NZ, NY = 8, 8
adapter_scale = 0.5


def flat(x, y, z, c):
    return (((x % 4) * 2 + (z % NZ) % 2) * NY + y % NY) * 8 + ((z % NZ) // 2) * 2 + c


def permute(value, move, keep=lambda x, y, z, c: True):
    pairs = [
        (flat(x, y, z, c), flat(*move(x, y, z, c)))
        for x in range(4)
        for y in range(NY)
        for z in range(NZ)
        for c in range(2)
        if keep(x, y, z, c)
    ]
    return lax.ppermute(value, AXES, pairs)


def z_step(value, step):
    return permute(value, lambda x, y, z, c: (x, y, z + step, c))


def core_swap(value):
    return permute(value, lambda x, y, z, c: (x, y, z, 1 - c))


def x_pair_swap(value):
    return permute(value, lambda x, y, z, c: (x ^ 1, y, z, c))


def nt_dot(a, b):
    return lax.dot_general(a, b, (((1,), (1,)), ((), ())), preferred_element_type=jnp.float32)


def project_kernel(dists, place, *refs):
    n = len(dists)
    pieces = [refs[2 * i : 2 * i + 2] for i in range(n)]
    weight, up, q_ref, kv_ref, acc, low = refs[2 * n :]
    z, zlo, core = place[0], place[1], place[2]
    half = acc.shape[1] // 2
    ranks = up.shape[0]
    started = set()
    for i, (dist, part) in enumerate(dists):
        rel = dist % 2
        zhi = lax.rem(z + dist, NZ) // 2
        for other in range(2):
            piece = pieces[i][other]
            block = zhi * 2 + (core if other == 0 else 1 - core)
            b = weight[:, pl.ds(block, 1)].reshape(NY * weight.shape[2], weight.shape[3])
            halves = (0, 1) if part is None else (part,)
            if piece.shape[0] > half * len(halves):
                down = piece[half * len(halves) :, :]
                down_of = down
            else:
                down_of = pieces[i + 1][other][half:, :]
            for k, xlo in enumerate(halves):
                rows = piece[half * k : half * (k + 1), :]
                at = pl.ds(half * xlo, half)
                prod = jnp.dot(rows, b, preferred_element_type=jnp.float32)
                lprod = nt_dot(rows, down_of)
                if (rel, xlo) in started:
                    acc[rel, at, :] += prod
                    low[rel, at, :] += lprod
                else:
                    started.add((rel, xlo))
                    acc[rel, at, :] = prod
                    low[rel, at, :] = lprod
    seg_rows = q_ref.shape[2]
    ch = q_ref.shape[3]
    for rel in range(2):
        zlo_at = zlo if rel == 0 else 1 - zlo
        for xlo in range(2):
            for seg in range(2):
                at = pl.ds(half * xlo + seg_rows * seg, seg_rows)
                column = lax.broadcasted_iota(jnp.int32, (seg_rows, ranks), 1)
                mine = column // (ranks // 2) == seg
                lowered = jnp.where(mine, low[rel, at, :], 0.0).astype(jnp.bfloat16)
                lifted = jnp.dot(lowered, up[...], preferred_element_type=jnp.float32)
                proj = acc[rel, at, :] + adapter_scale * lifted
                q_ref[xlo * 2 + zlo_at, seg] = proj[:, :ch]
                kv = proj[:, ch : 2 * ch] * proj[:, 2 * ch :]
                kv_ref[xlo * 2 + zlo_at, seg] = kv.astype(jnp.bfloat16)


def conv_kernel(place, q_ref, kv_ref, prev_ref, wrap_ref, taps_ref, start_ref, end_ref, out_ref, ext):
    xhi, y = place[0], place[1]
    rows, ch = kv_ref.shape[2], kv_ref.shape[3]
    taps = taps_ref.shape[0]
    out_ref[...] = jnp.zeros_like(out_ref)
    count = out_ref.shape[1]

    def block(n, carry):
        quarter, seg = n // 2, lax.rem(n, 2)
        at = jnp.where(y > 0, quarter, jnp.maximum(quarter - 1, 0))
        before = prev_ref[at, seg].astype(jnp.float32)
        wrapped = wrap_ref[seg].astype(jnp.float32)
        before = jnp.where((y == 0) & (quarter == 0), wrapped, before)
        ext[0, 0:8, :] = jnp.zeros((8, ch), jnp.float32)
        ext[0, 8 : 8 + rows, :] = before
        ext[0, 8 + rows :, :] = kv_ref[quarter, seg].astype(jnp.float32)
        for r in range(1, 8):
            ext[r, 8:, :] = ext[0, 8 - r : 8 - r + 2 * rows, :]
        for half in range(2):
            height = rows // 2
            total = jnp.zeros((height, ch), jnp.float32)
            for r in range(8):
                for s in range(taps // 8):
                    begin = 8 + rows + height * half - 8 * s
                    total = total + taps_ref[8 * s + r, :][None, :] * ext[r, begin : begin + height, :]
            gated = (q_ref[quarter, seg, height * half : height * (half + 1), :] * total).astype(jnp.bfloat16)
            x = xhi * 2 + quarter // 2
            base = ((x * 2 + lax.rem(quarter, 2)) * NY + y) * rows + height * half
            position = base + lax.broadcasted_iota(jnp.int32, (count, height), 1)
            inside = (position >= start_ref[seg]) & (position < end_ref[seg])
            member = inside.astype(jnp.float32).astype(jnp.bfloat16)
            out_ref[seg] += jnp.dot(member, gated, preferred_element_type=jnp.float32)
        return carry

    lax.fori_loop(0, 8, block, 0)


VMEM = pl.BlockSpec(memory_space=pltpu.VMEM)
SMEM = pl.BlockSpec(memory_space=pltpu.SMEM)


def local(tokens, in_weight, down_factors, up_factors, filters, task_ids, window_lengths, out_weight):
    segs, rows, depth = tokens.shape
    w_rows, _, channels = in_weight.shape
    ch = channels // 4
    xhi, xlo, zlo, y, zhi, core = (lax.axis_index(name) for name in AXES)
    quarter = xlo * 2 + zlo
    z = zhi * 2 + zlo

    by_quarter = in_weight.reshape(w_rows, 3, 4, ch).transpose(2, 0, 1, 3).reshape(4, w_rows, 3 * ch)
    spread = jnp.concatenate([by_quarter, by_quarter], axis=0)
    met = lax.all_to_all(spread, ("xhi", "xlo", "zlo"), 0, 0, tiled=True)
    weight = lax.all_gather(met, "y", axis=0, tiled=False)

    down = jnp.concatenate(
        [lax.dynamic_index_in_dim(down_factors, task_ids[s], 0, keepdims=False).T for s in range(segs)]
    )
    own = tokens.reshape(segs * rows, depth)
    other = x_pair_swap(own)
    first = xlo == 0
    piece = jnp.concatenate([jnp.where(first, own, other), jnp.where(first, other, own), down])
    half = segs * rows
    dists, held = [(0, None)], [piece]
    ahead = back = piece
    for step in range(1, NZ // 2):
        ahead, back = z_step(ahead, 1), z_step(back, -1)
        dists += [(NZ - step, None), (step, None)]
        held += [ahead, back]
    dists += [(NZ // 2, 0), (NZ // 2, 1)]
    held += [z_step(ahead[:half], 1), z_step(back[half:], -1)]
    swapped = [core_swap(h) for h in held]

    up = jnp.concatenate(
        [lax.dynamic_index_in_dim(up_factors, task_ids[s], 0, keepdims=False) for s in range(segs)]
    )
    up = lax.dynamic_slice_in_dim(up, quarter * ch, ch, 2).reshape(up.shape[0], 3 * ch)
    place = jnp.stack([z, zlo, core]).astype(jnp.int32)
    q, kv = pl.pallas_call(
        functools.partial(project_kernel, dists),
        out_shape=(
            jax.ShapeDtypeStruct((4, segs, rows, ch), jnp.float32),
            jax.ShapeDtypeStruct((4, segs, rows, ch), jnp.bfloat16),
        ),
        in_specs=[SMEM] + [VMEM] * (2 * len(held) + 2),
        out_specs=(VMEM, VMEM),
        scratch_shapes=[
            pltpu.VMEM((2, 2 * half, 3 * ch), jnp.float32),
            pltpu.VMEM((2, 2 * half, up.shape[0]), jnp.float32),
        ],
        compiler_params=pltpu.CompilerParams(vmem_limit_bytes=40 << 20),
        name="project",
    )(place, *[ref for pair in zip(held, swapped) for ref in pair], weight, up)

    prev = permute(kv, lambda x, y, z, c: (x, y + 1, z, c))
    wrap = lax.ppermute(
        kv[3],
        AXES,
        [
            (flat(xl, NY - 1, zz, c), flat(2 + xl, 0, zz, c))
            for xl in range(2)
            for zz in range(NZ)
            for c in range(2)
        ],
    )
    taps = lax.dynamic_slice_in_dim(filters, quarter * ch, ch, 0).astype(jnp.float32).T
    ends = jnp.cumsum(window_lengths, axis=1, dtype=jnp.int32)
    starts = ends - window_lengths
    windows = window_lengths.shape[1]
    total = pl.pallas_call(
        conv_kernel,
        out_shape=jax.ShapeDtypeStruct((segs, windows, ch), jnp.float32),
        in_specs=[SMEM] + [VMEM] * 7,
        out_specs=VMEM,
        scratch_shapes=[pltpu.VMEM((8, 8 + 2 * rows, ch), jnp.float32)],
        compiler_params=pltpu.CompilerParams(vmem_limit_bytes=24 << 20),
        name="conv_pool",
    )(jnp.stack([xhi, y]).astype(jnp.int32), q, kv, prev, wrap, taps, starts[:, :, None], ends[:, :, None])

    count = segs * windows
    parts = lax.all_to_all(total.reshape(count, ch), SEQ, 0, 0, tiled=True)
    summed = parts.reshape(2, 4, NY, ch).sum(axis=(0, 2)).reshape(channels)
    mine = lax.axis_index(SEQ)
    length = lax.dynamic_index_in_dim(window_lengths.reshape(count), mine, 0, keepdims=False)
    means = (summed / length.astype(jnp.float32)).astype(jnp.bfloat16)
    means = lax.all_to_all(jnp.broadcast_to(means[None], (count, channels)), SEQ, 0, 0, tiled=True)
    terms = jnp.dot(means, out_weight, preferred_element_type=jnp.float32)
    out_cols = out_weight.shape[1]
    terms = terms.reshape(segs, 8, windows // 8, out_cols).transpose(1, 0, 2, 3)
    terms = lax.all_to_all(terms, TENSOR, 0, 0, tiled=True)
    return terms.sum(axis=0).astype(jnp.bfloat16)


def solution(mesh):
    fine = Mesh(mesh.devices.reshape(SIZES), AXES)
    in_specs = (
        P(None, SEQ, TENSOR),
        P(SEQ, None, TENSOR),
        P(None, TENSOR, None),
        P(None, None, None, TENSOR),
        P(TENSOR, None),
        P(),
        P(),
        P(TENSOR, SEQ),
    )
    return jax.shard_map(local, mesh=fine, in_specs=in_specs, out_specs=P(None, TENSOR, SEQ), check_vma=False)
```

time: 1030 us -> 198 us (0.19); the launches traced: 1020 us -> 197 us
  waiting for transfers between devices: 828 us -> 30 us
  starting transfers between devices: 1.57 us -> 74.4 us
  blocking collectives: 74.5 us -> 40.7 us
  local copies, waits for them, and re-layouts: 45 us -> 11.9 us
  other arithmetic: 35.2 us -> 4.56 us
  Pallas kernels: 0 us -> 17.2 us
  matrix products: 13.5 us -> 0.15 us
    psum x1 -> x0, waiting for transfers between devices: 547 us -> none  [local(): window_total = lax.psum(local_total, 'seq')]
    all_gather x2 -> x1, waiting for transfers between devices: 278 us -> 0.02 us  [local(): weight = lax.all_gather(met, 'y', axis=0, tiled=False)]
    ppermute x1 -> x20, starting transfers between devices: 1.49 us -> 64.3 us  [the longest x19 63.7 us: permute(): return lax.ppermute(value, AXES, pairs)]
    unnamed x1 -> x0, blocking collectives: 52.9 us -> none
    all_to_all x0 -> x3, blocking collectives: none -> 40.7 us  [the longest x1 13.9 us: local(): terms = lax.all_to_all(terms, TENSOR, 0, 0, tiled=True)]
    all_gather x1 -> x0, blocking collectives: 21.6 us -> none  [local(): down_factor_full = lax.all_gather(down_sel, 'tensor', axis=1, tiled=True)]
    slice x9 -> x3, local copies, waits for them, and re-layouts: 23.5 us -> 2.12 us  [the longest x2 1.47 us: local(): held += [z_step(ahead[:half], 1), z_step(back[half:], -1)]]
    ppermute x1 -> x20, waiting for transfers between devices: 2.02 us -> 22.1 us  [the longest x19 22.1 us: permute(): return lax.ppermute(value, AXES, pairs)]
  transfers between devices with their start and end apart: 4 -> 22, of which waited for: 3 -> 5; matrix products, arithmetic and copies ran while one was open for 3% -> 4% of each run, Pallas kernels for 0% -> 0%
where the time goes in v1:
time: 198 us; the launch traced here: 197 us
  starting transfers between devices  74.4 us (38%)
  blocking collectives  40.7 us (21%)
  waiting for transfers between devices  30 us (15%)
  between operations  18.4 us (9%)
  Pallas kernels  17.2 us (9%)
  local copies, waits for them, and re-layouts  11.9 us (6%)
  other arithmetic  4.56 us (2%)
    ppermute x19, starting transfers between devices, permute(): return lax.ppermute(value, AXES, pairs)  63.7 us
    ppermute x19, waiting for transfers between devices, permute(): return lax.ppermute(value, AXES, pairs)  22.1 us
    all_to_all x1, blocking collectives, local(): terms = lax.all_to_all(terms, TENSOR, 0, 0, tiled=True)  13.9 us
    all_to_all x1, blocking collectives, local(): met = lax.all_to_all(spread, ('xhi', 'xlo', 'zlo'), 0, 0, tiled=True)  13.5 us
    all_to_all x1, blocking collectives, local(): lax.all_to_all(jnp.broadcast_to(means[None], (count, channels)), SEQ, 0,...  13.3 us
    all_to_all x1, starting transfers between devices, local(): parts = lax.all_to_all(total.reshape(count, ch), SEQ, 0, 0, tiled=True)  10 us
    pallas_call x1, Pallas kernels, local(): pl.pallas_call(functools.partial(project_kernel, dists), out_shape=(jax.S...  9.56 us
    all_to_all x1, waiting for transfers between devices, local(): parts = lax.all_to_all(total.reshape(count, ch), SEQ, 0, 0, tiled=True)  7.92 us
  transfers between devices with their start and end apart: 22, of which 5 were waited for; matrix products, arithmetic and copies ran while one was open for 4% of the time, Pallas kernels for 0%

profile of v1, /device:TPU:1, one launch (start us, length us, event | category | flops | bytes accessed | tf_op | source)
XLA Modules:
  0.0 197.3 jit_solution(13893190535802161114)
XLA Ops:
  6.5 1.0 reshape.44
  8.0 13.5 %all_to_all.25 = bf16[8,64,384]{2,1,0:T(8,128)(2,1)} all-to-all(bf16[8,64,384]{2,1,0:T(8,128)(2,1)S(1)} %pad_maximum_fusion.1), channel_id=1, replica_groups=mesh['xhi'=2,'xlo'=2,'zlo'=2,'y'=8,'zhi'=4,'core'=2] {'xhi','xlo','zlo'}, dimensions={0} | all-to-all | bytes 786432 | tf_op jit(solution)/shard_map/all_to_all | solution.py:150
  21.5 2.0 %collective-permute-start = (bf16[256,512]{1,0:T(8,128)(2,1)S(1)}, bf16[256,512]{1,0:T(8,128)(2,1)S(1)}, u32[]{:S(2)}, u32[]{:S(2)}) collective-permute-start(bf16[256,512]{1,0:T(8,128)(2,1)S(1)} %bitcast.56), channel_id=1, source_target_pairs={{0,128},{1,129},{64,192},{65,193},{2,130},{3,131},{66,194},{67,195... | collective-permute-start | bytes 786440 | tf_op jit(solution)/shard_map/ppermute | solution.py:30
  28.9 10.2 %collective-permute-start.4 = (bf16[544,512]{1,0:T(8,128)(2,1)S(1)}, bf16[544,512]{1,0:T(8,128)(2,1)S(1)}, u32[]{:S(2)}, u32[]{:S(2)}) collective-permute-start(bf16[544,512]{1,0:T(8,128)(2,1)S(1)} %pad_maximum_fusion.refs_0_), channel_id=1, source_target_pairs={{0,70},{1,71},{64,0},{65,1},{2,64},{3,65},{66,2},{67,3},{4,66},{5,... | collective-permute-start | bytes 1671176 | tf_op jit(solution)/shard_map/ppermute | solution.py:30
  39.1 1.9 collective-permute-start.2
  41.0 7.1 %collective-permute-done.4.refs_4_ = bf16[544,512]{1,0:T(8,128)(2,1)S(1)} collective-permute-done((bf16[544,512]{1,0:T(8,128)(2,1)S(1)}, bf16[544,512]{1,0:T(8,128)(2,1)S(1)}, u32[]{:S(2)}, u32[]{:S(2)}) %collective-permute-start.4) | collective-permute-done | bytes 557088 | tf_op jit(solution)/shard_map/ppermute | solution.py:30
  48.1 5.4 %collective-permute-start.8 = (bf16[544,512]{1,0:T(8,128)(2,1)S(1)}, bf16[544,512]{1,0:T(8,128)(2,1)S(1)}, u32[]{:S(2)}, u32[]{:S(2)}) collective-permute-start(bf16[544,512]{1,0:T(8,128)(2,1)S(1)} %collective-permute-done.4.refs_4_), channel_id=1, source_target_pairs={{0,70},{1,71},{64,0},{65,1},{2,64},{3,65},{66,2},{67,3},{4,66},{5,... | collective-permute-start | bytes 1671176 | tf_op jit(solution)/shard_map/ppermute | solution.py:30
  53.5 1.9 collective-permute-start.6
  55.4 6.2 %collective-permute-done.8.refs_8_ = bf16[544,512]{1,0:T(8,128)(2,1)S(1)} collective-permute-done((bf16[544,512]{1,0:T(8,128)(2,1)S(1)}, bf16[544,512]{1,0:T(8,128)(2,1)S(1)}, u32[]{:S(2)}, u32[]{:S(2)}) %collective-permute-start.8) | collective-permute-done | bytes 557088 | tf_op jit(solution)/shard_map/ppermute | solution.py:30
  61.7 5.4 %collective-permute-start.12 = (bf16[544,512]{1,0:T(8,128)(2,1)S(1)}, bf16[544,512]{1,0:T(8,128)(2,1)S(1)}, u32[]{:S(2)}, u32[]{:S(2)}) collective-permute-start(bf16[544,512]{1,0:T(8,128)(2,1)S(1)} %collective-permute-done.8.refs_8_), channel_id=1, source_target_pairs={{0,70},{1,71},{64,0},{65,1},{2,64},{3,65},{66,2},{67,3},{4,66},{5,... | collective-permute-start | bytes 1671176 | tf_op jit(solution)/shard_map/ppermute | solution.py:30
  67.1 1.9 collective-permute-start.10
  69.0 6.7 %collective-permute-start.1 = (bf16[544,512]{1,0:T(8,128)(2,1)S(1)}, bf16[544,512]{1,0:T(8,128)(2,1)}, u32[]{:S(2)}, u32[]{:S(2)}) collective-permute-start(bf16[544,512]{1,0:T(8,128)(2,1)S(1)} %pad_maximum_fusion.refs_0_), channel_id=1, source_target_pairs={{0,1},{1,0},{64,65},{65,64},{2,3},{3,2},{66,67},{67,66},{4,5},{5,4... | collective-permute-start | bytes 1671176 | tf_op jit(solution)/shard_map/ppermute | solution.py:30
  75.8 1.9 collective-permute-start.3
  77.7 2.4 %collective-permute-start.5 = (bf16[544,512]{1,0:T(8,128)(2,1)S(1)}, bf16[544,512]{1,0:T(8,128)(2,1)}, u32[]{:S(2)}, u32[]{:S(2)}) collective-permute-start(bf16[544,512]{1,0:T(8,128)(2,1)S(1)} %collective-permute-done.4.refs_4_), channel_id=1, source_target_pairs={{0,1},{1,0},{64,65},{65,64},{2,3},{3,2},{66,67},{67,66},{4,5},{5,4... | collective-permute-start | bytes 1671176 | tf_op jit(solution)/shard_map/ppermute | solution.py:30
  80.1 1.9 collective-permute-start.7
  83.7 5.1 %collective-permute-start.16 = (bf16[288,512]{1,0:T(8,128)(2,1)}, bf16[288,512]{1,0:T(8,128)(2,1)}, u32[]{:S(2)}, u32[]{:S(2)}) collective-permute-start(bf16[288,512]{1,0:T(8,128)(2,1)} %slice.23), channel_id=1, source_target_pairs={{0,70},{1,71},{64,0},{65,1},{2,64},{3,65},{66,2},{67,3},{4,66},{5,... | collective-permute-start | bytes 884744 | tf_op jit(solution)/shard_map/ppermute | solution.py:30
  89.5 1.9 collective-permute-start.14
  92.2 2.5 %collective-permute-start.9 = (bf16[544,512]{1,0:T(8,128)(2,1)S(1)}, bf16[544,512]{1,0:T(8,128)(2,1)}, u32[]{:S(2)}, u32[]{:S(2)}) collective-permute-start(bf16[544,512]{1,0:T(8,128)(2,1)S(1)} %collective-permute-done.8.refs_8_), channel_id=1, source_target_pairs={{0,1},{1,0},{64,65},{65,64},{2,3},{3,2},{66,67},{67,66},{4,5},{5,4... | collective-permute-start | bytes 1671176 | tf_op jit(solution)/shard_map/ppermute | solution.py:30
  94.8 1.9 collective-permute-start.11
  96.7 2.4 %collective-permute-start.13 = (bf16[544,512]{1,0:T(8,128)(2,1)S(1)}, bf16[544,512]{1,0:T(8,128)(2,1)}, u32[]{:S(2)}, u32[]{:S(2)}) collective-permute-start(bf16[544,512]{1,0:T(8,128)(2,1)S(1)} %collective-permute-done.12.refs_12_), channel_id=1, source_target_pairs={{0,1},{1,0},{64,65},{65,64},{2,3},{3,2},{66,67},{67,66},{4,5},{5,4... | collective-permute-start | bytes 1671176 | tf_op jit(solution)/shard_map/ppermute | solution.py:30
  99.2 1.1 collective-permute-done.14.refs_14_
  100.2 3.3 %collective-permute-start.15 = (bf16[256,512]{1,0:T(8,128)(2,1)}, bf16[256,512]{1,0:T(8,128)(2,1)}, u32[]{:S(2)}, u32[]{:S(2)}) collective-permute-start(bf16[256,512]{1,0:T(8,128)(2,1)} %collective-permute-done.14.refs_14_), channel_id=1, source_target_pairs={{0,1},{1,0},{64,65},{65,64},{2,3},{3,2},{66,67},{67,66},{4,5},{5,4... | collective-permute-start | bytes 786440 | tf_op jit(solution)/shard_map/ppermute | solution.py:30
  103.5 1.9 collective-permute-start.17
  108.5 1.9 copy-done.1
  111.1 9.6 %project.1 = (f32[4,2,128,128]{3,2,1,0:T(8,128)S(1)}, bf16[4,2,128,128]{3,2,1,0:T(8,128)(2,1)S(1)}) custom-call(s32[3]{0:T(128)S(1)} %pad_add_fusion.1.place, bf16[544,512]{1,0:T(8,128)(2,1)S(1)} %pad_maximum_fusion.refs_0_, bf16[544,512]{1,0:T(8,128)(2,1)} %collective-permute-done.1.refs_1_, bf16[544,512]{1,0:T(8,128)(2,1)S(1)} %collective-permute-done.2.refs_2_, ...), custom_call_target="tpu_custom_call" | custom-call | tf_op jit(solution)/shard_map/project/pallas_call | solution.py:176
  120.7 2.9 %collective-permute-start.18 = (bf16[4,2,128,128]{3,2,1,0:T(8,128)(2,1)S(1)}, bf16[4,2,128,128]{3,2,1,0:T(8,128)(2,1)S(1)}, u32[]{:S(2)}, u32[]{:S(2)}) collective-permute-start(bf16[4,2,128,128]{3,2,1,0:T(8,128)(2,1)S(1)} %get-tuple-element.8.kv_ref), channel_id=1, source_target_pairs={{0,8},{1,9},{64,72},{65,73},{2,10},{3,11},{66,74},{67,75},{4,12},{... | collective-permute-start | bytes 786440 | tf_op jit(solution)/shard_map/ppermute | solution.py:30
  124.4 7.7 %collective-permute-done.18.prev_ref = bf16[4,2,128,128]{3,2,1,0:T(8,128)(2,1)S(1)} collective-permute-done((bf16[4,2,128,128]{3,2,1,0:T(8,128)(2,1)S(1)}, bf16[4,2,128,128]{3,2,1,0:T(8,128)(2,1)S(1)}, u32[]{:S(2)}, u32[]{:S(2)}) %collective-permute-start.18) | collective-permute-done | bytes 262176 | tf_op jit(solution)/shard_map/ppermute | solution.py:30
  132.0 7.6 %conv_pool.1 = f32[2,32,128]{2,1,0:T(8,128)} custom-call(s32[2]{0:T(128)S(1)} %pad_add_fusion.place, f32[4,2,128,128]{3,2,1,0:T(8,128)S(1)} %get-tuple-element.7.q_ref, bf16[4,2,128,128]{3,2,1,0:T(8,128)(2,1)S(1)} %get-tuple-element.8.kv_ref, bf16[4,2,128,128]{3,2,1,0:T(8,128)(2,1)S(1)} %collective-permute-done.18.prev_ref, ...), custom_call_target="tpu_custom_call" | custom-call | tf_op jit(solution)/shard_map/conv_pool/pallas_call | solution.py:207
  139.7 10.0 %all-to-all-start.1 = ((f32[64,1,128]{2,1,0:T(1,128)}), f32[64,1,128]{2,1,0:T(1,128)S(1)}, u32[]{:S(2)}, u32[]{:S(2)}) async-start(f32[64,1,128]{2,1,0:T(1,128)} %bitcast.21), calls=%async_computation.1 | async-start | bytes 65536 | tf_op jit(solution)/shard_map/all_to_all | solution.py:218
  151.0 7.9 %all-to-all-done.1 = f32[64,1,128]{2,1,0:T(1,128)S(1)} async-done(((f32[64,1,128]{2,1,0:T(1,128)}), f32[64,1,128]{2,1,0:T(1,128)S(1)}, u32[]{:S(2)}, u32[]{:S(2)}) %all-to-all-start.1) | async-done | bytes 32800 | tf_op jit(solution)/shard_map/all_to_all | solution.py:218
  160.6 13.3 %all_to_all.26 = bf16[64,2,256]{2,1,0:T(2,128)(2,1)S(1)} all-to-all(bf16[64,2,256]{2,1,0:T(2,128)(2,1)S(1)} %reshape.52), channel_id=1, replica_groups=mesh['xhi'=2,'xlo'=2,'zlo'=2,'y'=8,'zhi'=4,'core'=2] {'xhi','xlo','zlo',..., dimensions={0} | all-to-all | bytes 131072 | tf_op jit(solution)/shard_map/all_to_all | solution.py:223
  174.6 13.9 %all_to_all.27 = f32[8,1,512]{2,1,0:T(1,128)S(1)} all-to-all(f32[8,1,512]{2,1,0:T(1,128)S(1)} %reshape.54), channel_id=1, replica_groups=mesh['xhi'=2,'xlo'=2,'zlo'=2,'y'=8,'zhi'=4,'core'=2] {'zhi','core'}, dimensions={0} | all-to-all | bytes 32768 | tf_op jit(solution)/shard_map/all_to_all | solution.py:227
  (76 shorter events, 14.4 us)
Async XLA Ops:
  6.5 75.5 %copy-start = (bf16[512,128]{1,0:T(8,128)(2,1)S(1)}, bf16[512,128]{1,0:T(8,128)(2,1)}, u32[]{:S(2)}) copy-start(bf16[512,128]{1,0:T(8,128)(2,1)} %param.12) | copy-start | bytes 393220
  6.5 102.0 %all-gather.3.cloned.1.call-start = ((), (), s32[]{:S(2)}) async-start(), calls=%async_computation.4 | async-start | bytes 3538944 | tf_op jit(solution)/shard_map/all_gather | solution.py:151
  7.7 13.8 %copy-start.5 = (bf16[2,128,512]{2,1,0:T(8,128)(2,1)S(1)}, bf16[2,128,512]{2,1,0:T(8,128)(2,1)}, u32[]{:S(2)}) copy-start(bf16[2,128,512]{2,1,0:T(8,128)(2,1)} %param.8) | copy-start | bytes 786436
  7.7 15.8 %copy-start.8 = (s32[2]{0:T(128)S(1)}, s32[2]{0:T(128)}, u32[]{:S(2)}) copy-start(s32[2]{0:T(128)} %param.13) | copy-start | bytes 28
  21.5 7.3 %collective-permute-start = (bf16[256,512]{1,0:T(8,128)(2,1)S(1)}, bf16[256,512]{1,0:T(8,128)(2,1)S(1)}, u32[]{:S(2)}, u32[]{:S(2)}) collective-permute-start(bf16[256,512]{1,0:T(8,128)(2,1)S(1)} %bitcast.56), channel_id=1, source_target_pairs={{0,128},{1,129},{64,192},{65,193},{2,130},{3,131},{66,194},{67,195... | collective-permute-start | bytes 786440 | tf_op jit(solution)/shard_map/ppermute | solution.py:30
  28.9 63.2 %copy-start.7 = (s32[2,32]{1,0:T(2,128)S(1)}, s32[2,32]{1,0:T(2,128)}, u32[]{:S(2)}) copy-start(s32[2,32]{1,0:T(2,128)} %param.14) | copy-start | bytes 772
  28.9 19.1 %collective-permute-start.4 = (bf16[544,512]{1,0:T(8,128)(2,1)S(1)}, bf16[544,512]{1,0:T(8,128)(2,1)S(1)}, u32[]{:S(2)}, u32[]{:S(2)}) collective-permute-start(bf16[544,512]{1,0:T(8,128)(2,1)S(1)} %pad_maximum_fusion.refs_0_), channel_id=1, source_target_pairs={{0,70},{1,71},{64,0},{65,1},{2,64},{3,65},{66,2},{67,3},{4,66},{5,... | collective-permute-start | bytes 1671176 | tf_op jit(solution)/shard_map/ppermute | solution.py:30
  39.1 14.4 %collective-permute-start.2 = (bf16[544,512]{1,0:T(8,128)(2,1)S(1)}, bf16[544,512]{1,0:T(8,128)(2,1)S(1)}, u32[]{:S(2)}, u32[]{:S(2)}) collective-permute-start(bf16[544,512]{1,0:T(8,128)(2,1)S(1)} %pad_maximum_fusion.refs_0_), channel_id=1, source_target_pairs={{0,64},{1,65},{64,2},{65,3},{2,66},{3,67},{66,4},{67,5},{4,68},{5,... | collective-permute-start | bytes 1671176 | tf_op jit(solution)/shard_map/ppermute | solution.py:30
  48.1 13.6 %collective-permute-start.8 = (bf16[544,512]{1,0:T(8,128)(2,1)S(1)}, bf16[544,512]{1,0:T(8,128)(2,1)S(1)}, u32[]{:S(2)}, u32[]{:S(2)}) collective-permute-start(bf16[544,512]{1,0:T(8,128)(2,1)S(1)} %collective-permute-done.4.refs_4_), channel_id=1, source_target_pairs={{0,70},{1,71},{64,0},{65,1},{2,64},{3,65},{66,2},{67,3},{4,66},{5,... | collective-permute-start | bytes 1671176 | tf_op jit(solution)/shard_map/ppermute | solution.py:30
  53.5 13.6 %collective-permute-start.6 = (bf16[544,512]{1,0:T(8,128)(2,1)S(1)}, bf16[544,512]{1,0:T(8,128)(2,1)}, u32[]{:S(2)}, u32[]{:S(2)}) collective-permute-start(bf16[544,512]{1,0:T(8,128)(2,1)S(1)} %collective-permute-done.2.refs_2_), channel_id=1, source_target_pairs={{0,64},{1,65},{64,2},{65,3},{2,66},{3,67},{66,4},{67,5},{4,68},{5,... | collective-permute-start | bytes 1671176 | tf_op jit(solution)/shard_map/ppermute | solution.py:30
  61.7 18.4 %collective-permute-start.12 = (bf16[544,512]{1,0:T(8,128)(2,1)S(1)}, bf16[544,512]{1,0:T(8,128)(2,1)S(1)}, u32[]{:S(2)}, u32[]{:S(2)}) collective-permute-start(bf16[544,512]{1,0:T(8,128)(2,1)S(1)} %collective-permute-done.8.refs_8_), channel_id=1, source_target_pairs={{0,70},{1,71},{64,0},{65,1},{2,64},{3,65},{66,2},{67,3},{4,66},{5,... | collective-permute-start | bytes 1671176 | tf_op jit(solution)/shard_map/ppermute | solution.py:30
  67.1 16.6 %collective-permute-start.10 = (bf16[544,512]{1,0:T(8,128)(2,1)}, bf16[544,512]{1,0:T(8,128)(2,1)S(1)}, u32[]{:S(2)}, u32[]{:S(2)}) collective-permute-start(bf16[544,512]{1,0:T(8,128)(2,1)} %collective-permute-done.6.refs_6_), channel_id=1, source_target_pairs={{0,64},{1,65},{64,2},{65,3},{2,66},{3,67},{66,4},{67,5},{4,68},{5,... | collective-permute-start | bytes 1671176 | tf_op jit(solution)/shard_map/ppermute | solution.py:30
  69.0 20.5 %collective-permute-start.1 = (bf16[544,512]{1,0:T(8,128)(2,1)S(1)}, bf16[544,512]{1,0:T(8,128)(2,1)}, u32[]{:S(2)}, u32[]{:S(2)}) collective-permute-start(bf16[544,512]{1,0:T(8,128)(2,1)S(1)} %pad_maximum_fusion.refs_0_), channel_id=1, source_target_pairs={{0,1},{1,0},{64,65},{65,64},{2,3},{3,2},{66,67},{67,66},{4,5},{5,4... | collective-permute-start | bytes 1671176 | tf_op jit(solution)/shard_map/ppermute | solution.py:30
  75.8 16.5 %collective-permute-start.3 = (bf16[544,512]{1,0:T(8,128)(2,1)S(1)}, bf16[544,512]{1,0:T(8,128)(2,1)}, u32[]{:S(2)}, u32[]{:S(2)}) collective-permute-start(bf16[544,512]{1,0:T(8,128)(2,1)S(1)} %collective-permute-done.2.refs_2_), channel_id=1, source_target_pairs={{0,1},{1,0},{64,65},{65,64},{2,3},{3,2},{66,67},{67,66},{4,5},{5,4... | collective-permute-start | bytes 1671176 | tf_op jit(solution)/shard_map/ppermute | solution.py:30
  77.7 17.1 %collective-permute-start.5 = (bf16[544,512]{1,0:T(8,128)(2,1)S(1)}, bf16[544,512]{1,0:T(8,128)(2,1)}, u32[]{:S(2)}, u32[]{:S(2)}) collective-permute-start(bf16[544,512]{1,0:T(8,128)(2,1)S(1)} %collective-permute-done.4.refs_4_), channel_id=1, source_target_pairs={{0,1},{1,0},{64,65},{65,64},{2,3},{3,2},{66,67},{67,66},{4,5},{5,4... | collective-permute-start | bytes 1671176 | tf_op jit(solution)/shard_map/ppermute | solution.py:30
  80.1 16.6 %collective-permute-start.7 = (bf16[544,512]{1,0:T(8,128)(2,1)}, bf16[544,512]{1,0:T(8,128)(2,1)}, u32[]{:S(2)}, u32[]{:S(2)}) collective-permute-start(bf16[544,512]{1,0:T(8,128)(2,1)} %collective-permute-done.6.refs_6_), channel_id=1, source_target_pairs={{0,1},{1,0},{64,65},{65,64},{2,3},{3,2},{66,67},{67,66},{4,5},{5,4... | collective-permute-start | bytes 1671176 | tf_op jit(solution)/shard_map/ppermute | solution.py:30
  83.7 19.9 %collective-permute-start.16 = (bf16[288,512]{1,0:T(8,128)(2,1)}, bf16[288,512]{1,0:T(8,128)(2,1)}, u32[]{:S(2)}, u32[]{:S(2)}) collective-permute-start(bf16[288,512]{1,0:T(8,128)(2,1)} %slice.23), channel_id=1, source_target_pairs={{0,70},{1,71},{64,0},{65,1},{2,64},{3,65},{66,2},{67,3},{4,66},{5,... | collective-permute-start | bytes 884744 | tf_op jit(solution)/shard_map/ppermute | solution.py:30
  89.5 10.7 %collective-permute-start.14 = (bf16[256,512]{1,0:T(8,128)(2,1)}, bf16[256,512]{1,0:T(8,128)(2,1)}, u32[]{:S(2)}, u32[]{:S(2)}) collective-permute-start(bf16[256,512]{1,0:T(8,128)(2,1)} %slice.22), channel_id=1, source_target_pairs={{0,64},{1,65},{64,2},{65,3},{2,66},{3,67},{66,4},{67,5},{4,68},{5,... | collective-permute-start | bytes 786440 | tf_op jit(solution)/shard_map/ppermute | solution.py:30
  92.2 16.2 %collective-permute-start.9 = (bf16[544,512]{1,0:T(8,128)(2,1)S(1)}, bf16[544,512]{1,0:T(8,128)(2,1)}, u32[]{:S(2)}, u32[]{:S(2)}) collective-permute-start(bf16[544,512]{1,0:T(8,128)(2,1)S(1)} %collective-permute-done.8.refs_8_), channel_id=1, source_target_pairs={{0,1},{1,0},{64,65},{65,64},{2,3},{3,2},{66,67},{67,66},{4,5},{5,4... | collective-permute-start | bytes 1671176 | tf_op jit(solution)/shard_map/ppermute | solution.py:30
  94.8 13.7 %collective-permute-start.11 = (bf16[544,512]{1,0:T(8,128)(2,1)S(1)}, bf16[544,512]{1,0:T(8,128)(2,1)}, u32[]{:S(2)}, u32[]{:S(2)}) collective-permute-start(bf16[544,512]{1,0:T(8,128)(2,1)S(1)} %collective-permute-done.10.refs_10_), channel_id=1, source_target_pairs={{0,1},{1,0},{64,65},{65,64},{2,3},{3,2},{66,67},{67,66},{4,5},{5,4... | collective-permute-start | bytes 1671176 | tf_op jit(solution)/shard_map/ppermute | solution.py:30
  96.7 11.7 %collective-permute-start.13 = (bf16[544,512]{1,0:T(8,128)(2,1)S(1)}, bf16[544,512]{1,0:T(8,128)(2,1)}, u32[]{:S(2)}, u32[]{:S(2)}) collective-permute-start(bf16[544,512]{1,0:T(8,128)(2,1)S(1)} %collective-permute-done.12.refs_12_), channel_id=1, source_target_pairs={{0,1},{1,0},{64,65},{65,64},{2,3},{3,2},{66,67},{67,66},{4,5},{5,4... | collective-permute-start | bytes 1671176 | tf_op jit(solution)/shard_map/ppermute | solution.py:30
  100.2 8.2 %collective-permute-start.15 = (bf16[256,512]{1,0:T(8,128)(2,1)}, bf16[256,512]{1,0:T(8,128)(2,1)}, u32[]{:S(2)}, u32[]{:S(2)}) collective-permute-start(bf16[256,512]{1,0:T(8,128)(2,1)} %collective-permute-done.14.refs_14_), channel_id=1, source_target_pairs={{0,1},{1,0},{64,65},{65,64},{2,3},{3,2},{66,67},{67,66},{4,5},{5,4... | collective-permute-start | bytes 786440 | tf_op jit(solution)/shard_map/ppermute | solution.py:30
  103.5 4.9 %collective-permute-start.17 = (bf16[288,512]{1,0:T(8,128)(2,1)}, bf16[288,512]{1,0:T(8,128)(2,1)}, u32[]{:S(2)}, u32[]{:S(2)}) collective-permute-start(bf16[288,512]{1,0:T(8,128)(2,1)} %collective-permute-done.16.refs_16_), channel_id=1, source_target_pairs={{0,1},{1,0},{64,65},{65,64},{2,3},{3,2},{66,67},{67,66},{4,5},{5,4... | collective-permute-start | bytes 884744 | tf_op jit(solution)/shard_map/ppermute | solution.py:30
  108.5 1.9 copy-start.1
  110.4 0.7 copy-start.4
  111.1 20.9 %copy-start.2 = (s32[2,32,1]{2,1,0:T(8,128)S(1)}, s32[2,32,1]{2,1,0:T(8,128)}, u32[]{:S(2)}) copy-start(s32[2,32,1]{2,1,0:T(8,128)} %copy.22.start_ref) | copy-start | bytes 772
  111.1 20.9 %copy-start.3 = (s32[2,32,1]{2,1,0:T(8,128)S(1)}, s32[2,32,1]{2,1,0:T(8,128)}, u32[]{:S(2)}) copy-start(s32[2,32,1]{2,1,0:T(8,128)} %copy.23.end_ref) | copy-start | bytes 772
  120.7 11.3 %collective-permute-start.18 = (bf16[4,2,128,128]{3,2,1,0:T(8,128)(2,1)S(1)}, bf16[4,2,128,128]{3,2,1,0:T(8,128)(2,1)S(1)}, u32[]{:S(2)}, u32[]{:S(2)}) collective-permute-start(bf16[4,2,128,128]{3,2,1,0:T(8,128)(2,1)S(1)} %get-tuple-element.8.kv_ref), channel_id=1, source_target_pairs={{0,8},{1,9},{64,72},{65,73},{2,10},{3,11},{66,74},{67,75},{4,12},{... | collective-permute-start | bytes 786440 | tf_op jit(solution)/shard_map/ppermute | solution.py:30
  123.6 0.8 collective-permute-start.19
  132.0 42.3 %copy-start.6 = (bf16[512,64]{0,1:T(8,128)(2,1)S(1)}, bf16[512,64]{0,1:T(8,128)(2,1)}, u32[]{:S(2)}) copy-start(bf16[512,64]{0,1:T(8,128)(2,1)} %param.15) | copy-start | bytes 196612
  139.7 19.3 %all-to-all-start.1 = ((f32[64,1,128]{2,1,0:T(1,128)}), f32[64,1,128]{2,1,0:T(1,128)S(1)}, u32[]{:S(2)}, u32[]{:S(2)}) async-start(f32[64,1,128]{2,1,0:T(1,128)} %bitcast.21), calls=%async_computation.1 | async-start | bytes 65536 | tf_op jit(solution)/shard_map/all_to_all | solution.py:218
Sparse Core Ops, SparseCore 0:
  21.6 50.8 all-gather.2

commit v2 on v1

v2 whole, which is shorter than its diff:
```python
import functools
import jax
import jax.numpy as jnp
from jax import lax
from jax.experimental import pallas as pl
from jax.experimental.pallas import tpu as pltpu
from jax.sharding import Mesh, PartitionSpec as P

AXES = ("xhi", "xlo", "zlo", "y", "zhi", "core")
SIZES = (2, 2, 2, 8, 4, 2)
SEQ = ("xhi", "xlo", "zlo", "y")
TENSOR = ("zhi", "core")
NZ, NY = 8, 8
adapter_scale = 0.5


def flat(x, y, z, c):
    return (((x % 4) * 2 + (z % NZ) % 2) * NY + y % NY) * 8 + ((z % NZ) // 2) * 2 + c


def permute(value, move, keep=lambda x, y, z, c: True):
    pairs = [
        (flat(x, y, z, c), flat(*move(x, y, z, c)))
        for x in range(4)
        for y in range(NY)
        for z in range(NZ)
        for c in range(2)
        if keep(x, y, z, c)
    ]
    return lax.ppermute(value, AXES, pairs)


def z_step(value, step):
    return permute(value, lambda x, y, z, c: (x, y, z + step, c))


def core_swap(value):
    return permute(value, lambda x, y, z, c: (x, y, z, 1 - c))


def x_pair_swap(value):
    return permute(value, lambda x, y, z, c: (x ^ 1, y, z, c))


def nt_dot(a, b):
    return lax.dot_general(a, b, (((1,), (1,)), ((), ())), preferred_element_type=jnp.float32)


def pieces_of(refs):
    return [refs[2 * d : 2 * d + 2] for d in range(NZ)]


def distances(rel):
    return [d for d in range(NZ) if d % 2 == rel]


def stacked_weight(weight, z, rel, side, columns):
    blocks = []
    for dist in distances(rel):
        zhi = lax.rem(z + dist, NZ) // 2
        block = weight[:, side, pl.ds(zhi, 1), :, columns]
        blocks.append(block.reshape(weight.shape[0] * weight.shape[3], block.shape[-1]))
    return jnp.concatenate(blocks, axis=0)


def stacked_rows(pieces, rel, pair, half):
    return jnp.concatenate([pieces[d][pair][:half, :] for d in distances(rel)], axis=1)


def project_kv_kernel(place, *refs):
    pieces = pieces_of(refs)
    weight, up, up_other, own_ref, send_ref, low_ref = refs[2 * NZ :]
    z = place[0]
    half = own_ref.shape[2]
    ch = up.shape[1] // 3
    ranks = up.shape[0]
    for rel in range(2):
        down = jnp.concatenate([pieces[d][0][half:, :] for d in distances(rel)], axis=1)
        lows = []
        for pair in range(2):
            low = nt_dot(stacked_rows(pieces, rel, pair, half), down)
            row = lax.broadcasted_iota(jnp.int32, (half, ranks), 0)
            column = lax.broadcasted_iota(jnp.int32, (half, ranks), 1)
            mine = (row >= half // 2) == (column >= ranks // 2)
            lows.append(jnp.where(mine, adapter_scale * low, 0.0).astype(jnp.bfloat16))
            low_ref[rel, pair] = lows[pair]
        for side in range(2):
            b = stacked_weight(weight, z, rel, side, slice(ch, 3 * ch))
            ups = (up if side == 0 else up_other)[:, ch:]
            for pair in range(2):
                a = stacked_rows(pieces, rel, pair, half)
                part = jnp.dot(a, b, preferred_element_type=jnp.float32)
                part += jnp.dot(lows[pair], ups, preferred_element_type=jnp.float32)
                if side == 0:
                    own_ref[rel, pair] = part
                else:
                    send_ref[rel, pair] = part.astype(send_ref.dtype)


def project_q_kernel(place, *refs):
    pieces = pieces_of(refs)
    weight, up, up_other, low_ref, own_ref, send_ref = refs[2 * NZ :]
    z = place[0]
    half = own_ref.shape[2]
    ch = up.shape[1] // 3
    for rel in range(2):
        b = jnp.concatenate([stacked_weight(weight, z, rel, side, slice(0, ch)) for side in range(2)], axis=1)
        ups = jnp.concatenate([up[:, :ch], up_other[:, :ch]], axis=1)
        for pair in range(2):
            a = stacked_rows(pieces, rel, pair, half)
            part = jnp.dot(a, b, preferred_element_type=jnp.float32)
            part += jnp.dot(low_ref[rel, pair], ups, preferred_element_type=jnp.float32)
            own_ref[rel, pair] = part[:, :ch]
            send_ref[rel, pair] = part[:, ch:].astype(send_ref.dtype)


def combine_kernel(place, own_ref, met_ref, kv_ref):
    xlo, zlo = place[3], place[1]
    rows, ch = kv_ref.shape[2], kv_ref.shape[3]
    for rel in range(2):
        for pair in range(2):
            quarter = (xlo if pair == 0 else 1 - xlo) * 2 + (zlo if rel == 0 else 1 - zlo)
            both = own_ref[rel, pair] + met_ref[rel, pair].astype(jnp.float32)
            kv = (both[:, :ch] * both[:, ch:]).astype(jnp.bfloat16)
            for seg in range(2):
                kv_ref[quarter, seg] = kv[rows * seg : rows * (seg + 1), :]


def spread_taps(taps_ref, tap, ch):
    return jnp.broadcast_to(taps_ref[tap : tap + 1, :], (8, ch))


def conv_own_kernel(kv_ref, taps_ref, part_ref, ext):
    rows, ch = kv_ref.shape[2], kv_ref.shape[3]
    groups = rows // 8

    def block(n, carry):
        quarter, seg = n // 2, lax.rem(n, 2)
        ext[0:8, :] = jnp.zeros((8, ch), jnp.float32)
        ext[8:, :] = kv_ref[quarter, seg].astype(jnp.float32)
        total = [jnp.zeros((8, ch), jnp.float32) for _ in range(groups)]
        for r in range(8):
            shifted = [ext[8 * g + 8 - r : 8 * g + 16 - r, :] for g in range(groups)]
            for s in range(groups):
                tap = spread_taps(taps_ref, 8 * s + r, ch)
                for g in range(s, groups):
                    total[g] = total[g] + tap * shifted[g - s]
        for g in range(groups):
            part_ref[quarter, seg, 8 * g : 8 * g + 8, :] = total[g]
        return carry

    lax.fori_loop(0, 8, block, 0)


def gate_kernel(place, part_ref, own_ref, met_ref, prev_ref, wrap_ref, taps_ref, start_ref, end_ref, out_ref, ext):
    z_lo, x_lo, x_hi, y = place[1], place[3], place[4], place[5]
    rows, ch = part_ref.shape[2], part_ref.shape[3]
    groups = rows // 8
    count = out_ref.shape[1]
    out_ref[0] = jnp.zeros((count, ch), jnp.float32)
    row = lax.broadcasted_iota(jnp.int32, (count, rows), 0)
    column = lax.broadcasted_iota(jnp.int32, (count, rows), 1)
    row_seg = lax.rem(row // 4, 2)

    def block(n, carry):
        rel, pair, seg = n // 4, lax.rem(n // 2, 2), lax.rem(n, 2)
        z_at = jnp.where(rel == 0, z_lo, 1 - z_lo)
        x_at = jnp.where(pair == 0, x_lo, 1 - x_lo)
        quarter = x_at * 2 + z_at
        at = jnp.where(y > 0, quarter, jnp.maximum(quarter - 1, 0))
        before = prev_ref[at, seg].astype(jnp.float32)
        wrapped = wrap_ref[seg].astype(jnp.float32)
        ext[0:8, :] = jnp.zeros((8, ch), jnp.float32)
        ext[8 : 8 + rows, :] = jnp.where((y == 0) & (quarter == 0), wrapped, before)
        ext[8 + rows :, :] = jnp.zeros((8, ch), jnp.float32)
        total = [part_ref[quarter, seg, 8 * g : 8 * g + 8, :] for g in range(groups)]
        for r in range(8):
            shifted = [ext[8 * g + 8 - r : 8 * g + 16 - r, :] for g in range(groups + (1 if r else 0))]
            for s in range(groups):
                tap = spread_taps(taps_ref, 8 * s + r, ch)
                for g in range(groups):
                    if groups + g - s < len(shifted):
                        total[g] = total[g] + tap * shifted[groups + g - s]
        at_rows = pl.ds(pl.multiple_of(seg * rows, rows), rows)
        q = own_ref[rel, pair, at_rows, :] + met_ref[rel, pair, at_rows, :].astype(jnp.float32)
        gated = (q * jnp.concatenate(total, axis=0)).astype(jnp.bfloat16)
        position = (((x_hi * 2 + x_at) * 2 + z_at) * NY + y) * rows + column
        inside = (position >= start_ref[...]) & (position < end_ref[...]) & (row_seg == seg)
        member = inside.astype(jnp.float32).astype(jnp.bfloat16)
        out_ref[0] += jnp.dot(member, gated, preferred_element_type=jnp.float32)
        return carry

    lax.fori_loop(0, 8, block, 0)
    for copy in range(1, out_ref.shape[0]):
        out_ref[copy] = out_ref[0]


def sum_kernel(met_ref, out_ref):
    total = met_ref[0]
    for i in range(1, met_ref.shape[0]):
        total = total + met_ref[i]
    for copy in range(out_ref.shape[0]):
        out_ref[copy] = total


def embed_kernel(met_ref, length_ref, weight_ref, out_ref):
    length = length_ref[...].astype(jnp.float32)
    means = []
    for t in range(met_ref.shape[2]):
        for quarter in range(met_ref.shape[1]):
            total = met_ref[0, quarter, t] + met_ref[1, quarter, t]
            means.append((total / length).astype(jnp.bfloat16))
    means = jnp.concatenate(means, axis=1)
    weight = weight_ref[...].astype(jnp.bfloat16)
    out_ref[...] = jnp.dot(means, weight, preferred_element_type=jnp.float32).astype(jnp.bfloat16)


VMEM = pl.BlockSpec(memory_space=pltpu.VMEM)
SMEM = pl.BlockSpec(memory_space=pltpu.SMEM)


def call(kernel, name, out, operands, scratch=(), vmem=32, scalars=True):
    return pl.pallas_call(
        kernel,
        out_shape=out,
        in_specs=[SMEM] * scalars + [VMEM] * (len(operands) - scalars),
        out_specs=jax.tree.map(lambda _: VMEM, out),
        scratch_shapes=list(scratch),
        compiler_params=pltpu.CompilerParams(vmem_limit_bytes=vmem << 20),
        name=name,
    )(*operands)


def local(tokens, in_weight, down_factors, up_factors, filters, task_ids, window_lengths, out_weight):
    f32, bf16 = jnp.float32, jnp.bfloat16
    segs, rows, depth = tokens.shape
    w_rows, _, channels = in_weight.shape
    ch = channels // 4
    windows = window_lengths.shape[1]
    xhi, xlo, zlo, y, zhi, core = (lax.axis_index(name) for name in AXES)
    quarter = xlo * 2 + zlo
    z = zhi * 2 + zlo
    place = jnp.stack([z, zlo, core, xlo, xhi, y]).astype(jnp.int32)
    half = segs * rows

    down = jnp.concatenate(
        [lax.dynamic_index_in_dim(down_factors, task_ids[s], 0, keepdims=False).T for s in range(segs)]
    )
    own = tokens.reshape(half, depth)
    other = x_pair_swap(own)
    own = jnp.concatenate([own, down])
    held = {(0, 0): own, (0, 1): other}
    for pair, value in enumerate((own, other)):
        ahead = back = value
        for step in range(1, NZ // 2):
            ahead, back = z_step(ahead, 1), z_step(back, -1)
            held[NZ - step, pair], held[step, pair] = ahead, back
        held[NZ // 2, pair] = z_step(ahead, 1) if pair == 0 else z_step(back, -1)
    pieces = [held[d, pair] for d in range(NZ) for pair in range(2)]

    by_quarter = in_weight.reshape(w_rows, 3, 4, ch).transpose(2, 0, 1, 3).reshape(4, w_rows, 3 * ch)
    met = lax.all_to_all(jnp.concatenate([by_quarter, by_quarter]), ("xhi", "xlo", "zlo"), 0, 0, tiled=True)
    met = met.reshape(4, 2, w_rows, 3 * ch)
    kept = lax.dynamic_index_in_dim(met, core, 1, keepdims=False)
    given = core_swap(lax.dynamic_index_in_dim(met, 1 - core, 1, keepdims=False))
    weight = lax.all_gather(jnp.stack([kept, given]), "y", axis=0, tiled=False)

    up = jnp.concatenate(
        [lax.dynamic_index_in_dim(up_factors, task_ids[s], 0, keepdims=False) for s in range(segs)]
    )
    up = lax.dynamic_slice_in_dim(up, quarter * ch, ch, 2).reshape(up.shape[0], 3 * ch)
    up_other = core_swap(up)
    taps = lax.dynamic_slice_in_dim(filters, quarter * ch, ch, 0).astype(f32).T
    ends = jnp.cumsum(window_lengths, axis=1, dtype=jnp.int32)
    count = segs * windows

    def by_owner(table):
        return table.reshape(segs, 8, windows // 8).transpose(1, 0, 2).reshape(count, 1)

    lengths = by_owner(window_lengths)
    ends = by_owner(ends)
    starts = ends - lengths

    cut = (2, 2, half)
    kv_own, kv_send, low = call(
        project_kv_kernel,
        "project_kv",
        (
            jax.ShapeDtypeStruct((*cut, 2 * ch), f32),
            jax.ShapeDtypeStruct((*cut, 2 * ch), bf16),
            jax.ShapeDtypeStruct((*cut, up.shape[0]), bf16),
        ),
        (place, *pieces, weight, up, up_other),
    )
    kv = call(
        combine_kernel,
        "combine_kv",
        jax.ShapeDtypeStruct((4, segs, rows, ch), bf16),
        (place, kv_own, core_swap(kv_send)),
    )
    prev = permute(kv, lambda x, y, z, c: (x, y + 1, z, c))
    wrap = permute(kv[3], lambda x, y, z, c: (x + 2, 0, z, c), lambda x, y, z, c: x < 2 and y == NY - 1)
    q_own, q_send = call(
        project_q_kernel,
        "project_q",
        (jax.ShapeDtypeStruct((*cut, ch), f32), jax.ShapeDtypeStruct((*cut, ch), bf16)),
        (place, *pieces, weight, up, up_other, low),
    )
    q_met = core_swap(q_send)
    part = call(
        conv_own_kernel,
        "conv_own",
        jax.ShapeDtypeStruct((4, segs, rows, ch), f32),
        (kv, taps),
        [pltpu.VMEM((8 + rows, ch), f32)],
        scalars=False,
    )
    total = call(
        gate_kernel,
        "gate_pool",
        jax.ShapeDtypeStruct((NY, count, ch), f32),
        (place, part, q_own, q_met, prev, wrap, taps, starts, ends),
        [pltpu.VMEM((16 + rows, ch), f32)],
    )

    met = lax.all_to_all(total, "y", 0, 0, tiled=True)
    total = call(sum_kernel, "sum_y", jax.ShapeDtypeStruct((8, count, ch), f32), (met,), scalars=False)
    rest = ("xhi", "xlo", "zlo", "zhi", "core")
    met = lax.all_to_all(total.reshape(64, 8, ch), rest, 0, 0, tiled=True)
    met = met.reshape(2, 4, 8, 8, ch)
    whole = lax.all_gather(out_weight.astype(f32), TENSOR, axis=0, tiled=True)
    mine = lax.dynamic_slice_in_dim(lengths, (zhi * 2 + core) * 8, 8, 0)
    out = call(
        embed_kernel,
        "embed",
        jax.ShapeDtypeStruct((8, out_weight.shape[1]), bf16),
        (met, mine, whole),
        scalars=False,
    )
    return out.reshape(segs, windows // 8, out_weight.shape[1])


def solution(mesh):
    fine = Mesh(mesh.devices.reshape(SIZES), AXES)
    in_specs = (
        P(None, SEQ, TENSOR),
        P(SEQ, None, TENSOR),
        P(None, TENSOR, None),
        P(None, None, None, TENSOR),
        P(TENSOR, None),
        P(),
        P(),
        P(TENSOR, SEQ),
    )
    return jax.shard_map(local, mesh=fine, in_specs=in_specs, out_specs=P(None, TENSOR, SEQ), check_vma=False)
```

time: 198 us -> 225 us (1.14)
  local copies, waits for them, and re-layouts: 11.9 us -> 57.6 us
  blocking collectives: 40.7 us -> 16 us
  starting transfers between devices: 74.4 us -> 83.3 us
  waiting for transfers between devices: 30 us -> 27.1 us
  other arithmetic: 4.56 us -> 1.84 us
    unnamed x23 -> x132, local copies, waits for them, and re-layouts: 3.61 us -> 51 us
    all_to_all x3 -> x1, blocking collectives: 40.7 us -> 16 us  [local(): met = lax.all_to_all(total, 'y', 0, 0, tiled=True)]
    ppermute x19 -> x21, waiting for transfers between devices: 22.1 us -> 7.03 us  [permute(): return lax.ppermute(value, AXES, pairs)]
    all_to_all x1 -> x2, waiting for transfers between devices: 7.92 us -> 20.1 us  [the longest x1 13.3 us: local(): met = lax.all_to_all(total.reshape(64, 8, ch), rest, 0, 0, tiled=True)]
    all_to_all x1 -> x2, starting transfers between devices: 10 us -> 15.9 us  [the longest x1 9.26 us: local(): met = lax.all_to_all(total.reshape(64, 8, ch), rest, 0, 0, tiled=True)]
    ppermute x19 -> x21, starting transfers between devices: 63.7 us -> 67.3 us  [permute(): return lax.ppermute(value, AXES, pairs)]
    pallas_call x2 -> x7, Pallas kernels: 17.2 us -> 17.3 us  [call(): pl.pallas_call(kernel, out_shape=out, in_specs=[SMEM] * scalars + [VMEM]...]
  transfers between devices with their start and end apart: 22 -> 25, of which waited for: 5 -> 6; matrix products, arithmetic and copies ran while one was open for 4% -> 3% of each run, Pallas kernels for 0% -> 5%
where the time goes in v2:
time: 225 us; the launch traced here: 222 us
  starting transfers between devices  83.3 us (37%)
  local copies, waits for them, and re-layouts  57.6 us (26%)
  waiting for transfers between devices  27.1 us (12%)
  between operations  19.2 us (9%)
  Pallas kernels  17.3 us (8%)
  blocking collectives  16 us (7%)
    ppermute x21, starting transfers between devices, permute(): return lax.ppermute(value, AXES, pairs)  67.3 us
    unnamed x132, local copies, waits for them, and re-layouts  51 us
    pallas_call x7, Pallas kernels, call(): pl.pallas_call(kernel, out_shape=out, in_specs=[SMEM] * scalars + [VMEM]...  17.3 us
    all_to_all x1, blocking collectives, local(): met = lax.all_to_all(total, 'y', 0, 0, tiled=True)  16 us
    all_to_all x1, waiting for transfers between devices, local(): met = lax.all_to_all(total.reshape(64, 8, ch), rest, 0, 0, tiled=True)  13.3 us
    all_to_all x1, starting transfers between devices, local(): met = lax.all_to_all(total.reshape(64, 8, ch), rest, 0, 0, tiled=True)  9.26 us
    ppermute x21, waiting for transfers between devices, permute(): return lax.ppermute(value, AXES, pairs)  7.03 us
    all_to_all x1, waiting for transfers between devices, local(): lax.all_to_all(jnp.concatenate([by_quarter, by_quarter]), ('xhi', 'xlo',...  6.79 us
  transfers between devices with their start and end apart: 25, of which 6 were waited for; matrix products, arithmetic and copies ran while one was open for 3% of the time, Pallas kernels for 5%

profile of v2, /device:TPU:1, one launch (start us, length us, event | category | flops | bytes accessed | tf_op | source)
XLA Modules:
  0.0 222.3 jit_solution(16849539280370048957)
XLA Ops:
  9.5 6.7 %all-to-all-start = ((bf16[8,64,384]{2,1,0:T(8,128)(2,1)}), bf16[8,64,384]{2,1,0:T(8,128)(2,1)S(1)}, u32[]{:S(2)}, u32[]{:S(2)}) async-start(bf16[8,64,384]{2,1,0:T(8,128)(2,1)} %pad_maximum_fusion), calls=%async_computation | async-start | bytes 786432 | tf_op jit(solution)/shard_map/all_to_all | solution.py:262
  16.3 6.8 %all-to-all-done = bf16[8,64,384]{2,1,0:T(8,128)(2,1)S(1)} async-done(((bf16[8,64,384]{2,1,0:T(8,128)(2,1)}), bf16[8,64,384]{2,1,0:T(8,128)(2,1)S(1)}, u32[]{:S(2)}, u32[]{:S(2)}) %all-to-all-start) | async-done | bytes 393248 | tf_op jit(solution)/shard_map/all_to_all | solution.py:262
  23.1 6.7 %collective-permute-start.15 = (bf16[4,64,384]{2,1,0:T(8,128)(2,1)S(1)}, bf16[4,64,384]{2,1,0:T(8,128)(2,1)S(1)}, u32[]{:S(2)}, u32[]{:S(2)}) collective-permute-start(bf16[4,64,384]{2,1,0:T(8,128)(2,1)S(1)} %get-tuple-element.18), channel_id=1, source_target_pairs={{0,1},{1,0},{64,65},{65,64},{2,3},{3,2},{66,67},{67,66},{4,5},{5,4... | collective-permute-start | bytes 589832 | tf_op jit(solution)/shard_map/ppermute | solution.py:30
  31.7 1.9 collective-permute-start
  38.9 2.8 %collective-permute-start.7 = (bf16[288,512]{1,0:T(8,128)(2,1)S(1)}, bf16[288,512]{1,0:T(8,128)(2,1)S(1)}, u32[]{:S(2)}, u32[]{:S(2)}) collective-permute-start(bf16[288,512]{1,0:T(8,128)(2,1)S(1)} %pad_maximum_fusion.2.refs_0_), channel_id=1, source_target_pairs={{0,64},{1,65},{64,2},{65,3},{2,66},{3,67},{66,4},{67,5},{4,68},{5,... | collective-permute-start | bytes 884744 | tf_op jit(solution)/shard_map/ppermute | solution.py:30
  41.6 6.7 %collective-permute-start.2 = (bf16[256,512]{1,0:T(8,128)(2,1)S(1)}, bf16[256,512]{1,0:T(8,128)(2,1)S(1)}, u32[]{:S(2)}, u32[]{:S(2)}) collective-permute-start(bf16[256,512]{1,0:T(8,128)(2,1)S(1)} %collective-permute-done.refs_1_), channel_id=1, source_target_pairs={{0,70},{1,71},{64,0},{65,1},{2,64},{3,65},{66,2},{67,3},{4,66},{5,... | collective-permute-start | bytes 786440 | tf_op jit(solution)/shard_map/ppermute | solution.py:30
  48.3 3.3 %collective-permute-start.1 = (bf16[288,512]{1,0:T(8,128)(2,1)S(1)}, bf16[288,512]{1,0:T(8,128)(2,1)S(1)}, u32[]{:S(2)}, u32[]{:S(2)}) collective-permute-start(bf16[288,512]{1,0:T(8,128)(2,1)S(1)} %pad_maximum_fusion.2.refs_0_), channel_id=1, source_target_pairs={{0,70},{1,71},{64,0},{65,1},{2,64},{3,65},{66,2},{67,3},{4,66},{5,... | collective-permute-start | bytes 884744 | tf_op jit(solution)/shard_map/ppermute | solution.py:30
  53.2 1.9 collective-permute-start.8
  55.8 1.9 collective-permute-start.12
  57.8 4.6 %collective-permute-start.4 = (bf16[256,512]{1,0:T(8,128)(2,1)S(1)}, bf16[256,512]{1,0:T(8,128)(2,1)S(1)}, u32[]{:S(2)}, u32[]{:S(2)}) collective-permute-start(bf16[256,512]{1,0:T(8,128)(2,1)S(1)} %collective-permute-done.2.refs_3_), channel_id=1, source_target_pairs={{0,70},{1,71},{64,0},{65,1},{2,64},{3,65},{66,2},{67,3},{4,66},{5,... | collective-permute-start | bytes 786440 | tf_op jit(solution)/shard_map/ppermute | solution.py:30
  63.1 3.4 %collective-permute-start.3 = (bf16[288,512]{1,0:T(8,128)(2,1)S(1)}, bf16[288,512]{1,0:T(8,128)(2,1)S(1)}, u32[]{:S(2)}, u32[]{:S(2)}) collective-permute-start(bf16[288,512]{1,0:T(8,128)(2,1)S(1)} %collective-permute-done.1.refs_2_), channel_id=1, source_target_pairs={{0,70},{1,71},{64,0},{65,1},{2,64},{3,65},{66,2},{67,3},{4,66},{5,... | collective-permute-start | bytes 884744 | tf_op jit(solution)/shard_map/ppermute | solution.py:30
  67.1 1.9 collective-permute-start.9
  69.8 1.9 collective-permute-start.13
  72.4 4.6 %collective-permute-start.6 = (bf16[256,512]{1,0:T(8,128)(2,1)S(1)}, bf16[256,512]{1,0:T(8,128)(2,1)S(1)}, u32[]{:S(2)}, u32[]{:S(2)}) collective-permute-start(bf16[256,512]{1,0:T(8,128)(2,1)S(1)} %collective-permute-done.4.refs_5_), channel_id=1, source_target_pairs={{0,70},{1,71},{64,0},{65,1},{2,64},{3,65},{66,2},{67,3},{4,66},{5,... | collective-permute-start | bytes 786440 | tf_op jit(solution)/shard_map/ppermute | solution.py:30
  77.7 3.4 %collective-permute-start.5 = (bf16[288,512]{1,0:T(8,128)(2,1)S(1)}, bf16[288,512]{1,0:T(8,128)(2,1)S(1)}, u32[]{:S(2)}, u32[]{:S(2)}) collective-permute-start(bf16[288,512]{1,0:T(8,128)(2,1)S(1)} %collective-permute-done.3.refs_4_), channel_id=1, source_target_pairs={{0,70},{1,71},{64,0},{65,1},{2,64},{3,65},{66,2},{67,3},{4,66},{5,... | collective-permute-start | bytes 884744 | tf_op jit(solution)/shard_map/ppermute | solution.py:30
  81.0 1.9 collective-permute-start.10
  83.7 1.9 collective-permute-start.14
  86.3 4.6 %collective-permute-start.11 = (bf16[256,512]{1,0:T(8,128)(2,1)S(1)}, bf16[256,512]{1,0:T(8,128)(2,1)S(1)}, u32[]{:S(2)}, u32[]{:S(2)}) collective-permute-start(bf16[256,512]{1,0:T(8,128)(2,1)S(1)} %collective-permute-done.6.refs_7_), channel_id=1, source_target_pairs={{0,70},{1,71},{64,0},{65,1},{2,64},{3,65},{66,2},{67,3},{4,66},{5,... | collective-permute-start | bytes 786440 | tf_op jit(solution)/shard_map/ppermute | solution.py:30
  92.4 6.0 %collective-permute-start.16 = (bf16[32,384]{1,0:T(8,128)(2,1)S(1)}, bf16[32,384]{1,0:T(8,128)(2,1)S(1)}, u32[]{:S(2)}, u32[]{:S(2)}) collective-permute-start(bf16[32,384]{1,0:T(8,128)(2,1)S(1)} %copy_bitcast_fusion.1.refs_17_), channel_id=1, source_target_pairs={{0,1},{1,0},{64,65},{65,64},{2,3},{3,2},{66,67},{67,66},{4,5},{5,4... | collective-permute-start | bytes 73736 | tf_op jit(solution)/shard_map/ppermute | solution.py:30
  102.8 1.9 copy-done.1
  120.5 5.2 %project_kv.1 = (f32[2,2,256,256]{3,2,1,0:T(8,128)S(1)}, bf16[2,2,256,256]{3,2,1,0:T(8,128)(2,1)}, bf16[2,2,256,32]{3,2,1,0:T(8,128)(2,1)S(1)}) custom-call(s32[6]{0:T(128)S(1)} %stack.36.place, bf16[288,512]{1,0:T(8,128)(2,1)S(1)} %copy-done.4, bf16[256,512]{1,0:T(8,128)(2,1)S(1)} %collective-permute-done.refs_1_, bf16[288,512]{1,0:T(8,128)(2,1)S(1)} %copy-done.11, ...), custom_call_target="tpu_custom_call" | custom-call | tf_op jit(solution)/shard_map/project_kv/pallas_call | solution.py:223
  127.4 2.2 %collective-permute-start.17 = (bf16[2,2,256,256]{3,2,1,0:T(8,128)(2,1)}, bf16[2,2,256,256]{3,2,1,0:T(8,128)(2,1)}, u32[]{:S(2)}, u32[]{:S(2)}) collective-permute-start(bf16[2,2,256,256]{3,2,1,0:T(8,128)(2,1)} %get-tuple-element.11), channel_id=1, source_target_pairs={{0,1},{1,0},{64,65},{65,64},{2,3},{3,2},{66,67},{67,66},{4,5},{5,4... | collective-permute-start | bytes 1572872 | tf_op jit(solution)/shard_map/ppermute | solution.py:30
  129.6 1.7 copy.45
  150.2 2.6 %project_q.1 = (f32[2,2,256,128]{3,2,1,0:T(8,128)S(1)}, bf16[2,2,256,128]{3,2,1,0:T(8,128)(2,1)}) custom-call(s32[6]{0:T(128)S(1)} %stack.36.place, bf16[288,512]{1,0:T(8,128)(2,1)S(1)} %copy-done.5, bf16[256,512]{1,0:T(8,128)(2,1)S(1)} %collective-permute-done.refs_1_, bf16[288,512]{1,0:T(8,128)(2,1)S(1)} %copy-done.12, bf16[256,512]{1,0:T(8,128)(2,1)S(1)} %copy-done.30, ...), custom_call_target="tpu_custom_call" | custom-call | tf_op jit(solution)/shard_map/project_q/pallas_call | solution.py:223
  152.9 2.0 collective-permute-start.18
  156.1 3.2 %collective-permute-start.19 = (bf16[4,2,128,128]{3,2,1,0:T(8,128)(2,1)S(1)}, bf16[4,2,128,128]{3,2,1,0:T(8,128)(2,1)S(1)}, u32[]{:S(2)}, u32[]{:S(2)}) collective-permute-start(bf16[4,2,128,128]{3,2,1,0:T(8,128)(2,1)S(1)} %combine_kv.1.kv_ref), channel_id=1, source_target_pairs={{0,8},{1,9},{64,72},{65,73},{2,10},{3,11},{66,74},{67,75},{4,12},{... | collective-permute-start | bytes 786440 | tf_op jit(solution)/shard_map/ppermute | solution.py:30
  160.8 2.4 %conv_own.1.part_ref = f32[4,2,128,128]{3,2,1,0:T(8,128)S(1)} custom-call(bf16[4,2,128,128]{3,2,1,0:T(8,128)(2,1)S(1)} %combine_kv.1.kv_ref, f32[128,128]{1,0:T(8,128)S(1)} %convert_bitcast_fusion.taps_ref), custom_call_target="tpu_custom_call" | custom-call | tf_op jit(solution)/shard_map/conv_own/pallas_call | solution.py:223
  163.2 4.4 %collective-permute-done.19.prev_ref = bf16[4,2,128,128]{3,2,1,0:T(8,128)(2,1)S(1)} collective-permute-done((bf16[4,2,128,128]{3,2,1,0:T(8,128)(2,1)S(1)}, bf16[4,2,128,128]{3,2,1,0:T(8,128)(2,1)S(1)}, u32[]{:S(2)}, u32[]{:S(2)}) %collective-permute-start.19) | collective-permute-done | bytes 262176 | tf_op jit(solution)/shard_map/ppermute | solution.py:30
  168.7 4.3 %gate_pool.1 = f32[8,64,128]{2,1,0:T(8,128)S(1)} custom-call(s32[6]{0:T(128)S(1)} %stack.36.place, f32[4,2,128,128]{3,2,1,0:T(8,128)S(1)} %conv_own.1.part_ref, f32[2,2,256,128]{3,2,1,0:T(8,128)S(1)} %copy-done.52, bf16[2,2,256,128]{3,2,1,0:T(8,128)(2,1)S(1)} %collective-permute-done.18.met_ref, ...), custom_call_target="tpu_custom_call" | custom-call | tf_op jit(solution)/shard_map/gate_pool/pallas_call | solution.py:223
  173.0 16.0 %all_to_all.15.met_ref = f32[8,64,128]{2,1,0:T(8,128)S(1)} all-to-all(f32[8,64,128]{2,1,0:T(8,128)S(1)} %gate_pool.1), channel_id=1, replica_groups=mesh['xhi'=2,'xlo'=2,'zlo'=2,'y'=8,'zhi'=4,'core'=2] {'y'}, dimensions={0} | all-to-all | bytes 524288 | tf_op jit(solution)/shard_map/all_to_all | solution.py:326
  189.7 9.3 %all-to-all-start.2 = ((f32[64,8,128]{2,1,0:T(8,128)}), f32[64,8,128]{2,1,0:T(8,128)S(1)}, u32[]{:S(2)}, u32[]{:S(2)}) async-start(f32[64,8,128]{2,1,0:T(8,128)} %bitcast.25), calls=%async_computation.2 | async-start | bytes 524288 | tf_op jit(solution)/shard_map/all_to_all | solution.py:329
  199.1 13.3 %all-to-all-done.2 = f32[64,8,128]{2,1,0:T(8,128)S(1)} async-done(((f32[64,8,128]{2,1,0:T(8,128)}), f32[64,8,128]{2,1,0:T(8,128)S(1)}, u32[]{:S(2)}, u32[]{:S(2)}) %all-to-all-start.2) | async-done | bytes 262176 | tf_op jit(solution)/shard_map/all_to_all | solution.py:329
  (187 shorter events, 62.1 us)
Async XLA Ops:
  7.4 123.9 %copy-start = (bf16[512,128]{1,0:T(8,128)(2,1)S(1)}, bf16[512,128]{1,0:T(8,128)(2,1)}, u32[]{:S(2)}) copy-start(bf16[512,128]{1,0:T(8,128)(2,1)} %param.12) | copy-start | bytes 393220
  7.4 24.3 %copy-start.61 = (bf16[2,128,512]{2,1,0:T(8,128)(2,1)S(1)}, bf16[2,128,512]{2,1,0:T(8,128)(2,1)}, u32[]{:S(2)}) copy-start(bf16[2,128,512]{2,1,0:T(8,128)(2,1)} %param.8) | copy-start | bytes 786436
  7.4 26.3 %copy-start.64 = (s32[2]{0:T(128)S(1)}, s32[2]{0:T(128)}, u32[]{:S(2)}) copy-start(s32[2]{0:T(128)} %param.13) | copy-start | bytes 28
  9.5 13.5 %all-to-all-start = ((bf16[8,64,384]{2,1,0:T(8,128)(2,1)}), bf16[8,64,384]{2,1,0:T(8,128)(2,1)S(1)}, u32[]{:S(2)}, u32[]{:S(2)}) async-start(bf16[8,64,384]{2,1,0:T(8,128)(2,1)} %pad_maximum_fusion), calls=%async_computation | async-start | bytes 786432 | tf_op jit(solution)/shard_map/all_to_all | solution.py:262
  16.2 86.6 %all-gather.6.cloned.1.call-start = ((), (), s32[]{:S(2)}) async-start(), calls=%async_computation.4 | async-start | bytes 3538944 | tf_op jit(solution)/shard_map/all_gather | solution.py:266
  23.1 7.7 %collective-permute-start.15 = (bf16[4,64,384]{2,1,0:T(8,128)(2,1)S(1)}, bf16[4,64,384]{2,1,0:T(8,128)(2,1)S(1)}, u32[]{:S(2)}, u32[]{:S(2)}) collective-permute-start(bf16[4,64,384]{2,1,0:T(8,128)(2,1)S(1)} %get-tuple-element.18), channel_id=1, source_target_pairs={{0,1},{1,0},{64,65},{65,64},{2,3},{3,2},{66,67},{67,66},{4,5},{5,4... | collective-permute-start | bytes 589832 | tf_op jit(solution)/shard_map/ppermute | solution.py:30
  31.6 167.5 %all-gather.4.cloned.1.call-start = ((), (), s32[]{:S(2)}) async-start(), calls=%async_computation.3 | async-start | bytes 2359296 | tf_op jit(solution)/shard_map/all_gather | solution.py:331
  31.7 9.9 %collective-permute-start = (bf16[256,512]{1,0:T(8,128)(2,1)S(1)}, bf16[256,512]{1,0:T(8,128)(2,1)S(1)}, u32[]{:S(2)}, u32[]{:S(2)}) collective-permute-start(bf16[256,512]{1,0:T(8,128)(2,1)S(1)} %bitcast.52), channel_id=1, source_target_pairs={{0,128},{1,129},{64,192},{65,193},{2,130},{3,131},{66,194},{67,195... | collective-permute-start | bytes 786440 | tf_op jit(solution)/shard_map/ppermute | solution.py:30
  38.9 14.3 %collective-permute-start.7 = (bf16[288,512]{1,0:T(8,128)(2,1)S(1)}, bf16[288,512]{1,0:T(8,128)(2,1)S(1)}, u32[]{:S(2)}, u32[]{:S(2)}) collective-permute-start(bf16[288,512]{1,0:T(8,128)(2,1)S(1)} %pad_maximum_fusion.2.refs_0_), channel_id=1, source_target_pairs={{0,64},{1,65},{64,2},{65,3},{2,66},{3,67},{66,4},{67,5},{4,68},{5,... | collective-permute-start | bytes 884744 | tf_op jit(solution)/shard_map/ppermute | solution.py:30
  41.6 16.1 %collective-permute-start.2 = (bf16[256,512]{1,0:T(8,128)(2,1)S(1)}, bf16[256,512]{1,0:T(8,128)(2,1)S(1)}, u32[]{:S(2)}, u32[]{:S(2)}) collective-permute-start(bf16[256,512]{1,0:T(8,128)(2,1)S(1)} %collective-permute-done.refs_1_), channel_id=1, source_target_pairs={{0,70},{1,71},{64,0},{65,1},{2,64},{3,65},{66,2},{67,3},{4,66},{5,... | collective-permute-start | bytes 786440 | tf_op jit(solution)/shard_map/ppermute | solution.py:30
  48.3 14.8 %collective-permute-start.1 = (bf16[288,512]{1,0:T(8,128)(2,1)S(1)}, bf16[288,512]{1,0:T(8,128)(2,1)S(1)}, u32[]{:S(2)}, u32[]{:S(2)}) collective-permute-start(bf16[288,512]{1,0:T(8,128)(2,1)S(1)} %pad_maximum_fusion.2.refs_0_), channel_id=1, source_target_pairs={{0,70},{1,71},{64,0},{65,1},{2,64},{3,65},{66,2},{67,3},{4,66},{5,... | collective-permute-start | bytes 884744 | tf_op jit(solution)/shard_map/ppermute | solution.py:30
  53.2 13.9 %collective-permute-start.8 = (bf16[288,512]{1,0:T(8,128)(2,1)S(1)}, bf16[288,512]{1,0:T(8,128)(2,1)S(1)}, u32[]{:S(2)}, u32[]{:S(2)}) collective-permute-start(bf16[288,512]{1,0:T(8,128)(2,1)S(1)} %collective-permute-done.7.refs_14_), channel_id=1, source_target_pairs={{0,64},{1,65},{64,2},{65,3},{2,66},{3,67},{66,4},{67,5},{4,68},{5,... | collective-permute-start | bytes 884744 | tf_op jit(solution)/shard_map/ppermute | solution.py:30
  55.8 13.9 %collective-permute-start.12 = (bf16[256,512]{1,0:T(8,128)(2,1)S(1)}, bf16[256,512]{1,0:T(8,128)(2,1)S(1)}, u32[]{:S(2)}, u32[]{:S(2)}) collective-permute-start(bf16[256,512]{1,0:T(8,128)(2,1)S(1)} %collective-permute-done.refs_1_), channel_id=1, source_target_pairs={{0,64},{1,65},{64,2},{65,3},{2,66},{3,67},{66,4},{67,5},{4,68},{5,... | collective-permute-start | bytes 786440 | tf_op jit(solution)/shard_map/ppermute | solution.py:30
  57.8 14.6 %collective-permute-start.4 = (bf16[256,512]{1,0:T(8,128)(2,1)S(1)}, bf16[256,512]{1,0:T(8,128)(2,1)S(1)}, u32[]{:S(2)}, u32[]{:S(2)}) collective-permute-start(bf16[256,512]{1,0:T(8,128)(2,1)S(1)} %collective-permute-done.2.refs_3_), channel_id=1, source_target_pairs={{0,70},{1,71},{64,0},{65,1},{2,64},{3,65},{66,2},{67,3},{4,66},{5,... | collective-permute-start | bytes 786440 | tf_op jit(solution)/shard_map/ppermute | solution.py:30
  63.1 14.6 %collective-permute-start.3 = (bf16[288,512]{1,0:T(8,128)(2,1)S(1)}, bf16[288,512]{1,0:T(8,128)(2,1)S(1)}, u32[]{:S(2)}, u32[]{:S(2)}) collective-permute-start(bf16[288,512]{1,0:T(8,128)(2,1)S(1)} %collective-permute-done.1.refs_2_), channel_id=1, source_target_pairs={{0,70},{1,71},{64,0},{65,1},{2,64},{3,65},{66,2},{67,3},{4,66},{5,... | collective-permute-start | bytes 884744 | tf_op jit(solution)/shard_map/ppermute | solution.py:30
  67.1 13.9 %collective-permute-start.9 = (bf16[288,512]{1,0:T(8,128)(2,1)S(1)}, bf16[288,512]{1,0:T(8,128)(2,1)S(1)}, u32[]{:S(2)}, u32[]{:S(2)}) collective-permute-start(bf16[288,512]{1,0:T(8,128)(2,1)S(1)} %collective-permute-done.8.refs_12_), channel_id=1, source_target_pairs={{0,64},{1,65},{64,2},{65,3},{2,66},{3,67},{66,4},{67,5},{4,68},{5,... | collective-permute-start | bytes 884744 | tf_op jit(solution)/shard_map/ppermute | solution.py:30
  69.8 13.9 %collective-permute-start.13 = (bf16[256,512]{1,0:T(8,128)(2,1)S(1)}, bf16[256,512]{1,0:T(8,128)(2,1)S(1)}, u32[]{:S(2)}, u32[]{:S(2)}) collective-permute-start(bf16[256,512]{1,0:T(8,128)(2,1)S(1)} %collective-permute-done.12.refs_15_), channel_id=1, source_target_pairs={{0,64},{1,65},{64,2},{65,3},{2,66},{3,67},{66,4},{67,5},{4,68},{5,... | collective-permute-start | bytes 786440 | tf_op jit(solution)/shard_map/ppermute | solution.py:30
  72.4 13.9 %collective-permute-start.6 = (bf16[256,512]{1,0:T(8,128)(2,1)S(1)}, bf16[256,512]{1,0:T(8,128)(2,1)S(1)}, u32[]{:S(2)}, u32[]{:S(2)}) collective-permute-start(bf16[256,512]{1,0:T(8,128)(2,1)S(1)} %collective-permute-done.4.refs_5_), channel_id=1, source_target_pairs={{0,70},{1,71},{64,0},{65,1},{2,64},{3,65},{66,2},{67,3},{4,66},{5,... | collective-permute-start | bytes 786440 | tf_op jit(solution)/shard_map/ppermute | solution.py:30
  77.7 25.1 %copy-start.16 = (bf16[288,512]{1,0:T(8,128)(2,1)}, bf16[288,512]{1,0:T(8,128)(2,1)S(1)}, u32[]{:S(2)}) copy-start(bf16[288,512]{1,0:T(8,128)(2,1)S(1)} %collective-permute-done.3.refs_4_) | copy-start | bytes 884740
  77.7 22.2 %collective-permute-start.5 = (bf16[288,512]{1,0:T(8,128)(2,1)S(1)}, bf16[288,512]{1,0:T(8,128)(2,1)S(1)}, u32[]{:S(2)}, u32[]{:S(2)}) collective-permute-start(bf16[288,512]{1,0:T(8,128)(2,1)S(1)} %collective-permute-done.3.refs_4_), channel_id=1, source_target_pairs={{0,70},{1,71},{64,0},{65,1},{2,64},{3,65},{66,2},{67,3},{4,66},{5,... | collective-permute-start | bytes 884744 | tf_op jit(solution)/shard_map/ppermute | solution.py:30
  81.0 20.3 %collective-permute-start.10 = (bf16[288,512]{1,0:T(8,128)(2,1)S(1)}, bf16[288,512]{1,0:T(8,128)(2,1)S(1)}, u32[]{:S(2)}, u32[]{:S(2)}) collective-permute-start(bf16[288,512]{1,0:T(8,128)(2,1)S(1)} %collective-permute-done.9.refs_10_), channel_id=1, source_target_pairs={{0,64},{1,65},{64,2},{65,3},{2,66},{3,67},{66,4},{67,5},{4,68},{5,... | collective-permute-start | bytes 884744 | tf_op jit(solution)/shard_map/ppermute | solution.py:30
  83.7 16.9 %collective-permute-start.14 = (bf16[256,512]{1,0:T(8,128)(2,1)S(1)}, bf16[256,512]{1,0:T(8,128)(2,1)S(1)}, u32[]{:S(2)}, u32[]{:S(2)}) collective-permute-start(bf16[256,512]{1,0:T(8,128)(2,1)S(1)} %collective-permute-done.13.refs_13_), channel_id=1, source_target_pairs={{0,64},{1,65},{64,2},{65,3},{2,66},{3,67},{66,4},{67,5},{4,68},{5,... | collective-permute-start | bytes 786440 | tf_op jit(solution)/shard_map/ppermute | solution.py:30
  86.3 15.7 %collective-permute-start.11 = (bf16[256,512]{1,0:T(8,128)(2,1)S(1)}, bf16[256,512]{1,0:T(8,128)(2,1)S(1)}, u32[]{:S(2)}, u32[]{:S(2)}) collective-permute-start(bf16[256,512]{1,0:T(8,128)(2,1)S(1)} %collective-permute-done.6.refs_7_), channel_id=1, source_target_pairs={{0,70},{1,71},{64,0},{65,1},{2,64},{3,65},{66,2},{67,3},{4,66},{5,... | collective-permute-start | bytes 786440 | tf_op jit(solution)/shard_map/ppermute | solution.py:30
  92.4 10.4 %copy-start.55 = (bf16[32,384]{1,0:T(8,128)(2,1)}, bf16[32,384]{1,0:T(8,128)(2,1)S(1)}, u32[]{:S(2)}) copy-start(bf16[32,384]{1,0:T(8,128)(2,1)S(1)} %copy_bitcast_fusion.1.refs_17_) | copy-start | bytes 73732
  92.4 6.8 %collective-permute-start.16 = (bf16[32,384]{1,0:T(8,128)(2,1)S(1)}, bf16[32,384]{1,0:T(8,128)(2,1)S(1)}, u32[]{:S(2)}, u32[]{:S(2)}) collective-permute-start(bf16[32,384]{1,0:T(8,128)(2,1)S(1)} %copy_bitcast_fusion.1.refs_17_), channel_id=1, source_target_pairs={{0,1},{1,0},{64,65},{65,64},{2,3},{3,2},{66,67},{67,66},{4,5},{5,4... | collective-permute-start | bytes 73736 | tf_op jit(solution)/shard_map/ppermute | solution.py:30
  120.5 12.9 %copy-start.2 = (bf16[16,4,64,384]{3,2,1,0:T(8,128)(2,1)S(1)}, bf16[16,4,64,384]{3,2,1,0:T(8,128)(2,1)}, u32[]{:S(2)}) copy-start(bf16[16,4,64,384]{3,2,1,0:T(8,128)(2,1)} %all-gather.6.cloned.1.call-done) | copy-start | bytes 9437188
  127.4 27.5 %collective-permute-start.17 = (bf16[2,2,256,256]{3,2,1,0:T(8,128)(2,1)}, bf16[2,2,256,256]{3,2,1,0:T(8,128)(2,1)}, u32[]{:S(2)}, u32[]{:S(2)}) collective-permute-start(bf16[2,2,256,256]{3,2,1,0:T(8,128)(2,1)} %get-tuple-element.11), channel_id=1, source_target_pairs={{0,1},{1,0},{64,65},{65,64},{2,3},{3,2},{66,67},{67,66},{4,5},{5,4... | collective-permute-start | bytes 1572872 | tf_op jit(solution)/shard_map/ppermute | solution.py:30
  150.2 9.8 %copy-start.63 = (s32[2,32]{1,0:T(2,128)S(1)}, s32[2,32]{1,0:T(2,128)}, u32[]{:S(2)}) copy-start(s32[2,32]{1,0:T(2,128)} %param.14) | copy-start | bytes 772
  152.9 10.4 %collective-permute-start.18 = (bf16[2,2,256,128]{3,2,1,0:T(8,128)(2,1)}, bf16[2,2,256,128]{3,2,1,0:T(8,128)(2,1)S(1)}, u32[]{:S(2)}, u32[]{:S(2)}) collective-permute-start(bf16[2,2,256,128]{3,2,1,0:T(8,128)(2,1)} %get-tuple-element.14), channel_id=1, source_target_pairs={{0,1},{1,0},{64,65},{65,64},{2,3},{3,2},{66,67},{67,66},{4,5},{5,4... | collective-permute-start | bytes 786440 | tf_op jit(solution)/shard_map/ppermute | solution.py:30
  156.1 11.5 %collective-permute-start.19 = (bf16[4,2,128,128]{3,2,1,0:T(8,128)(2,1)S(1)}, bf16[4,2,128,128]{3,2,1,0:T(8,128)(2,1)S(1)}, u32[]{:S(2)}, u32[]{:S(2)}) collective-permute-start(bf16[4,2,128,128]{3,2,1,0:T(8,128)(2,1)S(1)} %combine_kv.1.kv_ref), channel_id=1, source_target_pairs={{0,8},{1,9},{64,72},{65,73},{2,10},{3,11},{66,74},{67,75},{4,12},{... | collective-permute-start | bytes 786440 | tf_op jit(solution)/shard_map/ppermute | solution.py:30
  159.3 3.9 %collective-permute-start.20 = (bf16[2,128,128]{2,1,0:T(8,128)(2,1)S(1)}, bf16[2,128,128]{2,1,0:T(8,128)(2,1)S(1)}, u32[]{:S(2)}, u32[]{:S(2)}) collective-permute-start(bf16[2,128,128]{2,1,0:T(8,128)(2,1)S(1)} %slice_bitcast_fusion), channel_id=1, source_target_pairs={{56,256},{57,257},{120,320},{121,321},{58,258},{59,259},{122,322},... | collective-permute-start | bytes 196616 | tf_op jit(solution)/shard_map/ppermute | solution.py:30
  189.7 22.7 %all-to-all-start.2 = ((f32[64,8,128]{2,1,0:T(8,128)}), f32[64,8,128]{2,1,0:T(8,128)S(1)}, u32[]{:S(2)}, u32[]{:S(2)}) async-start(f32[64,8,128]{2,1,0:T(8,128)} %bitcast.25), calls=%async_computation.2 | async-start | bytes 524288 | tf_op jit(solution)/shard_map/all_to_all | solution.py:329
  (58 other events, 70.4 us)
Sparse Core Ops, SparseCore 0:
  31.8 46.2 all-gather.5
Sparse Core Ops, SparseCore 1:
  131.4 37.4 all-gather.3

commit v3 on v2

--- a/solution.py
+++ b/solution.py
@@ -46,8 +46,16 @@
     return lax.dot_general(a, b, (((1,), (1,)), ((), ())), preferred_element_type=jnp.float32)
 
 
-def pieces_of(refs):
-    return [refs[2 * d : 2 * d + 2] for d in range(NZ)]
+def fetch(sources, targets, sems):
+    copies = [pltpu.make_async_copy(a, b, sems.at[i]) for i, (a, b) in enumerate(zip(sources, targets))]
+    for copy in copies:
+        copy.start()
+    return copies
+
+
+def targets_of(own_buf, other_buf, weight_buf):
+    rows = [buf.at[d] for d in range(NZ) for buf in (own_buf, other_buf)]
+    return rows + [weight_buf.at[side] for side in range(2)]
 
 
 def distances(rel):
@@ -58,8 +66,8 @@
     blocks = []
     for dist in distances(rel):
         zhi = lax.rem(z + dist, NZ) // 2
-        block = weight[:, side, pl.ds(zhi, 1), :, columns]
-        blocks.append(block.reshape(weight.shape[0] * weight.shape[3], block.shape[-1]))
+        block = weight[side, :, pl.ds(zhi, 1), :, columns]
+        blocks.append(block.reshape(weight.shape[1] * weight.shape[3], block.shape[-1]))
     return jnp.concatenate(blocks, axis=0)
 
 
@@ -68,8 +76,11 @@
 
 
 def project_kv_kernel(place, *refs):
-    pieces = pieces_of(refs)
-    weight, up, up_other, own_ref, send_ref, low_ref = refs[2 * NZ :]
+    sources = refs[: 2 * NZ + 2]
+    up, up_other, own_ref, send_ref, low_ref, own_buf, other_buf, weight, sems = refs[2 * NZ + 2 :]
+    for copy in fetch(sources, targets_of(own_buf, other_buf, weight), sems):
+        copy.wait()
+    pieces = [(own_buf.at[d], other_buf.at[d]) for d in range(NZ)]
     z = place[0]
     half = own_ref.shape[2]
     ch = up.shape[1] // 3
@@ -98,8 +109,11 @@
 
 
 def project_q_kernel(place, *refs):
-    pieces = pieces_of(refs)
-    weight, up, up_other, low_ref, own_ref, send_ref = refs[2 * NZ :]
+    sources = refs[: 2 * NZ + 2]
+    up, up_other, low_ref, own_ref, send_ref, own_buf, other_buf, weight, sems = refs[2 * NZ + 2 :]
+    for copy in fetch(sources, targets_of(own_buf, other_buf, weight), sems):
+        copy.wait()
+    pieces = [(own_buf.at[d], other_buf.at[d]) for d in range(NZ)]
     z = place[0]
     half = own_ref.shape[2]
     ch = up.shape[1] // 3
@@ -152,12 +166,12 @@
     lax.fori_loop(0, 8, block, 0)
 
 
-def gate_kernel(place, part_ref, own_ref, met_ref, prev_ref, wrap_ref, taps_ref, start_ref, end_ref, out_ref, ext):
+def gate_kernel(place, part_ref, own_ref, met_ref, prev_ref, wrap_ref, taps_ref, start_ref, end_ref, out_ref, ext, sums):
     z_lo, x_lo, x_hi, y = place[1], place[3], place[4], place[5]
     rows, ch = part_ref.shape[2], part_ref.shape[3]
     groups = rows // 8
     count = out_ref.shape[1]
-    out_ref[0] = jnp.zeros((count, ch), jnp.float32)
+    sums[...] = jnp.zeros((count, ch), jnp.float32)
     row = lax.broadcasted_iota(jnp.int32, (count, rows), 0)
     column = lax.broadcasted_iota(jnp.int32, (count, rows), 1)
     row_seg = lax.rem(row // 4, 2)
@@ -187,20 +201,20 @@
         position = (((x_hi * 2 + x_at) * 2 + z_at) * NY + y) * rows + column
         inside = (position >= start_ref[...]) & (position < end_ref[...]) & (row_seg == seg)
         member = inside.astype(jnp.float32).astype(jnp.bfloat16)
-        out_ref[0] += jnp.dot(member, gated, preferred_element_type=jnp.float32)
+        sums[...] += jnp.dot(member, gated, preferred_element_type=jnp.float32)
         return carry
 
     lax.fori_loop(0, 8, block, 0)
-    for copy in range(1, out_ref.shape[0]):
-        out_ref[copy] = out_ref[0]
+    for copy in range(out_ref.shape[0]):
+        out_ref[copy] = sums[...].astype(out_ref.dtype)
 
 
 def sum_kernel(met_ref, out_ref):
-    total = met_ref[0]
+    total = met_ref[0].astype(jnp.float32)
     for i in range(1, met_ref.shape[0]):
-        total = total + met_ref[i]
+        total = total + met_ref[i].astype(jnp.float32)
     for copy in range(out_ref.shape[0]):
-        out_ref[copy] = total
+        out_ref[copy] = total.astype(out_ref.dtype)
 
 
 def embed_kernel(met_ref, length_ref, weight_ref, out_ref):
@@ -208,7 +222,7 @@
     means = []
     for t in range(met_ref.shape[2]):
         for quarter in range(met_ref.shape[1]):
-            total = met_ref[0, quarter, t] + met_ref[1, quarter, t]
+            total = met_ref[0, quarter, t].astype(jnp.float32) + met_ref[1, quarter, t].astype(jnp.float32)
             means.append((total / length).astype(jnp.bfloat16))
     means = jnp.concatenate(means, axis=1)
     weight = weight_ref[...].astype(jnp.bfloat16)
@@ -219,11 +233,14 @@
 SMEM = pl.BlockSpec(memory_space=pltpu.SMEM)
 
 
-def call(kernel, name, out, operands, scratch=(), vmem=32, scalars=True):
+ANY = pl.BlockSpec(memory_space=pl.ANY)
+
+
+def call(kernel, name, out, operands, scratch=(), vmem=24, scalars=True, where=0):
     return pl.pallas_call(
         kernel,
         out_shape=out,
-        in_specs=[SMEM] * scalars + [VMEM] * (len(operands) - scalars),
+        in_specs=[SMEM] * scalars + [ANY] * where + [VMEM] * (len(operands) - scalars - where),
         out_specs=jax.tree.map(lambda _: VMEM, out),
         scratch_shapes=list(scratch),
         compiler_params=pltpu.CompilerParams(vmem_limit_bytes=vmem << 20),
@@ -249,21 +266,15 @@
     own = tokens.reshape(half, depth)
     other = x_pair_swap(own)
     own = jnp.concatenate([own, down])
-    held = {(0, 0): own, (0, 1): other}
-    for pair, value in enumerate((own, other)):
-        ahead = back = value
-        for step in range(1, NZ // 2):
-            ahead, back = z_step(ahead, 1), z_step(back, -1)
-            held[NZ - step, pair], held[step, pair] = ahead, back
-        held[NZ // 2, pair] = z_step(ahead, 1) if pair == 0 else z_step(back, -1)
-    pieces = [held[d, pair] for d in range(NZ) for pair in range(2)]
+    ahead, back = z_step(own, 1), z_step(own, -1)
 
     by_quarter = in_weight.reshape(w_rows, 3, 4, ch).transpose(2, 0, 1, 3).reshape(4, w_rows, 3 * ch)
     met = lax.all_to_all(jnp.concatenate([by_quarter, by_quarter]), ("xhi", "xlo", "zlo"), 0, 0, tiled=True)
+    ahead, back, other, met = lax.optimization_barrier((ahead, back, other, met))
     met = met.reshape(4, 2, w_rows, 3 * ch)
     kept = lax.dynamic_index_in_dim(met, core, 1, keepdims=False)
     given = core_swap(lax.dynamic_index_in_dim(met, 1 - core, 1, keepdims=False))
-    weight = lax.all_gather(jnp.stack([kept, given]), "y", axis=0, tiled=False)
+    weights = [lax.all_gather(side, "y", axis=0, tiled=False) for side in (kept, given)]
 
     up = jnp.concatenate(
         [lax.dynamic_index_in_dim(up_factors, task_ids[s], 0, keepdims=False) for s in range(segs)]
@@ -280,8 +291,32 @@
     lengths = by_owner(window_lengths)
     ends = by_owner(ends)
     starts = ends - lengths
+    mine = lax.dynamic_slice_in_dim(lengths, (zhi * 2 + core) * 8, 8, 0)
+    wide = out_weight.astype(f32)
+
+    held = {(0, 0): own, (0, 1): other, (NZ - 1, 0): ahead, (1, 0): back}
+    held[NZ - 1, 1], held[1, 1] = z_step(other, 1), z_step(other, -1)
+    for step in range(2, NZ // 2):
+        for pair in range(2):
+            held[NZ - step, pair] = z_step(held[NZ - step + 1, pair], 1)
+            held[step, pair] = z_step(held[step - 1, pair], -1)
+        if step == 2:
+            early = [held[NZ - 2, 0], up, up_other, taps, starts, ends, mine, wide, place]
+            early = lax.optimization_barrier(early)
+            held[NZ - 2, 0], up, up_other, taps, starts, ends, mine, wide, place = early
+    held[NZ // 2, 0] = z_step(held[NZ // 2 + 1, 0], 1)
+    held[NZ // 2, 1] = z_step(held[NZ // 2 - 1, 1], -1)
+    pieces = [held[d, pair] for d in range(NZ) for pair in range(2)]
+    *weights, wide = lax.optimization_barrier((*weights, wide))
+    whole = lax.all_gather(wide, TENSOR, axis=0, tiled=True)
 
     cut = (2, 2, half)
+    buffers = [
+        pltpu.VMEM((NZ, *own.shape), bf16),
+        pltpu.VMEM((NZ, *other.shape), bf16),
+        pltpu.VMEM((2, *weights[0].shape), bf16),
+        pltpu.SemaphoreType.DMA((2 * NZ + 2,)),
+    ]
     kv_own, kv_send, low = call(
         project_kv_kernel,
         "project_kv",
@@ -290,7 +325,9 @@
             jax.ShapeDtypeStruct((*cut, 2 * ch), bf16),
             jax.ShapeDtypeStruct((*cut, up.shape[0]), bf16),
         ),
-        (place, *pieces, weight, up, up_other),
+        (place, *pieces, *weights, up, up_other),
+        buffers,
+        where=len(pieces) + 2,
     )
     kv = call(
         combine_kernel,
@@ -304,7 +341,9 @@
         project_q_kernel,
         "project_q",
         (jax.ShapeDtypeStruct((*cut, ch), f32), jax.ShapeDtypeStruct((*cut, ch), bf16)),
-        (place, *pieces, weight, up, up_other, low),
+        (place, *pieces, *weights, up, up_other, low),
+        buffers,
+        where=len(pieces) + 2,
     )
     q_met = core_swap(q_send)
     part = call(
@@ -318,18 +357,17 @@
     total = call(
         gate_kernel,
         "gate_pool",
-        jax.ShapeDtypeStruct((NY, count, ch), f32),
+        jax.ShapeDtypeStruct((NY, count, ch), bf16),
         (place, part, q_own, q_met, prev, wrap, taps, starts, ends),
-        [pltpu.VMEM((16 + rows, ch), f32)],
+        [pltpu.VMEM((16 + rows, ch), f32), pltpu.VMEM((count, ch), f32)],
     )
 
     met = lax.all_to_all(total, "y", 0, 0, tiled=True)
-    total = call(sum_kernel, "sum_y", jax.ShapeDtypeStruct((8, count, ch), f32), (met,), scalars=False)
+    total = call(sum_kernel, "sum_y", jax.ShapeDtypeStruct((8, count, ch), bf16), (met,), scalars=False)
     rest = ("xhi", "xlo", "zlo", "zhi", "core")
+    total, whole, mine = lax.optimization_barrier((total, whole, mine))
     met = lax.all_to_all(total.reshape(64, 8, ch), rest, 0, 0, tiled=True)
     met = met.reshape(2, 4, 8, 8, ch)
-    whole = lax.all_gather(out_weight.astype(f32), TENSOR, axis=0, tiled=True)
-    mine = lax.dynamic_slice_in_dim(lengths, (zhi * 2 + core) * 8, 8, 0)
     out = call(
         embed_kernel,
         "embed",

time: 225 us -> 260 us (1.16)
  waiting for transfers between devices: 27.1 us -> 97.4 us
  local copies, waits for them, and re-layouts: 57.6 us -> 10.3 us
  blocking collectives: 16 us -> 37.4 us
  starting transfers between devices: 83.3 us -> 78.1 us
    all_gather x2 -> x3, waiting for transfers between devices: 0.01 us -> 61.1 us  [the longest x2 61.1 us: local(): lax.all_gather(side, 'y', axis=0, tiled=False)]
    unnamed x132 -> x20, local copies, waits for them, and re-layouts: 51 us -> 5.34 us
    ppermute x21, waiting for transfers between devices: 7.03 us -> 36.2 us  [permute(): return lax.ppermute(value, AXES, pairs)]
    all_to_all x0 -> x1, blocking collectives: none -> 25.7 us  [local(): met = lax.all_to_all(total.reshape(64, 8, ch), rest, 0, 0, tiled=True)]
    all_to_all x1 -> x0, waiting for transfers between devices: 13.3 us -> none  [local(): met = lax.all_to_all(total.reshape(64, 8, ch), rest, 0, 0, tiled=True)]
    all_to_all x1 -> x0, starting transfers between devices: 9.26 us -> none  [local(): met = lax.all_to_all(total.reshape(64, 8, ch), rest, 0, 0, tiled=True)]
    all_to_all x1, waiting for transfers between devices: 6.79 us -> 0.01 us  [local(): lax.all_to_all(jnp.concatenate([by_quarter, by_quarter]), ('xhi', 'xlo',...]
    all_to_all x1, blocking collectives: 16 us -> 11.7 us  [local(): met = lax.all_to_all(total, 'y', 0, 0, tiled=True)]
  transfers between devices with their start and end apart: 25 -> 25, of which waited for: 6 -> 9; matrix products, arithmetic and copies ran while one was open for 3% -> 2% of each run, Pallas kernels for 5% -> 6%
where the time goes in v3:
time: 260 us; the launch traced here: 259 us
  waiting for transfers between devices  97.4 us (37%)
  starting transfers between devices  78.1 us (30%)
  blocking collectives  37.4 us (14%)
  between operations  17.5 us (7%)
  Pallas kernels  16.6 us (6%)
  local copies, waits for them, and re-layouts  10.3 us (4%)
    ppermute x21, starting transfers between devices, permute(): return lax.ppermute(value, AXES, pairs)  71.2 us
    all_gather x2, waiting for transfers between devices, local(): lax.all_gather(side, 'y', axis=0, tiled=False)  61.1 us
    ppermute x21, waiting for transfers between devices, permute(): return lax.ppermute(value, AXES, pairs)  36.2 us
    all_to_all x1, blocking collectives, local(): met = lax.all_to_all(total.reshape(64, 8, ch), rest, 0, 0, tiled=True)  25.7 us
    pallas_call x7, Pallas kernels, call(): pl.pallas_call(kernel, out_shape=out, in_specs=[SMEM] * scalars + [ANY] *...  16.6 us
    all_to_all x1, blocking collectives, local(): met = lax.all_to_all(total, 'y', 0, 0, tiled=True)  11.7 us
    all_to_all x1, starting transfers between devices, local(): lax.all_to_all(jnp.concatenate([by_quarter, by_quarter]), ('xhi', 'xlo',...  6.79 us
    unnamed x20, local copies, waits for them, and re-layouts  5.34 us
  transfers between devices with their start and end apart: 25, of which 9 were waited for; matrix products, arithmetic and copies ran while one was open for 2% of the time, Pallas kernels for 6%

profile of v3, /device:TPU:1, one launch (start us, length us, event | category | flops | bytes accessed | tf_op | source)
XLA Modules:
  0.0 259.1 jit_solution(3471315322237723613)
XLA Ops:
  8.7 6.8 %all-to-all-start = ((bf16[8,64,384]{2,1,0:T(8,128)(2,1)}), bf16[8,64,384]{2,1,0:T(8,128)(2,1)S(1)}, u32[]{:S(2)}, u32[]{:S(2)}) async-start(bf16[8,64,384]{2,1,0:T(8,128)(2,1)} %pad_maximum_fusion), calls=%async_computation | async-start | bytes 786432 | tf_op jit(solution)/shard_map/all_to_all | solution.py:272
  21.0 3.3 %collective-permute-start = (bf16[288,512]{1,0:T(8,128)(2,1)S(1)}, bf16[288,512]{1,0:T(8,128)(2,1)S(1)}, u32[]{:S(2)}, u32[]{:S(2)}) collective-permute-start(bf16[288,512]{1,0:T(8,128)(2,1)S(1)} %pad_maximum_fusion.1.refs_0_), channel_id=1, source_target_pairs={{0,64},{1,65},{64,2},{65,3},{2,66},{3,67},{66,4},{67,5},{4,68},{5,... | collective-permute-start | bytes 884744 | tf_op jit(solution)/shard_map/ppermute | solution.py:30
  24.3 8.6 %collective-permute-start.1 = (bf16[288,512]{1,0:T(8,128)(2,1)S(1)}, bf16[288,512]{1,0:T(8,128)(2,1)S(1)}, u32[]{:S(2)}, u32[]{:S(2)}) collective-permute-start(bf16[288,512]{1,0:T(8,128)(2,1)S(1)} %pad_maximum_fusion.1.refs_0_), channel_id=1, source_target_pairs={{0,70},{1,71},{64,0},{65,1},{2,64},{3,65},{66,2},{67,3},{4,66},{5,... | collective-permute-start | bytes 884744 | tf_op jit(solution)/shard_map/ppermute | solution.py:30
  32.9 3.1 %collective-permute-start.2 = (bf16[256,512]{1,0:T(8,128)(2,1)S(1)}, bf16[256,512]{1,0:T(8,128)(2,1)S(1)}, u32[]{:S(2)}, u32[]{:S(2)}) collective-permute-start(bf16[256,512]{1,0:T(8,128)(2,1)S(1)} %bitcast.54), channel_id=1, source_target_pairs={{0,128},{1,129},{64,192},{65,193},{2,130},{3,131},{66,194},{67,195... | collective-permute-start | bytes 786440 | tf_op jit(solution)/shard_map/ppermute | solution.py:30
  36.0 5.1 %collective-permute-done.2.refs_1_ = bf16[256,512]{1,0:T(8,128)(2,1)S(1)} collective-permute-done((bf16[256,512]{1,0:T(8,128)(2,1)S(1)}, bf16[256,512]{1,0:T(8,128)(2,1)S(1)}, u32[]{:S(2)}, u32[]{:S(2)}) %collective-permute-start.2) | collective-permute-done | bytes 262176 | tf_op jit(solution)/shard_map/ppermute | solution.py:30
  41.9 4.3 %collective-permute-start.16 = (bf16[4,64,384]{2,1,0:T(8,128)(2,1)S(1)}, bf16[4,64,384]{2,1,0:T(8,128)(2,1)S(1)}, u32[]{:S(2)}, u32[]{:S(2)}) collective-permute-start(bf16[4,64,384]{2,1,0:T(8,128)(2,1)S(1)} %get-tuple-element.53), channel_id=1, source_target_pairs={{0,1},{1,0},{64,65},{65,64},{2,3},{3,2},{66,67},{67,66},{4,5},{5,4... | collective-permute-start | bytes 589832 | tf_op jit(solution)/shard_map/ppermute | solution.py:30
  48.9 2.3 collective-permute-start.4
  53.4 4.6 %collective-permute-start.5 = (bf16[256,512]{1,0:T(8,128)(2,1)S(1)}, bf16[256,512]{1,0:T(8,128)(2,1)S(1)}, u32[]{:S(2)}, u32[]{:S(2)}) collective-permute-start(bf16[256,512]{1,0:T(8,128)(2,1)S(1)} %collective-permute-done.2.refs_1_), channel_id=1, source_target_pairs={{0,70},{1,71},{64,0},{65,1},{2,64},{3,65},{66,2},{67,3},{4,66},{5,... | collective-permute-start | bytes 786440 | tf_op jit(solution)/shard_map/ppermute | solution.py:30
  59.5 3.6 %collective-permute-done.3.refs_12_ = bf16[288,512]{1,0:T(8,128)(2,1)S(1)} collective-permute-done((bf16[288,512]{1,0:T(8,128)(2,1)S(1)}, bf16[288,512]{1,0:T(8,128)(2,1)S(1)}, u32[]{:S(2)}, u32[]{:S(2)}) %collective-permute-start.3) | collective-permute-done | bytes 294944 | tf_op jit(solution)/shard_map/ppermute | solution.py:30
  63.1 17.6 %all-gather.8.cloned.1.call-done = bf16[32,1,64,384]{3,2,1,0:T(8,128)(2,1)} async-done(((bf16[4,1,64,384]{3,2,1,0:T(8,128)(2,1)}), bf16[32,1,64,384]{3,2,1,0:T(8,128)(2,1)}) %all-gather.8.cloned.1.call-update) | async-done | bytes 1572880 | tf_op jit(solution)/shard_map/all_gather | solution.py:277
  80.7 43.5 %all-gather.10.cloned.1.call-done = bf16[32,64,384]{2,1,0:T(8,128)(2,1)} async-done(((bf16[4,64,384]{2,1,0:T(8,128)(2,1)}), bf16[32,64,384]{2,1,0:T(8,128)(2,1)}) %all-gather.10.cloned.1.call-update) | async-done | bytes 1572880 | tf_op jit(solution)/shard_map/all_gather | solution.py:277
  124.2 3.3 %collective-permute-start.13 = (bf16[256,512]{1,0:T(8,128)(2,1)S(1)}, bf16[256,512]{1,0:T(8,128)(2,1)S(1)}, u32[]{:S(2)}, u32[]{:S(2)}) collective-permute-start(bf16[256,512]{1,0:T(8,128)(2,1)S(1)} %collective-permute-done.2.refs_1_), channel_id=1, source_target_pairs={{0,64},{1,65},{64,2},{65,3},{2,66},{3,67},{66,4},{67,5},{4,68},{5,... | collective-permute-start | bytes 786440 | tf_op jit(solution)/shard_map/ppermute | solution.py:30
  127.5 4.2 %collective-permute-start.7 = (bf16[256,512]{1,0:T(8,128)(2,1)S(1)}, bf16[256,512]{1,0:T(8,128)(2,1)S(1)}, u32[]{:S(2)}, u32[]{:S(2)}) collective-permute-start(bf16[256,512]{1,0:T(8,128)(2,1)S(1)} %collective-permute-done.5.refs_3_), channel_id=1, source_target_pairs={{0,70},{1,71},{64,0},{65,1},{2,64},{3,65},{66,2},{67,3},{4,66},{5,... | collective-permute-start | bytes 786440 | tf_op jit(solution)/shard_map/ppermute | solution.py:30
  131.7 3.4 %collective-permute-start.6 = (bf16[288,512]{1,0:T(8,128)(2,1)S(1)}, bf16[288,512]{1,0:T(8,128)(2,1)S(1)}, u32[]{:S(2)}, u32[]{:S(2)}) collective-permute-start(bf16[288,512]{1,0:T(8,128)(2,1)S(1)} %collective-permute-done.1.refs_2_), channel_id=1, source_target_pairs={{0,70},{1,71},{64,0},{65,1},{2,64},{3,65},{66,2},{67,3},{4,66},{5,... | collective-permute-start | bytes 884744 | tf_op jit(solution)/shard_map/ppermute | solution.py:30
  135.1 1.9 collective-permute-start.10
  137.0 1.9 collective-permute-start.14
  139.0 4.6 %collective-permute-start.9 = (bf16[256,512]{1,0:T(8,128)(2,1)S(1)}, bf16[256,512]{1,0:T(8,128)(2,1)S(1)}, u32[]{:S(2)}, u32[]{:S(2)}) collective-permute-start(bf16[256,512]{1,0:T(8,128)(2,1)S(1)} %collective-permute-done.7.refs_5_), channel_id=1, source_target_pairs={{0,70},{1,71},{64,0},{65,1},{2,64},{3,65},{66,2},{67,3},{4,66},{5,... | collective-permute-start | bytes 786440 | tf_op jit(solution)/shard_map/ppermute | solution.py:30
  143.6 3.4 %collective-permute-start.8 = (bf16[288,512]{1,0:T(8,128)(2,1)S(1)}, bf16[288,512]{1,0:T(8,128)(2,1)S(1)}, u32[]{:S(2)}, u32[]{:S(2)}) collective-permute-start(bf16[288,512]{1,0:T(8,128)(2,1)S(1)} %collective-permute-done.6.refs_4_), channel_id=1, source_target_pairs={{0,70},{1,71},{64,0},{65,1},{2,64},{3,65},{66,2},{67,3},{4,66},{5,... | collective-permute-start | bytes 884744 | tf_op jit(solution)/shard_map/ppermute | solution.py:30
  148.9 2.0 collective-permute-start.15
  150.9 3.3 %collective-permute-done.9.refs_7_ = bf16[256,512]{1,0:T(8,128)(2,1)S(1)} collective-permute-done((bf16[256,512]{1,0:T(8,128)(2,1)S(1)}, bf16[256,512]{1,0:T(8,128)(2,1)S(1)}, u32[]{:S(2)}, u32[]{:S(2)}) %collective-permute-start.9) | collective-permute-done | bytes 262176 | tf_op jit(solution)/shard_map/ppermute | solution.py:30
  154.2 6.2 %collective-permute-start.12 = (bf16[256,512]{1,0:T(8,128)(2,1)S(1)}, bf16[256,512]{1,0:T(8,128)(2,1)S(1)}, u32[]{:S(2)}, u32[]{:S(2)}) collective-permute-start(bf16[256,512]{1,0:T(8,128)(2,1)S(1)} %collective-permute-done.9.refs_7_), channel_id=1, source_target_pairs={{0,70},{1,71},{64,0},{65,1},{2,64},{3,65},{66,2},{67,3},{4,66},{5,... | collective-permute-start | bytes 786440 | tf_op jit(solution)/shard_map/ppermute | solution.py:30
  160.5 11.0 %collective-permute-done.8.refs_6_ = bf16[288,512]{1,0:T(8,128)(2,1)S(1)} collective-permute-done((bf16[288,512]{1,0:T(8,128)(2,1)S(1)}, bf16[288,512]{1,0:T(8,128)(2,1)S(1)}, u32[]{:S(2)}, u32[]{:S(2)}) %collective-permute-start.8) | collective-permute-done | bytes 294944 | tf_op jit(solution)/shard_map/ppermute | solution.py:30
  171.5 7.8 %collective-permute-done.15.refs_11_ = bf16[256,512]{1,0:T(8,128)(2,1)S(1)} collective-permute-done((bf16[256,512]{1,0:T(8,128)(2,1)S(1)}, bf16[256,512]{1,0:T(8,128)(2,1)S(1)}, u32[]{:S(2)}, u32[]{:S(2)}) %collective-permute-start.15) | collective-permute-done | bytes 262176 | tf_op jit(solution)/shard_map/ppermute | solution.py:30
  182.0 5.4 %project_kv.1 = (f32[2,2,256,256]{3,2,1,0:T(8,128)S(1)}, bf16[2,2,256,256]{3,2,1,0:T(8,128)(2,1)S(1)}, bf16[2,2,256,32]{3,2,1,0:T(8,128)(2,1)S(1)}) custom-call(s32[6]{0:T(128)S(1)} %stack.27.place, bf16[288,512]{1,0:T(8,128)(2,1)S(1)} %pad_maximum_fusion.1.refs_0_, bf16[256,512]{1,0:T(8,128)(2,1)S(1)} %collective-permute-done.2.refs_1_, ...), custom_call_target="tpu_custom_call" | custom-call | tf_op jit(solution)/shard_map/project_kv/pallas_call | solution.py:240
  187.4 4.8 %collective-permute-start.17 = (bf16[2,2,256,256]{3,2,1,0:T(8,128)(2,1)S(1)}, bf16[2,2,256,256]{3,2,1,0:T(8,128)(2,1)S(1)}, u32[]{:S(2)}, u32[]{:S(2)}) collective-permute-start(bf16[2,2,256,256]{3,2,1,0:T(8,128)(2,1)S(1)} %get-tuple-element.41), channel_id=1, source_target_pairs={{0,1},{1,0},{64,65},{65,64},{2,3},{3,2},{66,67},{67,66},{4,5},{5,4... | collective-permute-start | bytes 1572872 | tf_op jit(solution)/shard_map/ppermute | solution.py:30
  192.3 3.0 %project_q.1 = (f32[2,2,256,128]{3,2,1,0:T(8,128)S(1)}, bf16[2,2,256,128]{3,2,1,0:T(8,128)(2,1)S(1)}) custom-call(s32[6]{0:T(128)S(1)} %stack.27.place, bf16[288,512]{1,0:T(8,128)(2,1)S(1)} %pad_maximum_fusion.1.refs_0_, bf16[256,512]{1,0:T(8,128)(2,1)S(1)} %collective-permute-done.2.refs_1_, bf16[288,512]{1,0:T(8,128)(2,1)S(1)} %collective-permute-done.1.refs_2_, ...), custom_call_target="tpu_custom_call" | custom-call | tf_op jit(solution)/shard_map/project_q/pallas_call | solution.py:240
  197.8 2.9 %collective-permute-start.19 = (bf16[4,2,128,128]{3,2,1,0:T(8,128)(2,1)S(1)}, bf16[4,2,128,128]{3,2,1,0:T(8,128)(2,1)S(1)}, u32[]{:S(2)}, u32[]{:S(2)}) collective-permute-start(bf16[4,2,128,128]{3,2,1,0:T(8,128)(2,1)S(1)} %combine_kv.1.kv_ref), channel_id=1, source_target_pairs={{0,8},{1,9},{64,72},{65,73},{2,10},{3,11},{66,74},{67,75},{4,12},{... | collective-permute-start | bytes 786440 | tf_op jit(solution)/shard_map/ppermute | solution.py:30
  201.5 2.4 conv_own.1.part_ref
  203.9 4.4 %collective-permute-done.19.prev_ref = bf16[4,2,128,128]{3,2,1,0:T(8,128)(2,1)S(1)} collective-permute-done((bf16[4,2,128,128]{3,2,1,0:T(8,128)(2,1)S(1)}, bf16[4,2,128,128]{3,2,1,0:T(8,128)(2,1)S(1)}, u32[]{:S(2)}, u32[]{:S(2)}) %collective-permute-start.19) | collective-permute-done | bytes 262176 | tf_op jit(solution)/shard_map/ppermute | solution.py:30
  208.3 4.3 %gate_pool.1 = bf16[8,64,128]{2,1,0:T(8,128)(2,1)S(1)} custom-call(s32[6]{0:T(128)S(1)} %stack.27.place, f32[4,2,128,128]{3,2,1,0:T(8,128)S(1)} %conv_own.1.part_ref, f32[2,2,256,128]{3,2,1,0:T(8,128)S(1)} %get-tuple-element.44.own_ref, bf16[2,2,256,128]{3,2,1,0:T(8,128)(2,1)S(1)} %collective-permute-done.18.met_ref, ...), custom_call_target="tpu_custom_call" | custom-call | tf_op jit(solution)/shard_map/gate_pool/pallas_call | solution.py:240
  212.6 11.7 %all_to_all.15.met_ref = bf16[8,64,128]{2,1,0:T(8,128)(2,1)S(1)} all-to-all(bf16[8,64,128]{2,1,0:T(8,128)(2,1)S(1)} %gate_pool.1), channel_id=1, replica_groups=mesh['xhi'=2,'xlo'=2,'zlo'=2,'y'=8,'zhi'=4,'core'=2] {'y'}, dimensions={0} | all-to-all | bytes 262144 | tf_op jit(solution)/shard_map/all_to_all | solution.py:365
  224.4 25.7 %all_to_all.16 = bf16[64,8,128]{2,1,0:T(8,128)(2,1)S(1)} all-to-all(bf16[64,8,128]{2,1,0:T(8,128)(2,1)S(1)} %bitcast.50), channel_id=1, replica_groups=mesh['xhi'=2,'xlo'=2,'zlo'=2,'y'=8,'zhi'=4,'core'=2] {'xhi','xlo','zlo',..., dimensions={0} | all-to-all | bytes 262144 | tf_op jit(solution)/shard_map/all_to_all | solution.py:369
  (76 shorter events, 21.3 us)
Async XLA Ops:
  6.5 44.7 %copy-start = (bf16[512,128]{1,0:T(8,128)(2,1)S(1)}, bf16[512,128]{1,0:T(8,128)(2,1)}, u32[]{:S(2)}) copy-start(bf16[512,128]{1,0:T(8,128)(2,1)} %param.12) | copy-start | bytes 393220
  6.5 9.0 %copy-start.8 = (s32[2]{0:T(128)S(1)}, s32[2]{0:T(128)}, u32[]{:S(2)}) copy-start(s32[2]{0:T(128)} %param.13) | copy-start | bytes 28
  6.5 14.4 %copy-start.4 = (bf16[2,128,512]{2,1,0:T(8,128)(2,1)S(1)}, bf16[2,128,512]{2,1,0:T(8,128)(2,1)}, u32[]{:S(2)}) copy-start(bf16[2,128,512]{2,1,0:T(8,128)(2,1)} %param.8) | copy-start | bytes 786436
  8.7 42.6 %copy-start.7 = (s32[2,32]{1,0:T(2,128)S(1)}, s32[2,32]{1,0:T(2,128)}, u32[]{:S(2)}) copy-start(s32[2,32]{1,0:T(2,128)} %param.14) | copy-start | bytes 772
  8.7 49.9 %copy-start.6 = (bf16[512,64]{0,1:T(8,128)(2,1)S(1)}, bf16[512,64]{0,1:T(8,128)(2,1)}, u32[]{:S(2)}) copy-start(bf16[512,64]{0,1:T(8,128)(2,1)} %param.15) | copy-start | bytes 196612
  8.7 32.4 %all-to-all-start = ((bf16[8,64,384]{2,1,0:T(8,128)(2,1)}), bf16[8,64,384]{2,1,0:T(8,128)(2,1)S(1)}, u32[]{:S(2)}, u32[]{:S(2)}) async-start(bf16[8,64,384]{2,1,0:T(8,128)(2,1)} %pad_maximum_fusion), calls=%async_computation | async-start | bytes 786432 | tf_op jit(solution)/shard_map/all_to_all | solution.py:272
  15.5 65.2 %all-gather.8.cloned.1.call-start = ((), (), s32[]{:S(2)}) async-start(), calls=%async_computation.4 | async-start | bytes 1769472 | tf_op jit(solution)/shard_map/all_gather | solution.py:277
  21.0 20.1 %collective-permute-start = (bf16[288,512]{1,0:T(8,128)(2,1)S(1)}, bf16[288,512]{1,0:T(8,128)(2,1)S(1)}, u32[]{:S(2)}, u32[]{:S(2)}) collective-permute-start(bf16[288,512]{1,0:T(8,128)(2,1)S(1)} %pad_maximum_fusion.1.refs_0_), channel_id=1, source_target_pairs={{0,64},{1,65},{64,2},{65,3},{2,66},{3,67},{66,4},{67,5},{4,68},{5,... | collective-permute-start | bytes 884744 | tf_op jit(solution)/shard_map/ppermute | solution.py:30
  24.3 16.8 %collective-permute-start.1 = (bf16[288,512]{1,0:T(8,128)(2,1)S(1)}, bf16[288,512]{1,0:T(8,128)(2,1)S(1)}, u32[]{:S(2)}, u32[]{:S(2)}) collective-permute-start(bf16[288,512]{1,0:T(8,128)(2,1)S(1)} %pad_maximum_fusion.1.refs_0_), channel_id=1, source_target_pairs={{0,70},{1,71},{64,0},{65,1},{2,64},{3,65},{66,2},{67,3},{4,66},{5,... | collective-permute-start | bytes 884744 | tf_op jit(solution)/shard_map/ppermute | solution.py:30
  32.9 8.2 %collective-permute-start.2 = (bf16[256,512]{1,0:T(8,128)(2,1)S(1)}, bf16[256,512]{1,0:T(8,128)(2,1)S(1)}, u32[]{:S(2)}, u32[]{:S(2)}) collective-permute-start(bf16[256,512]{1,0:T(8,128)(2,1)S(1)} %bitcast.54), channel_id=1, source_target_pairs={{0,128},{1,129},{64,192},{65,193},{2,130},{3,131},{66,194},{67,195... | collective-permute-start | bytes 786440 | tf_op jit(solution)/shard_map/ppermute | solution.py:30
  41.8 82.3 %all-gather.10.cloned.1.call-start = ((), (), s32[]{:S(2)}) async-start(), calls=%async_computation.5 | async-start | bytes 1769472 | tf_op jit(solution)/shard_map/all_gather | solution.py:277
  41.9 5.4 %collective-permute-start.16 = (bf16[4,64,384]{2,1,0:T(8,128)(2,1)S(1)}, bf16[4,64,384]{2,1,0:T(8,128)(2,1)S(1)}, u32[]{:S(2)}, u32[]{:S(2)}) collective-permute-start(bf16[4,64,384]{2,1,0:T(8,128)(2,1)S(1)} %get-tuple-element.53), channel_id=1, source_target_pairs={{0,1},{1,0},{64,65},{65,64},{2,3},{3,2},{66,67},{67,66},{4,5},{5,4... | collective-permute-start | bytes 589832 | tf_op jit(solution)/shard_map/ppermute | solution.py:30
  48.0 176.4 %all-gather.6.cloned.1.call-start = ((), (), s32[]{:S(2)}) async-start(), calls=%async_computation.3 | async-start | bytes 2359296 | tf_op jit(solution)/shard_map/all_gather | solution.py:311
  48.9 10.6 %collective-permute-start.4 = (bf16[32,384]{1,0:T(8,128)(2,1)S(1)}, bf16[32,384]{1,0:T(8,128)(2,1)S(1)}, u32[]{:S(2)}, u32[]{:S(2)}) collective-permute-start(bf16[32,384]{1,0:T(8,128)(2,1)S(1)} %copy_bitcast_fusion.1.refs_18_), channel_id=1, source_target_pairs={{0,1},{1,0},{64,65},{65,64},{2,3},{3,2},{66,67},{67,66},{4,5},{5,4... | collective-permute-start | bytes 73736 | tf_op jit(solution)/shard_map/ppermute | solution.py:30
  51.5 11.6 %collective-permute-start.3 = (bf16[288,512]{1,0:T(8,128)(2,1)S(1)}, bf16[288,512]{1,0:T(8,128)(2,1)S(1)}, u32[]{:S(2)}, u32[]{:S(2)}) collective-permute-start(bf16[288,512]{1,0:T(8,128)(2,1)S(1)} %collective-permute-done.refs_14_), channel_id=1, source_target_pairs={{0,64},{1,65},{64,2},{65,3},{2,66},{3,67},{66,4},{67,5},{4,68},{5,... | collective-permute-start | bytes 884744 | tf_op jit(solution)/shard_map/ppermute | solution.py:30
  53.4 74.1 %collective-permute-start.5 = (bf16[256,512]{1,0:T(8,128)(2,1)S(1)}, bf16[256,512]{1,0:T(8,128)(2,1)S(1)}, u32[]{:S(2)}, u32[]{:S(2)}) collective-permute-start(bf16[256,512]{1,0:T(8,128)(2,1)S(1)} %collective-permute-done.2.refs_1_), channel_id=1, source_target_pairs={{0,70},{1,71},{64,0},{65,1},{2,64},{3,65},{66,2},{67,3},{4,66},{5,... | collective-permute-start | bytes 786440 | tf_op jit(solution)/shard_map/ppermute | solution.py:30
  124.2 12.8 %collective-permute-start.13 = (bf16[256,512]{1,0:T(8,128)(2,1)S(1)}, bf16[256,512]{1,0:T(8,128)(2,1)S(1)}, u32[]{:S(2)}, u32[]{:S(2)}) collective-permute-start(bf16[256,512]{1,0:T(8,128)(2,1)S(1)} %collective-permute-done.2.refs_1_), channel_id=1, source_target_pairs={{0,64},{1,65},{64,2},{65,3},{2,66},{3,67},{66,4},{67,5},{4,68},{5,... | collective-permute-start | bytes 786440 | tf_op jit(solution)/shard_map/ppermute | solution.py:30
  127.5 11.5 %collective-permute-start.7 = (bf16[256,512]{1,0:T(8,128)(2,1)S(1)}, bf16[256,512]{1,0:T(8,128)(2,1)S(1)}, u32[]{:S(2)}, u32[]{:S(2)}) collective-permute-start(bf16[256,512]{1,0:T(8,128)(2,1)S(1)} %collective-permute-done.5.refs_3_), channel_id=1, source_target_pairs={{0,70},{1,71},{64,0},{65,1},{2,64},{3,65},{66,2},{67,3},{4,66},{5,... | collective-permute-start | bytes 786440 | tf_op jit(solution)/shard_map/ppermute | solution.py:30
  131.7 11.8 %collective-permute-start.6 = (bf16[288,512]{1,0:T(8,128)(2,1)S(1)}, bf16[288,512]{1,0:T(8,128)(2,1)S(1)}, u32[]{:S(2)}, u32[]{:S(2)}) collective-permute-start(bf16[288,512]{1,0:T(8,128)(2,1)S(1)} %collective-permute-done.1.refs_2_), channel_id=1, source_target_pairs={{0,70},{1,71},{64,0},{65,1},{2,64},{3,65},{66,2},{67,3},{4,66},{5,... | collective-permute-start | bytes 884744 | tf_op jit(solution)/shard_map/ppermute | solution.py:30
  135.1 11.8 %collective-permute-start.10 = (bf16[288,512]{1,0:T(8,128)(2,1)S(1)}, bf16[288,512]{1,0:T(8,128)(2,1)S(1)}, u32[]{:S(2)}, u32[]{:S(2)}) collective-permute-start(bf16[288,512]{1,0:T(8,128)(2,1)S(1)} %collective-permute-done.3.refs_12_), channel_id=1, source_target_pairs={{0,64},{1,65},{64,2},{65,3},{2,66},{3,67},{66,4},{67,5},{4,68},{5,... | collective-permute-start | bytes 884744 | tf_op jit(solution)/shard_map/ppermute | solution.py:30
  137.0 11.8 %collective-permute-start.14 = (bf16[256,512]{1,0:T(8,128)(2,1)S(1)}, bf16[256,512]{1,0:T(8,128)(2,1)S(1)}, u32[]{:S(2)}, u32[]{:S(2)}) collective-permute-start(bf16[256,512]{1,0:T(8,128)(2,1)S(1)} %collective-permute-done.13.refs_15_), channel_id=1, source_target_pairs={{0,64},{1,65},{64,2},{65,3},{2,66},{3,67},{66,4},{67,5},{4,68},{5,... | collective-permute-start | bytes 786440 | tf_op jit(solution)/shard_map/ppermute | solution.py:30
  139.0 15.3 %collective-permute-start.9 = (bf16[256,512]{1,0:T(8,128)(2,1)S(1)}, bf16[256,512]{1,0:T(8,128)(2,1)S(1)}, u32[]{:S(2)}, u32[]{:S(2)}) collective-permute-start(bf16[256,512]{1,0:T(8,128)(2,1)S(1)} %collective-permute-done.7.refs_5_), channel_id=1, source_target_pairs={{0,70},{1,71},{64,0},{65,1},{2,64},{3,65},{66,2},{67,3},{4,66},{5,... | collective-permute-start | bytes 786440 | tf_op jit(solution)/shard_map/ppermute | solution.py:30
  143.6 27.9 %collective-permute-start.8 = (bf16[288,512]{1,0:T(8,128)(2,1)S(1)}, bf16[288,512]{1,0:T(8,128)(2,1)S(1)}, u32[]{:S(2)}, u32[]{:S(2)}) collective-permute-start(bf16[288,512]{1,0:T(8,128)(2,1)S(1)} %collective-permute-done.6.refs_4_), channel_id=1, source_target_pairs={{0,70},{1,71},{64,0},{65,1},{2,64},{3,65},{66,2},{67,3},{4,66},{5,... | collective-permute-start | bytes 884744 | tf_op jit(solution)/shard_map/ppermute | solution.py:30
  147.0 32.3 %collective-permute-start.11 = (bf16[288,512]{1,0:T(8,128)(2,1)S(1)}, bf16[288,512]{1,0:T(8,128)(2,1)S(1)}, u32[]{:S(2)}, u32[]{:S(2)}) collective-permute-start(bf16[288,512]{1,0:T(8,128)(2,1)S(1)} %collective-permute-done.10.refs_10_), channel_id=1, source_target_pairs={{0,64},{1,65},{64,2},{65,3},{2,66},{3,67},{66,4},{67,5},{4,68},{5,... | collective-permute-start | bytes 884744 | tf_op jit(solution)/shard_map/ppermute | solution.py:30
  148.9 30.3 %collective-permute-start.15 = (bf16[256,512]{1,0:T(8,128)(2,1)S(1)}, bf16[256,512]{1,0:T(8,128)(2,1)S(1)}, u32[]{:S(2)}, u32[]{:S(2)}) collective-permute-start(bf16[256,512]{1,0:T(8,128)(2,1)S(1)} %collective-permute-done.14.refs_13_), channel_id=1, source_target_pairs={{0,64},{1,65},{64,2},{65,3},{2,66},{3,67},{66,4},{67,5},{4,68},{5,... | collective-permute-start | bytes 786440 | tf_op jit(solution)/shard_map/ppermute | solution.py:30
  154.2 25.0 %collective-permute-start.12 = (bf16[256,512]{1,0:T(8,128)(2,1)S(1)}, bf16[256,512]{1,0:T(8,128)(2,1)S(1)}, u32[]{:S(2)}, u32[]{:S(2)}) collective-permute-start(bf16[256,512]{1,0:T(8,128)(2,1)S(1)} %collective-permute-done.9.refs_7_), channel_id=1, source_target_pairs={{0,70},{1,71},{64,0},{65,1},{2,64},{3,65},{66,2},{67,3},{4,66},{5,... | collective-permute-start | bytes 786440 | tf_op jit(solution)/shard_map/ppermute | solution.py:30
  179.2 1.4 copy-start.1
  187.4 9.8 %collective-permute-start.17 = (bf16[2,2,256,256]{3,2,1,0:T(8,128)(2,1)S(1)}, bf16[2,2,256,256]{3,2,1,0:T(8,128)(2,1)S(1)}, u32[]{:S(2)}, u32[]{:S(2)}) collective-permute-start(bf16[2,2,256,256]{3,2,1,0:T(8,128)(2,1)S(1)} %get-tuple-element.41), channel_id=1, source_target_pairs={{0,1},{1,0},{64,65},{65,64},{2,3},{3,2},{66,67},{67,66},{4,5},{5,4... | collective-permute-start | bytes 1572872 | tf_op jit(solution)/shard_map/ppermute | solution.py:30
  195.3 8.6 %collective-permute-start.18 = (bf16[2,2,256,128]{3,2,1,0:T(8,128)(2,1)S(1)}, bf16[2,2,256,128]{3,2,1,0:T(8,128)(2,1)S(1)}, u32[]{:S(2)}, u32[]{:S(2)}) collective-permute-start(bf16[2,2,256,128]{3,2,1,0:T(8,128)(2,1)S(1)} %get-tuple-element.45), channel_id=1, source_target_pairs={{0,1},{1,0},{64,65},{65,64},{2,3},{3,2},{66,67},{67,66},{4,5},{5,4... | collective-permute-start | bytes 786440 | tf_op jit(solution)/shard_map/ppermute | solution.py:30
  197.8 10.5 %collective-permute-start.19 = (bf16[4,2,128,128]{3,2,1,0:T(8,128)(2,1)S(1)}, bf16[4,2,128,128]{3,2,1,0:T(8,128)(2,1)S(1)}, u32[]{:S(2)}, u32[]{:S(2)}) collective-permute-start(bf16[4,2,128,128]{3,2,1,0:T(8,128)(2,1)S(1)} %combine_kv.1.kv_ref), channel_id=1, source_target_pairs={{0,8},{1,9},{64,72},{65,73},{2,10},{3,11},{66,74},{67,75},{4,12},{... | collective-permute-start | bytes 786440 | tf_op jit(solution)/shard_map/ppermute | solution.py:30
  200.7 3.2 %collective-permute-start.20 = (bf16[2,128,128]{2,1,0:T(8,128)(2,1)S(1)}, bf16[2,128,128]{2,1,0:T(8,128)(2,1)S(1)}, u32[]{:S(2)}, u32[]{:S(2)}) collective-permute-start(bf16[2,128,128]{2,1,0:T(8,128)(2,1)S(1)} %slice_bitcast_fusion), channel_id=1, source_target_pairs={{56,256},{57,257},{120,320},{121,321},{58,258},{59,259},{122,322},... | collective-permute-start | bytes 196616 | tf_op jit(solution)/shard_map/ppermute | solution.py:30
  250.1 1.6 copy-start.3
  (2 other events, 2.1 us)
Sparse Core Ops, SparseCore 0:
  42.0 38.6 all-gather.7
  82.8 41.3 all-gather.9
  126.3 50.8 all-gather.5

commit v4 on v2

v4 whole, which is shorter than its diff:
```python
import functools
import jax
import jax.numpy as jnp
from jax import lax
from jax.experimental import pallas as pl
from jax.experimental.pallas import tpu as pltpu
from jax.sharding import Mesh, PartitionSpec as P

AXES = ("xhi", "xlo", "zlo", "y", "zhi", "core")
SIZES = (2, 2, 2, 8, 4, 2)
SEQ = ("xhi", "xlo", "zlo", "y")
TENSOR = ("zhi", "core")
NZ, NY = 8, 8
adapter_scale = 0.5


def flat(x, y, z, c):
    return (((x % 4) * 2 + (z % NZ) % 2) * NY + y % NY) * 8 + ((z % NZ) // 2) * 2 + c


def permute(value, move, keep=lambda x, y, z, c: True):
    pairs = [
        (flat(x, y, z, c), flat(*move(x, y, z, c)))
        for x in range(4)
        for y in range(NY)
        for z in range(NZ)
        for c in range(2)
        if keep(x, y, z, c)
    ]
    return lax.ppermute(value, AXES, pairs)


def y_step(value, step):
    return permute(value, lambda x, y, z, c: (x, y + step, z, c))


def core_swap(value):
    return permute(value, lambda x, y, z, c: (x, y, z, 1 - c))


def x_pair_swap(value):
    return permute(value, lambda x, y, z, c: (x ^ 1, y, z, c))


def nt_dot(a, b):
    return lax.dot_general(a, b, (((1,), (1,)), ((), ())), preferred_element_type=jnp.float32)


def position():
    x_hi, x_lo, z_lo, y, z_hi, core = (lax.axis_index(name) for name in AXES)
    return x_hi, x_lo, z_lo, y, z_hi, core


def fetch(sources, targets, sems):
    copies = [pltpu.make_async_copy(a, b, sems.at[i]) for i, (a, b) in enumerate(zip(sources, targets))]
    for copy in copies:
        copy.start()
    for copy in copies:
        copy.wait()


def stacked_weight(weight, side, columns):
    blocks = [weight[:, side, z_hi, :, columns] for z_hi in range(weight.shape[2])]
    return jnp.concatenate([b.reshape(-1, b.shape[-1]) for b in blocks], axis=0)


def project_kernel(tokens_ref, *refs):
    pieces, refs = refs[:NY], refs[NY:]
    up, up_other, kv_own, kv_send, q_own, q_send, tokens, weight, sems = refs
    copies = [pltpu.make_async_copy(tokens_ref.at[z], tokens.at[z], sems.at[z]) for z in range(NZ)]
    for z_lo in range(2):
        for z in range(z_lo, NZ, 2):
            copies[z].start()
    y = position()[3]
    for dist in range(NY):
        weight[lax.rem(y + dist, NY)] = pieces[dist][...]
    half = kv_own.shape[1]
    ch = up.shape[1] // 3
    ranks = up.shape[0]
    row = lax.broadcasted_iota(jnp.int32, (half, ranks), 0)
    column = lax.broadcasted_iota(jnp.int32, (half, ranks), 1)
    mine = (row >= half // 2) == (column >= ranks // 2)
    kv_columns, q_columns = slice(ch, 3 * ch), slice(0, ch)
    kv_weight = [stacked_weight(weight, side, kv_columns) for side in range(2)]
    q_weight = jnp.concatenate([stacked_weight(weight, side, q_columns) for side in range(2)], axis=1)
    q_up = jnp.concatenate([up[:, q_columns], up_other[:, q_columns]], axis=1)
    for z_lo in range(2):
        for z in range(z_lo, NZ, 2):
            copies[z].wait()
        down = jnp.concatenate([tokens[z, 2 * half :, :] for z in range(z_lo, NZ, 2)], axis=1)
        for x_lo in range(2):
            quarter = x_lo * 2 + z_lo
            rows = [tokens[z, half * x_lo : half * (x_lo + 1), :] for z in range(z_lo, NZ, 2)]
            a = jnp.concatenate(rows, axis=1)
            low = jnp.where(mine, adapter_scale * nt_dot(a, down), 0.0).astype(jnp.bfloat16)
            for side in range(2):
                part = jnp.dot(a, kv_weight[side], preferred_element_type=jnp.float32)
                ups = (up if side == 0 else up_other)[:, kv_columns]
                part += jnp.dot(low, ups, preferred_element_type=jnp.float32)
                if side == 0:
                    kv_own[quarter] = part
                else:
                    kv_send[quarter] = part.astype(kv_send.dtype)
            part = jnp.dot(a, q_weight, preferred_element_type=jnp.float32)
            part += jnp.dot(low, q_up, preferred_element_type=jnp.float32)
            q_own[quarter] = part[:, :ch]
            q_send[quarter] = part[:, ch:].astype(q_send.dtype)


def combine_kernel(own_ref, met_ref, kv_ref):
    rows, ch = kv_ref.shape[2], kv_ref.shape[3]
    for quarter in range(4):
        both = own_ref[quarter] + met_ref[quarter].astype(jnp.float32)
        kv = (both[:, :ch] * both[:, ch:]).astype(jnp.bfloat16)
        for seg in range(2):
            kv_ref[quarter, seg] = kv[rows * seg : rows * (seg + 1), :]


def prepare_kernel(tasks, down_ref, up_ref, down_out, up_out, sems):
    _, x_lo, z_lo, _, _, _ = position()
    ranks = down_ref.shape[1]
    ch = up_out.shape[1] // 3
    columns = pl.ds(pl.multiple_of((x_lo * 2 + z_lo) * ch, ch), ch)
    pairs = []
    for seg in range(2):
        at = pl.ds(seg * ranks, ranks)
        pairs.append((down_ref.at[tasks[seg]], down_out.at[at]))
        for stream in range(3):
            pairs.append((up_ref.at[tasks[seg], stream, :, columns], up_out.at[at, pl.ds(stream * ch, ch)]))
    fetch(*zip(*pairs), sems)


def join_kernel(own_ref, other_ref, down_ref, out_ref):
    x_lo = position()[1]
    half = own_ref.shape[0]
    out_ref[pl.ds(pl.multiple_of(x_lo * half, half), half), :] = own_ref[...]
    out_ref[pl.ds(pl.multiple_of((1 - x_lo) * half, half), half), :] = other_ref[...]
    out_ref[2 * half :, :] = down_ref[...]


def split_kernel(met_ref, kept_ref, given_ref):
    core = position()[5]
    for block in range(kept_ref.shape[0]):
        kept_ref[block] = met_ref[2 * block + core]
        given_ref[block] = met_ref[2 * block + 1 - core]


def spread_kernel(weight_ref, out_ref):
    ch = out_ref.shape[2] // 3
    for quarter in range(4):
        for stream in range(3):
            block = weight_ref[stream, :, quarter * ch : (quarter + 1) * ch]
            for copy in range(2):
                out_ref[copy * 4 + quarter, :, stream * ch : (stream + 1) * ch] = block


def spread_taps(taps_ref, tap, ch):
    return jnp.broadcast_to(taps_ref[tap : tap + 1, :], (8, ch))


def fill_taps(filters_ref, taps):
    _, x_lo, z_lo, _, _, _ = position()
    ch = taps.shape[1]
    mine = filters_ref[pl.ds(pl.multiple_of((x_lo * 2 + z_lo) * ch, ch), ch), :]
    taps[...] = mine.astype(jnp.float32).T


def conv_own_kernel(kv_ref, filters_ref, part_ref, ext, taps):
    rows, ch = kv_ref.shape[2], kv_ref.shape[3]
    groups = rows // 8
    fill_taps(filters_ref, taps)

    def block(n, carry):
        quarter, seg = n // 2, lax.rem(n, 2)
        ext[0:8, :] = jnp.zeros((8, ch), jnp.float32)
        ext[8:, :] = kv_ref[quarter, seg].astype(jnp.float32)
        total = [jnp.zeros((8, ch), jnp.float32) for _ in range(groups)]
        for r in range(8):
            shifted = [ext[8 * g + 8 - r : 8 * g + 16 - r, :] for g in range(groups)]
            for s in range(groups):
                tap = spread_taps(taps, 8 * s + r, ch)
                for g in range(s, groups):
                    total[g] = total[g] + tap * shifted[g - s]
        for g in range(groups):
            part_ref[quarter, seg, 8 * g : 8 * g + 8, :] = total[g]
        return carry

    lax.fori_loop(0, 8, block, 0)


def gate_kernel(lengths, part_ref, own_ref, met_ref, prev_ref, wrap_ref, filters_ref, out_ref, ext, sums, taps, edges):
    x_hi, _, _, y, _, _ = position()
    rows, ch = part_ref.shape[2], part_ref.shape[3]
    groups = rows // 8
    count = out_ref.shape[1]
    each = lengths.shape[1] // 8
    fill_taps(filters_ref, taps)
    for seg in range(2):
        start = jnp.int32(0)
        for window in range(lengths.shape[1]):
            at = (window // each) * 2 * each + seg * each + window % each
            end = start + lengths[seg, window]
            edges[0, at : at + 1, :] = jnp.full((1, rows), start, jnp.int32)
            edges[1, at : at + 1, :] = jnp.full((1, rows), end, jnp.int32)
            start = end
    sums[...] = jnp.zeros((count, ch), jnp.float32)
    row = lax.broadcasted_iota(jnp.int32, (count, rows), 0)
    column = lax.broadcasted_iota(jnp.int32, (count, rows), 1)
    row_seg = lax.rem(row // each, 2)

    def block(n, carry):
        quarter, seg = n // 2, lax.rem(n, 2)
        at = jnp.where(y > 0, quarter, jnp.maximum(quarter - 1, 0))
        before = prev_ref[at, seg].astype(jnp.float32)
        wrapped = wrap_ref[seg].astype(jnp.float32)
        ext[0:8, :] = jnp.zeros((8, ch), jnp.float32)
        ext[8 : 8 + rows, :] = jnp.where((y == 0) & (quarter == 0), wrapped, before)
        ext[8 + rows :, :] = jnp.zeros((8, ch), jnp.float32)
        total = [part_ref[quarter, seg, 8 * g : 8 * g + 8, :] for g in range(groups)]
        for r in range(8):
            shifted = [ext[8 * g + 8 - r : 8 * g + 16 - r, :] for g in range(groups + (1 if r else 0))]
            for s in range(groups):
                tap = spread_taps(taps, 8 * s + r, ch)
                for g in range(groups):
                    if groups + g - s < len(shifted):
                        total[g] = total[g] + tap * shifted[groups + g - s]
        at_rows = pl.ds(pl.multiple_of(seg * rows, rows), rows)
        q = own_ref[quarter, at_rows, :] + met_ref[quarter, at_rows, :].astype(jnp.float32)
        gated = (q * jnp.concatenate(total, axis=0)).astype(jnp.bfloat16)
        place = ((x_hi * 4 + quarter) * NY + y) * rows + column
        inside = (place >= edges[0]) & (place < edges[1]) & (row_seg == seg)
        member = inside.astype(jnp.float32).astype(jnp.bfloat16)
        sums[...] += jnp.dot(member, gated, preferred_element_type=jnp.float32)
        return carry

    lax.fori_loop(0, 8, block, 0)
    for copy in range(out_ref.shape[0]):
        out_ref[copy] = sums[...].astype(out_ref.dtype)


def sum_kernel(met_ref, out_ref):
    total = met_ref[0].astype(jnp.float32)
    for i in range(1, met_ref.shape[0]):
        total = total + met_ref[i].astype(jnp.float32)
    for copy in range(out_ref.shape[0]):
        out_ref[copy] = total.astype(out_ref.dtype)


def embed_kernel(lengths, met_ref, weight_ref, out_ref):
    _, _, _, _, z_hi, core = position()
    rows, ch = met_ref.shape[3], met_ref.shape[4]
    each = rows // 2
    row = lax.broadcasted_iota(jnp.int32, (rows, ch), 0)
    length = jnp.zeros((rows, ch), jnp.int32)
    for r in range(rows):
        length = jnp.where(row == r, lengths[r // each, (z_hi * 2 + core) * each + r % each], length)
    length = length.astype(jnp.float32)
    columns = weight_ref.shape[0] // met_ref.shape[2]
    total = jnp.zeros((rows, columns), jnp.float32)
    for t in range(met_ref.shape[2]):
        means = []
        for quarter in range(met_ref.shape[1]):
            both = met_ref[0, quarter, t].astype(jnp.float32) + met_ref[1, quarter, t].astype(jnp.float32)
            means.append((both / length).astype(jnp.bfloat16))
        weight = weight_ref[t * columns : (t + 1) * columns, :].astype(jnp.bfloat16)
        total += nt_dot(jnp.concatenate(means, axis=1), weight)
    out_ref[...] = total.astype(out_ref.dtype)


VMEM = pl.BlockSpec(memory_space=pltpu.VMEM)
SMEM = pl.BlockSpec(memory_space=pltpu.SMEM)


ANY = pl.BlockSpec(memory_space=pltpu.HBM)


def call(kernel, name, out, operands, scratch=(), vmem=24, scalars=False, where=0):
    return pl.pallas_call(
        kernel,
        out_shape=out,
        in_specs=[SMEM] * scalars + [ANY] * where + [VMEM] * (len(operands) - scalars - where),
        out_specs=jax.tree.map(lambda _: VMEM, out),
        scratch_shapes=list(scratch),
        compiler_params=pltpu.CompilerParams(vmem_limit_bytes=vmem << 20),
        name=name,
    )(*operands)


def local(tokens, in_weight, down_factors, up_factors, filters, task_ids, window_lengths, out_weight):
    f32, bf16 = jnp.float32, jnp.bfloat16
    segs, rows, depth = tokens.shape
    w_rows, _, channels = in_weight.shape
    ch = channels // 4
    windows = window_lengths.shape[1]
    ranks = segs * down_factors.shape[2]
    half = segs * rows
    count = segs * windows

    down, up = call(
        prepare_kernel,
        "adapters",
        (jax.ShapeDtypeStruct((ranks, depth), bf16), jax.ShapeDtypeStruct((ranks, 3 * ch), bf16)),
        (task_ids, down_factors.transpose(0, 2, 1), up_factors.transpose(0, 2, 1, 3)),
        [pltpu.SemaphoreType.DMA((8,))],
        scalars=True,
        where=2,
    )
    own = tokens.reshape(half, depth)
    other = x_pair_swap(own)
    piece = call(
        join_kernel, "join_rows", jax.ShapeDtypeStruct((2 * half + ranks, depth), bf16), (own, other, down)
    )
    gathered = lax.all_gather(piece, ("zhi", "zlo"), axis=0, tiled=False)

    spread = call(
        spread_kernel,
        "spread_weight",
        jax.ShapeDtypeStruct((8, w_rows, 3 * ch), bf16),
        (in_weight.transpose(1, 0, 2),),
    )
    spread, piece = lax.optimization_barrier((spread, piece))
    met = lax.all_to_all(spread, ("xhi", "xlo", "zlo"), 0, 0, tiled=True)
    split = jax.ShapeDtypeStruct((4, w_rows, 3 * ch), bf16)
    kept, given = call(split_kernel, "split_rows", (split, split), (met,))
    weight = {0: jnp.stack([kept, core_swap(given)])}
    for step in range(1, NY // 2):
        weight[NY - step] = y_step(weight[(NY - step + 1) % NY], 1)
        weight[step] = y_step(weight[step - 1], -1)
    weight[NY // 2] = y_step(weight[NY // 2 + 1], 1)
    up_other = core_swap(up)

    cut = (4, half)
    kv_own, kv_send, q_own, q_send = call(
        project_kernel,
        "project",
        (
            jax.ShapeDtypeStruct((*cut, 2 * ch), f32),
            jax.ShapeDtypeStruct((*cut, 2 * ch), bf16),
            jax.ShapeDtypeStruct((*cut, ch), f32),
            jax.ShapeDtypeStruct((*cut, ch), bf16),
        ),
        (gathered, *[weight[d] for d in range(NY)], up, up_other),
        [
            pltpu.VMEM(gathered.shape, bf16),
            pltpu.VMEM((NY, *weight[0].shape), bf16),
            pltpu.SemaphoreType.DMA((NZ,)),
        ],
        vmem=48,
        where=1,
    )
    kv = call(
        combine_kernel,
        "combine_kv",
        jax.ShapeDtypeStruct((4, segs, rows, ch), bf16),
        (kv_own, core_swap(kv_send)),
    )
    prev = permute(kv, lambda x, y, z, c: (x, y + 1, z, c))
    wrap = permute(kv[3], lambda x, y, z, c: (x + 2, 0, z, c), lambda x, y, z, c: x < 2 and y == NY - 1)
    q_met = core_swap(q_send)
    part = call(
        conv_own_kernel,
        "conv_own",
        jax.ShapeDtypeStruct((4, segs, rows, ch), f32),
        (kv, filters),
        [pltpu.VMEM((8 + rows, ch), f32), pltpu.VMEM((filters.shape[1], ch), f32)],
    )
    total = call(
        gate_kernel,
        "gate_pool",
        jax.ShapeDtypeStruct((NY, count, ch), bf16),
        (window_lengths, part, q_own, q_met, prev, wrap, filters),
        [
            pltpu.VMEM((16 + rows, ch), f32),
            pltpu.VMEM((count, ch), f32),
            pltpu.VMEM((filters.shape[1], ch), f32),
            pltpu.VMEM((2, count, rows), jnp.int32),
        ],
        scalars=True,
    )

    met = lax.all_to_all(total, "y", 0, 0, tiled=True)
    total = call(sum_kernel, "sum_y", jax.ShapeDtypeStruct((8, count, ch), bf16), (met,))
    rest = ("xhi", "xlo", "zlo", "zhi", "core")
    met = lax.all_to_all(total.reshape(64, 8, ch), rest, 0, 0, tiled=True)
    met = met.reshape(2, 4, 8, 8, ch)
    wide, kv_send = lax.optimization_barrier((out_weight.T.astype(f32), kv_send))
    whole = lax.all_gather(wide, TENSOR, axis=0, tiled=True)
    out = call(
        embed_kernel,
        "embed",
        jax.ShapeDtypeStruct((8, out_weight.shape[1]), bf16),
        (window_lengths, met, whole),
        scalars=True,
    )
    return out.reshape(segs, windows // 8, out_weight.shape[1])


def solution(mesh):
    fine = Mesh(mesh.devices.reshape(SIZES), AXES)
    in_specs = (
        P(None, SEQ, TENSOR),
        P(SEQ, None, TENSOR),
        P(None, TENSOR, None),
        P(None, None, None, TENSOR),
        P(TENSOR, None),
        P(),
        P(),
        P(TENSOR, SEQ),
    )
    return jax.shard_map(local, mesh=fine, in_specs=in_specs, out_specs=P(None, TENSOR, SEQ), check_vma=False)
```

time: 225 us -> 173 us (0.77)
  local copies, waits for them, and re-layouts: 57.6 us -> 14.1 us
  starting transfers between devices: 83.3 us -> 44.7 us
  blocking collectives: 16 us -> 52.3 us
  between operations: 19.2 us -> 13.7 us
    all_to_all x0 -> x2, blocking collectives: none -> 39.2 us  [the longest x1 24.4 us: local(): met = lax.all_to_all(total.reshape(64, 8, ch), rest, 0, 0, tiled=True)]
    unnamed x132 -> x38, local copies, waits for them, and re-layouts: 51 us -> 14.1 us
    ppermute x21 -> x14, starting transfers between devices: 67.3 us -> 44.6 us  [permute(): return lax.ppermute(value, AXES, pairs)]
    ppermute x21 -> x14, waiting for transfers between devices: 7.03 us -> 28.9 us  [permute(): return lax.ppermute(value, AXES, pairs)]
    all_to_all x2 -> x0, waiting for transfers between devices: 20.1 us -> none  [the longest x1 13.3 us: local(): met = lax.all_to_all(total.reshape(64, 8, ch), rest, 0, 0, tiled=True)]
    all_to_all x2 -> x0, starting transfers between devices: 15.9 us -> none  [the longest x1 9.26 us: local(): met = lax.all_to_all(total.reshape(64, 8, ch), rest, 0, 0, tiled=True)]
    all_to_all x1, blocking collectives: 16 us -> 13 us  [local(): met = lax.all_to_all(total, 'y', 0, 0, tiled=True)]
    pallas_call x7 -> x10, Pallas kernels: 17.3 us -> 17.9 us  [call(): pl.pallas_call(kernel, out_shape=out, in_specs=[SMEM] * scalars + [ANY] *...]
  transfers between devices with their start and end apart: 25 -> 16, of which waited for: 6 -> 8; matrix products, arithmetic and copies ran while one was open for 3% -> 0% of each run, Pallas kernels for 5% -> 4%
where the time goes in v4:
time: 173 us; the launch traced here: 172 us
  blocking collectives  52.3 us (30%)
  starting transfers between devices  44.7 us (26%)
  waiting for transfers between devices  28.9 us (17%)
  Pallas kernels  17.9 us (10%)
  local copies, waits for them, and re-layouts  14.1 us (8%)
  between operations  13.7 us (8%)
    ppermute x14, starting transfers between devices, permute(): return lax.ppermute(value, AXES, pairs)  44.6 us
    ppermute x14, waiting for transfers between devices, permute(): return lax.ppermute(value, AXES, pairs)  28.9 us
    all_to_all x1, blocking collectives, local(): met = lax.all_to_all(total.reshape(64, 8, ch), rest, 0, 0, tiled=True)  24.4 us
    pallas_call x10, Pallas kernels, call(): pl.pallas_call(kernel, out_shape=out, in_specs=[SMEM] * scalars + [ANY] *...  17.9 us
    all_to_all x1, blocking collectives, local(): met = lax.all_to_all(spread, ('xhi', 'xlo', 'zlo'), 0, 0, tiled=True)  14.9 us
    unnamed x38, local copies, waits for them, and re-layouts  14.1 us
    all_to_all x1, blocking collectives, local(): met = lax.all_to_all(total, 'y', 0, 0, tiled=True)  13 us
  transfers between devices with their start and end apart: 16, of which 8 were waited for; matrix products, arithmetic and copies ran while one was open for 0% of the time, Pallas kernels for 4%

profile of v4, /device:TPU:1, one launch (start us, length us, event | category | flops | bytes accessed | tf_op | source)
XLA Modules:
  0.0 172.3 jit_solution(18348287967136890705)
XLA Ops:
  6.5 3.9 %collective-permute-start = (bf16[256,512]{1,0:T(8,128)(2,1)}, bf16[256,512]{1,0:T(8,128)(2,1)S(1)}, u32[]{:S(2)}, u32[]{:S(2)}) collective-permute-start(bf16[256,512]{1,0:T(8,128)(2,1)} %bitcast.17), channel_id=1, source_target_pairs={{0,128},{1,129},{64,192},{65,193},{2,130},{3,131},{66,194},{67,195... | collective-permute-start | bytes 786440 | tf_op jit(solution)/shard_map/ppermute | solution.py:30
  10.5 1.0 copy-done.2
  17.3 14.9 %all_to_all.15.met_ref = bf16[8,64,384]{2,1,0:T(8,128)(2,1)S(1)} all-to-all(bf16[8,64,384]{2,1,0:T(8,128)(2,1)S(1)} %spread_weight.1), channel_id=1, replica_groups=mesh['xhi'=2,'xlo'=2,'zlo'=2,'y'=8,'zhi'=4,'core'=2] {'xhi','xlo','zlo'}, dimensions={0} | all-to-all | bytes 786432 | tf_op jit(solution)/shard_map/all_to_all | solution.py:322
  32.2 5.0 %collective-permute-start.1 = (bf16[4,64,384]{2,1,0:T(8,128)(2,1)S(1)}, bf16[4,64,384]{2,1,0:T(8,128)(2,1)S(1)}, u32[]{:S(2)}, u32[]{:S(2)}) collective-permute-start(bf16[4,64,384]{2,1,0:T(8,128)(2,1)S(1)} %get-tuple-element.18), channel_id=1, source_target_pairs={{0,1},{1,0},{64,65},{65,64},{2,3},{3,2},{66,67},{67,66},{4,5},{5,4... | collective-permute-start | bytes 589832 | tf_op jit(solution)/shard_map/ppermute | solution.py:30
  37.2 1.0 collective-permute-done.1
  38.3 3.0 %collective-permute-start.5 = (bf16[2,4,64,384]{3,2,1,0:T(8,128)(2,1)S(1)}, bf16[2,4,64,384]{3,2,1,0:T(8,128)(2,1)S(1)}, u32[]{:S(2)}, u32[]{:S(2)}) collective-permute-start(bf16[2,4,64,384]{3,2,1,0:T(8,128)(2,1)S(1)} %pad_maximum_fusion.refs_0_), channel_id=1, source_target_pairs={{0,8},{1,9},{64,72},{65,73},{2,10},{3,11},{66,74},{67,75},{4,12},{... | collective-permute-start | bytes 1179656 | tf_op jit(solution)/shard_map/ppermute | solution.py:30
  41.3 3.8 %collective-permute-start.2 = (bf16[2,4,64,384]{3,2,1,0:T(8,128)(2,1)S(1)}, bf16[2,4,64,384]{3,2,1,0:T(8,128)(2,1)S(1)}, u32[]{:S(2)}, u32[]{:S(2)}) collective-permute-start(bf16[2,4,64,384]{3,2,1,0:T(8,128)(2,1)S(1)} %pad_maximum_fusion.refs_0_), channel_id=1, source_target_pairs={{0,56},{1,57},{64,120},{65,121},{2,58},{3,59},{66,122},{67,123},{4... | collective-permute-start | bytes 1179656 | tf_op jit(solution)/shard_map/ppermute | solution.py:30
  45.1 7.3 %collective-permute-done.5.refs_7_ = bf16[2,4,64,384]{3,2,1,0:T(8,128)(2,1)S(1)} collective-permute-done((bf16[2,4,64,384]{3,2,1,0:T(8,128)(2,1)S(1)}, bf16[2,4,64,384]{3,2,1,0:T(8,128)(2,1)S(1)}, u32[]{:S(2)}, u32[]{:S(2)}) %collective-permute-start.5) | collective-permute-done | bytes 393248 | tf_op jit(solution)/shard_map/ppermute | solution.py:30
  52.5 1.9 %collective-permute-start.6 = (bf16[2,4,64,384]{3,2,1,0:T(8,128)(2,1)S(1)}, bf16[2,4,64,384]{3,2,1,0:T(8,128)(2,1)S(1)}, u32[]{:S(2)}, u32[]{:S(2)}) collective-permute-start(bf16[2,4,64,384]{3,2,1,0:T(8,128)(2,1)S(1)} %collective-permute-done.5.refs_7_), channel_id=1, source_target_pairs={{0,8},{1,9},{64,72},{65,73},{2,10},{3,11},{66,74},{67,75},{4,12},{... | collective-permute-start | bytes 1179656 | tf_op jit(solution)/shard_map/ppermute | solution.py:30
  54.4 4.6 %collective-permute-start.3 = (bf16[2,4,64,384]{3,2,1,0:T(8,128)(2,1)S(1)}, bf16[2,4,64,384]{3,2,1,0:T(8,128)(2,1)S(1)}, u32[]{:S(2)}, u32[]{:S(2)}) collective-permute-start(bf16[2,4,64,384]{3,2,1,0:T(8,128)(2,1)S(1)} %collective-permute-done.2.refs_1_), channel_id=1, source_target_pairs={{0,56},{1,57},{64,120},{65,121},{2,58},{3,59},{66,122},{67,123},{4... | collective-permute-start | bytes 1179656 | tf_op jit(solution)/shard_map/ppermute | solution.py:30
  59.0 6.6 %collective-permute-done.6.refs_6_ = bf16[2,4,64,384]{3,2,1,0:T(8,128)(2,1)S(1)} collective-permute-done((bf16[2,4,64,384]{3,2,1,0:T(8,128)(2,1)S(1)}, bf16[2,4,64,384]{3,2,1,0:T(8,128)(2,1)S(1)}, u32[]{:S(2)}, u32[]{:S(2)}) %collective-permute-start.6) | collective-permute-done | bytes 393248 | tf_op jit(solution)/shard_map/ppermute | solution.py:30
  65.6 1.9 %collective-permute-start.7 = (bf16[2,4,64,384]{3,2,1,0:T(8,128)(2,1)S(1)}, bf16[2,4,64,384]{3,2,1,0:T(8,128)(2,1)S(1)}, u32[]{:S(2)}, u32[]{:S(2)}) collective-permute-start(bf16[2,4,64,384]{3,2,1,0:T(8,128)(2,1)S(1)} %collective-permute-done.6.refs_6_), channel_id=1, source_target_pairs={{0,8},{1,9},{64,72},{65,73},{2,10},{3,11},{66,74},{67,75},{4,12},{... | collective-permute-start | bytes 1179656 | tf_op jit(solution)/shard_map/ppermute | solution.py:30
  67.5 4.6 %collective-permute-start.4 = (bf16[2,4,64,384]{3,2,1,0:T(8,128)(2,1)S(1)}, bf16[2,4,64,384]{3,2,1,0:T(8,128)(2,1)S(1)}, u32[]{:S(2)}, u32[]{:S(2)}) collective-permute-start(bf16[2,4,64,384]{3,2,1,0:T(8,128)(2,1)S(1)} %collective-permute-done.3.refs_2_), channel_id=1, source_target_pairs={{0,56},{1,57},{64,120},{65,121},{2,58},{3,59},{66,122},{67,123},{4... | collective-permute-start | bytes 1179656 | tf_op jit(solution)/shard_map/ppermute | solution.py:30
  72.8 5.0 %collective-permute-done.7.refs_5_ = bf16[2,4,64,384]{3,2,1,0:T(8,128)(2,1)S(1)} collective-permute-done((bf16[2,4,64,384]{3,2,1,0:T(8,128)(2,1)S(1)}, bf16[2,4,64,384]{3,2,1,0:T(8,128)(2,1)S(1)}, u32[]{:S(2)}, u32[]{:S(2)}) %collective-permute-start.7) | collective-permute-done | bytes 393248 | tf_op jit(solution)/shard_map/ppermute | solution.py:30
  77.8 1.9 %collective-permute-start.8 = (bf16[2,4,64,384]{3,2,1,0:T(8,128)(2,1)S(1)}, bf16[2,4,64,384]{3,2,1,0:T(8,128)(2,1)S(1)}, u32[]{:S(2)}, u32[]{:S(2)}) collective-permute-start(bf16[2,4,64,384]{3,2,1,0:T(8,128)(2,1)S(1)} %collective-permute-done.7.refs_5_), channel_id=1, source_target_pairs={{0,8},{1,9},{64,72},{65,73},{2,10},{3,11},{66,74},{67,75},{4,12},{... | collective-permute-start | bytes 1179656 | tf_op jit(solution)/shard_map/ppermute | solution.py:30
  80.5 4.3 %collective-permute-start.9 = (bf16[32,384]{1,0:T(8,128)(2,1)S(1)}, bf16[32,384]{1,0:T(8,128)(2,1)S(1)}, u32[]{:S(2)}, u32[]{:S(2)}) collective-permute-start(bf16[32,384]{1,0:T(8,128)(2,1)S(1)} %get-tuple-element.19.refs_8_), channel_id=1, source_target_pairs={{0,1},{1,0},{64,65},{65,64},{2,3},{3,2},{66,67},{67,66},{4,5},{5,4... | collective-permute-start | bytes 73736 | tf_op jit(solution)/shard_map/ppermute | solution.py:30
  86.3 2.8 %collective-permute-done.8.refs_4_ = bf16[2,4,64,384]{3,2,1,0:T(8,128)(2,1)S(1)} collective-permute-done((bf16[2,4,64,384]{3,2,1,0:T(8,128)(2,1)S(1)}, bf16[2,4,64,384]{3,2,1,0:T(8,128)(2,1)S(1)}, u32[]{:S(2)}, u32[]{:S(2)}) %collective-permute-start.8) | collective-permute-done | bytes 393248 | tf_op jit(solution)/shard_map/ppermute | solution.py:30
  89.9 1.0 copy-done.4
  90.9 1.0 copy-done.6
  91.9 1.0 copy-done.8
  92.9 1.0 copy-done.10
  93.9 8.1 %project.1 = (f32[4,256,256]{2,1,0:T(8,128)S(1)}, bf16[4,256,256]{2,1,0:T(8,128)(2,1)S(1)}, f32[4,256,128]{2,1,0:T(8,128)S(1)}, bf16[4,256,128]{2,1,0:T(8,128)(2,1)S(1)}) custom-call(bf16[8,544,512]{2,1,0:T(8,128)(2,1)} %bitcast.22, bf16[2,4,64,384]{3,2,1,0:T(8,128)(2,1)S(1)} %pad_maximum_fusion.refs_0_, ...), custom_call_target="tpu_custom_call" | custom-call | tf_op jit(solution)/shard_map/project/pallas_call | solution.py:278
  103.5 5.2 %collective-permute-start.10 = (bf16[4,256,256]{2,1,0:T(8,128)(2,1)}, bf16[4,256,256]{2,1,0:T(8,128)(2,1)S(1)}, u32[]{:S(2)}, u32[]{:S(2)}) collective-permute-start(bf16[4,256,256]{2,1,0:T(8,128)(2,1)} %copy-done.16), channel_id=1, source_target_pairs={{0,1},{1,0},{64,65},{65,64},{2,3},{3,2},{66,67},{67,66},{4,5},{5,4... | collective-permute-start | bytes 1572872 | tf_op jit(solution)/shard_map/ppermute | solution.py:30
  108.7 1.9 %collective-permute-start.11 = (bf16[4,256,128]{2,1,0:T(8,128)(2,1)}, bf16[4,256,128]{2,1,0:T(8,128)(2,1)S(1)}, u32[]{:S(2)}, u32[]{:S(2)}) collective-permute-start(bf16[4,256,128]{2,1,0:T(8,128)(2,1)} %copy-done.17), channel_id=1, source_target_pairs={{0,1},{1,0},{64,65},{65,64},{2,3},{3,2},{66,67},{67,66},{4,5},{5,4... | collective-permute-start | bytes 786440 | tf_op jit(solution)/shard_map/ppermute | solution.py:30
  110.8 1.9 %collective-permute-start.12 = (bf16[4,2,128,128]{3,2,1,0:T(8,128)(2,1)S(1)}, bf16[4,2,128,128]{3,2,1,0:T(8,128)(2,1)S(1)}, u32[]{:S(2)}, u32[]{:S(2)}) collective-permute-start(bf16[4,2,128,128]{3,2,1,0:T(8,128)(2,1)S(1)} %combine_kv.1.kv_ref), channel_id=1, source_target_pairs={{0,8},{1,9},{64,72},{65,73},{2,10},{3,11},{66,74},{67,75},{4,12},{... | collective-permute-start | bytes 786440 | tf_op jit(solution)/shard_map/ppermute | solution.py:30
  113.4 2.5 %conv_own.1.part_ref = f32[4,2,128,128]{3,2,1,0:T(8,128)S(1)} custom-call(bf16[4,2,128,128]{3,2,1,0:T(8,128)(2,1)S(1)} %combine_kv.1.kv_ref, bf16[512,128]{1,0:T(8,128)(2,1)S(1)} %copy-done.1), custom_call_target="tpu_custom_call" | custom-call | tf_op jit(solution)/shard_map/conv_own/pallas_call | solution.py:278
  115.9 5.3 %collective-permute-done.12.prev_ref = bf16[4,2,128,128]{3,2,1,0:T(8,128)(2,1)S(1)} collective-permute-done((bf16[4,2,128,128]{3,2,1,0:T(8,128)(2,1)S(1)}, bf16[4,2,128,128]{3,2,1,0:T(8,128)(2,1)S(1)}, u32[]{:S(2)}, u32[]{:S(2)}) %collective-permute-start.12) | collective-permute-done | bytes 262176 | tf_op jit(solution)/shard_map/ppermute | solution.py:30
  121.2 4.2 %gate_pool.1 = bf16[8,64,128]{2,1,0:T(8,128)(2,1)S(1)} custom-call(s32[2,32]{1,0:T(2,128)S(1)} %copy-done.14, f32[4,2,128,128]{3,2,1,0:T(8,128)S(1)} %conv_own.1.part_ref, f32[4,256,128]{2,1,0:T(8,128)S(1)} %get-tuple-element.22.own_ref, bf16[4,256,128]{2,1,0:T(8,128)(2,1)S(1)} %collective-permute-done.11.met_ref, ...), custom_call_target="tpu_custom_call" | custom-call | tf_op jit(solution)/shard_map/gate_pool/pallas_call | solution.py:278
  125.4 13.0 %all_to_all.16.met_ref = bf16[8,64,128]{2,1,0:T(8,128)(2,1)S(1)} all-to-all(bf16[8,64,128]{2,1,0:T(8,128)(2,1)S(1)} %gate_pool.1), channel_id=1, replica_groups=mesh['xhi'=2,'xlo'=2,'zlo'=2,'y'=8,'zhi'=4,'core'=2] {'y'}, dimensions={0} | all-to-all | bytes 262144 | tf_op jit(solution)/shard_map/all_to_all | solution.py:381
  138.4 24.4 %all_to_all.17 = bf16[64,8,128]{2,1,0:T(8,128)(2,1)S(1)} all-to-all(bf16[64,8,128]{2,1,0:T(8,128)(2,1)S(1)} %bitcast.14), channel_id=1, replica_groups=mesh['xhi'=2,'xlo'=2,'zlo'=2,'y'=8,'zhi'=4,'core'=2] {'xhi','xlo','zlo',..., dimensions={0} | all-to-all | bytes 262144 | tf_op jit(solution)/shard_map/all_to_all | solution.py:384
  162.8 1.2 copy-done
  164.0 1.4 embed.1
  (56 shorter events, 12.0 us)
Async XLA Ops:
  6.5 83.3 %all-gather.6.cloned.1.call-start = ((), (), s32[]{:S(2)}) async-start(), calls=%async_computation.4 | async-start | bytes 5013504 | tf_op jit(solution)/shard_map/all_gather | solution.py:313
  6.5 7.9 %collective-permute-start = (bf16[256,512]{1,0:T(8,128)(2,1)}, bf16[256,512]{1,0:T(8,128)(2,1)S(1)}, u32[]{:S(2)}, u32[]{:S(2)}) collective-permute-start(bf16[256,512]{1,0:T(8,128)(2,1)} %bitcast.17), channel_id=1, source_target_pairs={{0,128},{1,129},{64,192},{65,193},{2,130},{3,131},{66,194},{67,195... | collective-permute-start | bytes 786440 | tf_op jit(solution)/shard_map/ppermute | solution.py:30
  10.5 1.0 copy-start.2
  11.5 0.9 copy-start.13
  13.0 71.7 %copy-start.18 = (bf16[512,64]{0,1:T(8,128)(2,1)S(1)}, bf16[512,64]{0,1:T(8,128)(2,1)}, u32[]{:S(2)}) copy-start(bf16[512,64]{0,1:T(8,128)(2,1)} %param.15) | copy-start | bytes 196612
  14.4 1.0 copy-start.11
  16.3 146.5 %all-gather.4.cloned.1.call-start = ((), (), s32[]{:S(2)}) async-start(), calls=%async_computation.3 | async-start | bytes 1179648 | tf_op jit(solution)/shard_map/all_gather | solution.py:387
  16.3 0.9 copy-start.12
  32.2 6.0 %collective-permute-start.1 = (bf16[4,64,384]{2,1,0:T(8,128)(2,1)S(1)}, bf16[4,64,384]{2,1,0:T(8,128)(2,1)S(1)}, u32[]{:S(2)}, u32[]{:S(2)}) collective-permute-start(bf16[4,64,384]{2,1,0:T(8,128)(2,1)S(1)} %get-tuple-element.18), channel_id=1, source_target_pairs={{0,1},{1,0},{64,65},{65,64},{2,3},{3,2},{66,67},{67,66},{4,5},{5,4... | collective-permute-start | bytes 589832 | tf_op jit(solution)/shard_map/ppermute | solution.py:30
  38.3 14.2 %collective-permute-start.5 = (bf16[2,4,64,384]{3,2,1,0:T(8,128)(2,1)S(1)}, bf16[2,4,64,384]{3,2,1,0:T(8,128)(2,1)S(1)}, u32[]{:S(2)}, u32[]{:S(2)}) collective-permute-start(bf16[2,4,64,384]{3,2,1,0:T(8,128)(2,1)S(1)} %pad_maximum_fusion.refs_0_), channel_id=1, source_target_pairs={{0,8},{1,9},{64,72},{65,73},{2,10},{3,11},{66,74},{67,75},{4,12},{... | collective-permute-start | bytes 1179656 | tf_op jit(solution)/shard_map/ppermute | solution.py:30
  41.3 13.1 %collective-permute-start.2 = (bf16[2,4,64,384]{3,2,1,0:T(8,128)(2,1)S(1)}, bf16[2,4,64,384]{3,2,1,0:T(8,128)(2,1)S(1)}, u32[]{:S(2)}, u32[]{:S(2)}) collective-permute-start(bf16[2,4,64,384]{3,2,1,0:T(8,128)(2,1)S(1)} %pad_maximum_fusion.refs_0_), channel_id=1, source_target_pairs={{0,56},{1,57},{64,120},{65,121},{2,58},{3,59},{66,122},{67,123},{4... | collective-permute-start | bytes 1179656 | tf_op jit(solution)/shard_map/ppermute | solution.py:30
  52.5 13.1 %collective-permute-start.6 = (bf16[2,4,64,384]{3,2,1,0:T(8,128)(2,1)S(1)}, bf16[2,4,64,384]{3,2,1,0:T(8,128)(2,1)S(1)}, u32[]{:S(2)}, u32[]{:S(2)}) collective-permute-start(bf16[2,4,64,384]{3,2,1,0:T(8,128)(2,1)S(1)} %collective-permute-done.5.refs_7_), channel_id=1, source_target_pairs={{0,8},{1,9},{64,72},{65,73},{2,10},{3,11},{66,74},{67,75},{4,12},{... | collective-permute-start | bytes 1179656 | tf_op jit(solution)/shard_map/ppermute | solution.py:30
  54.4 13.1 %collective-permute-start.3 = (bf16[2,4,64,384]{3,2,1,0:T(8,128)(2,1)S(1)}, bf16[2,4,64,384]{3,2,1,0:T(8,128)(2,1)S(1)}, u32[]{:S(2)}, u32[]{:S(2)}) collective-permute-start(bf16[2,4,64,384]{3,2,1,0:T(8,128)(2,1)S(1)} %collective-permute-done.2.refs_1_), channel_id=1, source_target_pairs={{0,56},{1,57},{64,120},{65,121},{2,58},{3,59},{66,122},{67,123},{4... | collective-permute-start | bytes 1179656 | tf_op jit(solution)/shard_map/ppermute | solution.py:30
  65.6 12.2 %collective-permute-start.7 = (bf16[2,4,64,384]{3,2,1,0:T(8,128)(2,1)S(1)}, bf16[2,4,64,384]{3,2,1,0:T(8,128)(2,1)S(1)}, u32[]{:S(2)}, u32[]{:S(2)}) collective-permute-start(bf16[2,4,64,384]{3,2,1,0:T(8,128)(2,1)S(1)} %collective-permute-done.6.refs_6_), channel_id=1, source_target_pairs={{0,8},{1,9},{64,72},{65,73},{2,10},{3,11},{66,74},{67,75},{4,12},{... | collective-permute-start | bytes 1179656 | tf_op jit(solution)/shard_map/ppermute | solution.py:30
  67.5 18.1 %collective-permute-start.4 = (bf16[2,4,64,384]{3,2,1,0:T(8,128)(2,1)S(1)}, bf16[2,4,64,384]{3,2,1,0:T(8,128)(2,1)S(1)}, u32[]{:S(2)}, u32[]{:S(2)}) collective-permute-start(bf16[2,4,64,384]{3,2,1,0:T(8,128)(2,1)S(1)} %collective-permute-done.3.refs_2_), channel_id=1, source_target_pairs={{0,56},{1,57},{64,120},{65,121},{2,58},{3,59},{66,122},{67,123},{4... | collective-permute-start | bytes 1179656 | tf_op jit(solution)/shard_map/ppermute | solution.py:30
  72.1 0.8 copy-start.3
  77.8 11.3 %collective-permute-start.8 = (bf16[2,4,64,384]{3,2,1,0:T(8,128)(2,1)S(1)}, bf16[2,4,64,384]{3,2,1,0:T(8,128)(2,1)S(1)}, u32[]{:S(2)}, u32[]{:S(2)}) collective-permute-start(bf16[2,4,64,384]{3,2,1,0:T(8,128)(2,1)S(1)} %collective-permute-done.7.refs_5_), channel_id=1, source_target_pairs={{0,8},{1,9},{64,72},{65,73},{2,10},{3,11},{66,74},{67,75},{4,12},{... | collective-permute-start | bytes 1179656 | tf_op jit(solution)/shard_map/ppermute | solution.py:30
  80.5 5.1 %collective-permute-start.9 = (bf16[32,384]{1,0:T(8,128)(2,1)S(1)}, bf16[32,384]{1,0:T(8,128)(2,1)S(1)}, u32[]{:S(2)}, u32[]{:S(2)}) collective-permute-start(bf16[32,384]{1,0:T(8,128)(2,1)S(1)} %get-tuple-element.19.refs_8_), channel_id=1, source_target_pairs={{0,1},{1,0},{64,65},{65,64},{2,3},{3,2},{66,67},{67,66},{4,5},{5,4... | collective-permute-start | bytes 73736 | tf_op jit(solution)/shard_map/ppermute | solution.py:30
  85.6 0.8 copy-start.7
  89.1 0.8 copy-start.9
  89.9 1.0 copy-start.4
  90.9 1.0 copy-start.6
  91.9 1.0 copy-start.8
  92.9 1.0 copy-start.10
  93.9 19.5 %copy-start.1 = (bf16[512,128]{1,0:T(8,128)(2,1)S(1)}, bf16[512,128]{1,0:T(8,128)(2,1)}, u32[]{:S(2)}) copy-start(bf16[512,128]{1,0:T(8,128)(2,1)} %filters_ref.3) | copy-start | bytes 393220
  93.9 27.4 %copy-start.14 = (s32[2,32]{1,0:T(2,128)S(1)}, s32[2,32]{1,0:T(2,128)}, u32[]{:S(2)}) copy-start(s32[2,32]{1,0:T(2,128)} %lengths.3) | copy-start | bytes 772
  102.0 0.8 copy-start.16
  103.5 7.2 %collective-permute-start.10 = (bf16[4,256,256]{2,1,0:T(8,128)(2,1)}, bf16[4,256,256]{2,1,0:T(8,128)(2,1)S(1)}, u32[]{:S(2)}, u32[]{:S(2)}) collective-permute-start(bf16[4,256,256]{2,1,0:T(8,128)(2,1)} %copy-done.16), channel_id=1, source_target_pairs={{0,1},{1,0},{64,65},{65,64},{2,3},{3,2},{66,67},{67,66},{4,5},{5,4... | collective-permute-start | bytes 1572872 | tf_op jit(solution)/shard_map/ppermute | solution.py:30
  108.7 7.2 %collective-permute-start.11 = (bf16[4,256,128]{2,1,0:T(8,128)(2,1)}, bf16[4,256,128]{2,1,0:T(8,128)(2,1)S(1)}, u32[]{:S(2)}, u32[]{:S(2)}) collective-permute-start(bf16[4,256,128]{2,1,0:T(8,128)(2,1)} %copy-done.17), channel_id=1, source_target_pairs={{0,1},{1,0},{64,65},{65,64},{2,3},{3,2},{66,67},{67,66},{4,5},{5,4... | collective-permute-start | bytes 786440 | tf_op jit(solution)/shard_map/ppermute | solution.py:30
  110.8 10.5 %collective-permute-start.12 = (bf16[4,2,128,128]{3,2,1,0:T(8,128)(2,1)S(1)}, bf16[4,2,128,128]{3,2,1,0:T(8,128)(2,1)S(1)}, u32[]{:S(2)}, u32[]{:S(2)}) collective-permute-start(bf16[4,2,128,128]{3,2,1,0:T(8,128)(2,1)S(1)} %combine_kv.1.kv_ref), channel_id=1, source_target_pairs={{0,8},{1,9},{64,72},{65,73},{2,10},{3,11},{66,74},{67,75},{4,12},{... | collective-permute-start | bytes 786440 | tf_op jit(solution)/shard_map/ppermute | solution.py:30
  112.7 3.2 %collective-permute-start.13 = (bf16[2,128,128]{2,1,0:T(8,128)(2,1)S(1)}, bf16[2,128,128]{2,1,0:T(8,128)(2,1)S(1)}, u32[]{:S(2)}, u32[]{:S(2)}) collective-permute-start(bf16[2,128,128]{2,1,0:T(8,128)(2,1)S(1)} %slice_bitcast_fusion), channel_id=1, source_target_pairs={{56,256},{57,257},{120,320},{121,321},{58,258},{59,259},{122,322},... | collective-permute-start | bytes 196616 | tf_op jit(solution)/shard_map/ppermute | solution.py:30
  162.8 1.2 copy-start
  (3 other events, 2.1 us)
Sparse Core Ops, SparseCore 0:
  16.4 68.4 all-gather.5
  103.6 36.7 all-gather.3

commit v5 on v4

--- a/solution.py
+++ b/solution.py
@@ -59,52 +59,62 @@
         copy.wait()
 
 
-def stacked_weight(weight, side, columns):
-    blocks = [weight[:, side, z_hi, :, columns] for z_hi in range(weight.shape[2])]
-    return jnp.concatenate([b.reshape(-1, b.shape[-1]) for b in blocks], axis=0)
-
-
-def project_kernel(tokens_ref, *refs):
-    pieces, refs = refs[:NY], refs[NY:]
-    up, up_other, kv_own, kv_send, q_own, q_send, tokens, weight, sems = refs
-    copies = [pltpu.make_async_copy(tokens_ref.at[z], tokens.at[z], sems.at[z]) for z in range(NZ)]
-    for z_lo in range(2):
-        for z in range(z_lo, NZ, 2):
-            copies[z].start()
-    y = position()[3]
-    for dist in range(NY):
-        weight[lax.rem(y + dist, NY)] = pieces[dist][...]
+def rows_of(tokens, quarter, half):
+    x_lo, z_lo = quarter // 2, quarter % 2
+    return jnp.concatenate([tokens[z, half * x_lo : half * (x_lo + 1), :] for z in range(z_lo, NZ, 2)], axis=1)
+
+
+def place_rows(target, piece, y):
+    _, blocks, w_rows, columns = piece.shape
+    ch = columns // 3
+    for block in range(blocks):
+        at = pl.ds(pl.multiple_of((block * NY + y) * w_rows, w_rows), w_rows)
+        for side in range(2):
+            target[side, at, :] = piece[side, block, :, ch:]
+            target[2, at, side * ch : (side + 1) * ch] = piece[side, block, :, :ch]
+
+
+def pack_kernel(*refs):
+    count = NY - 1
+    out_ref, held, sems = refs[count:]
+    copies = [pltpu.make_async_copy(refs[i], held.at[i], sems.at[i]) for i in range(count)]
+    for copy in copies:
+        copy.start()
+    for i, dist in enumerate(d for d in range(NY) if d != NY // 2):
+        copies[i].wait()
+        place_rows(out_ref, held.at[i], lax.rem(position()[3] + dist, NY))
+
+
+def project_kernel(tokens, packed, last, up, up_other, kv_own, kv_send, q_own, q_send, weight):
+    weight[...] = packed[...]
+    place_rows(weight, last, lax.rem(position()[3] + NY // 2, NY))
     half = kv_own.shape[1]
     ch = up.shape[1] // 3
     ranks = up.shape[0]
     row = lax.broadcasted_iota(jnp.int32, (half, ranks), 0)
     column = lax.broadcasted_iota(jnp.int32, (half, ranks), 1)
     mine = (row >= half // 2) == (column >= ranks // 2)
-    kv_columns, q_columns = slice(ch, 3 * ch), slice(0, ch)
-    kv_weight = [stacked_weight(weight, side, kv_columns) for side in range(2)]
-    q_weight = jnp.concatenate([stacked_weight(weight, side, q_columns) for side in range(2)], axis=1)
-    q_up = jnp.concatenate([up[:, q_columns], up_other[:, q_columns]], axis=1)
-    for z_lo in range(2):
-        for z in range(z_lo, NZ, 2):
-            copies[z].wait()
+    q_up = jnp.concatenate([up[:, :ch], up_other[:, :ch]], axis=1)
+    lows = {}
+    for quarter in (0, 2, 1, 3):
+        z_lo = quarter % 2
         down = jnp.concatenate([tokens[z, 2 * half :, :] for z in range(z_lo, NZ, 2)], axis=1)
-        for x_lo in range(2):
-            quarter = x_lo * 2 + z_lo
-            rows = [tokens[z, half * x_lo : half * (x_lo + 1), :] for z in range(z_lo, NZ, 2)]
-            a = jnp.concatenate(rows, axis=1)
-            low = jnp.where(mine, adapter_scale * nt_dot(a, down), 0.0).astype(jnp.bfloat16)
-            for side in range(2):
-                part = jnp.dot(a, kv_weight[side], preferred_element_type=jnp.float32)
-                ups = (up if side == 0 else up_other)[:, kv_columns]
-                part += jnp.dot(low, ups, preferred_element_type=jnp.float32)
-                if side == 0:
-                    kv_own[quarter] = part
-                else:
-                    kv_send[quarter] = part.astype(kv_send.dtype)
-            part = jnp.dot(a, q_weight, preferred_element_type=jnp.float32)
-            part += jnp.dot(low, q_up, preferred_element_type=jnp.float32)
-            q_own[quarter] = part[:, :ch]
-            q_send[quarter] = part[:, ch:].astype(q_send.dtype)
+        a = rows_of(tokens, quarter, half)
+        low = jnp.where(mine, adapter_scale * nt_dot(a, down), 0.0).astype(jnp.bfloat16)
+        lows[quarter] = low
+        for side in range(2):
+            part = jnp.dot(a, weight[side], preferred_element_type=jnp.float32)
+            ups = (up if side == 0 else up_other)[:, ch:]
+            part += jnp.dot(low, ups, preferred_element_type=jnp.float32)
+            if side == 0:
+                kv_own[quarter] = part
+            else:
+                kv_send[quarter] = part.astype(kv_send.dtype)
+    for quarter in range(4):
+        part = jnp.dot(rows_of(tokens, quarter, half), weight[2], preferred_element_type=jnp.float32)
+        part += jnp.dot(lows[quarter], q_up, preferred_element_type=jnp.float32)
+        q_own[quarter] = part[:, :ch]
+        q_send[quarter] = part[:, ch:].astype(q_send.dtype)
 
 
 def combine_kernel(own_ref, met_ref, kv_ref):
@@ -242,8 +252,11 @@
     total = met_ref[0].astype(jnp.float32)
     for i in range(1, met_ref.shape[0]):
         total = total + met_ref[i].astype(jnp.float32)
-    for copy in range(out_ref.shape[0]):
-        out_ref[copy] = total.astype(out_ref.dtype)
+    rows = out_ref.shape[2]
+    for place in range(out_ref.shape[0]):
+        mine = total[place * rows : (place + 1) * rows, :].astype(out_ref.dtype)
+        for copy in range(out_ref.shape[1]):
+            out_ref[place, copy] = mine
 
 
 def embed_kernel(lengths, met_ref, weight_ref, out_ref):
@@ -255,12 +268,12 @@
     for r in range(rows):
         length = jnp.where(row == r, lengths[r // each, (z_hi * 2 + core) * each + r % each], length)
     length = length.astype(jnp.float32)
-    columns = weight_ref.shape[0] // met_ref.shape[2]
+    columns = weight_ref.shape[0] // met_ref.shape[0]
     total = jnp.zeros((rows, columns), jnp.float32)
-    for t in range(met_ref.shape[2]):
+    for t in range(met_ref.shape[0]):
         means = []
-        for quarter in range(met_ref.shape[1]):
-            both = met_ref[0, quarter, t].astype(jnp.float32) + met_ref[1, quarter, t].astype(jnp.float32)
+        for quarter in range(met_ref.shape[2]):
+            both = met_ref[t, 0, quarter].astype(jnp.float32) + met_ref[t, 1, quarter].astype(jnp.float32)
             means.append((both / length).astype(jnp.bfloat16))
         weight = weight_ref[t * columns : (t + 1) * columns, :].astype(jnp.bfloat16)
         total += nt_dot(jnp.concatenate(means, axis=1), weight)
@@ -330,6 +343,18 @@
     up_other = core_swap(up)
 
     cut = (4, half)
+    features = w_rows * NY * 4
+    early = [weight[d] for d in range(NY) if d != NY // 2]
+    gathered, *early = lax.optimization_barrier((gathered, *early))
+    packed = call(
+        pack_kernel,
+        "pack_weights",
+        jax.ShapeDtypeStruct((3, features, 2 * ch), bf16),
+        tuple(early),
+        [pltpu.VMEM((NY - 1, *weight[0].shape), bf16), pltpu.SemaphoreType.DMA((NY - 1,))],
+        vmem=56,
+        where=NY - 1,
+    )
     kv_own, kv_send, q_own, q_send = call(
         project_kernel,
         "project",
@@ -339,14 +364,8 @@
             jax.ShapeDtypeStruct((*cut, ch), f32),
             jax.ShapeDtypeStruct((*cut, ch), bf16),
         ),
-        (gathered, *[weight[d] for d in range(NY)], up, up_other),
-        [
-            pltpu.VMEM(gathered.shape, bf16),
-            pltpu.VMEM((NY, *weight[0].shape), bf16),
-            pltpu.SemaphoreType.DMA((NZ,)),
-        ],
-        vmem=48,
-        where=1,
+        (gathered, packed, weight[NY // 2], up, up_other),
+        [pltpu.VMEM(packed.shape, bf16)],
     )
     kv = call(
         combine_kernel,
@@ -354,6 +373,8 @@
         jax.ShapeDtypeStruct((4, segs, rows, ch), bf16),
         (kv_own, core_swap(kv_send)),
     )
+    wide, kv = lax.optimization_barrier((out_weight.T.astype(f32), kv))
+    whole = lax.all_gather(wide, TENSOR, axis=0, tiled=True)
     prev = permute(kv, lambda x, y, z, c: (x, y + 1, z, c))
     wrap = permute(kv[3], lambda x, y, z, c: (x + 2, 0, z, c), lambda x, y, z, c: x < 2 and y == NY - 1)
     q_met = core_swap(q_send)
@@ -379,12 +400,10 @@
     )
 
     met = lax.all_to_all(total, "y", 0, 0, tiled=True)
-    total = call(sum_kernel, "sum_y", jax.ShapeDtypeStruct((8, count, ch), bf16), (met,))
-    rest = ("xhi", "xlo", "zlo", "zhi", "core")
+    total = call(sum_kernel, "sum_y", jax.ShapeDtypeStruct((8, 8, 8, ch), bf16), (met,))
+    rest = TENSOR + ("xhi", "xlo", "zlo")
     met = lax.all_to_all(total.reshape(64, 8, ch), rest, 0, 0, tiled=True)
-    met = met.reshape(2, 4, 8, 8, ch)
-    wide, kv_send = lax.optimization_barrier((out_weight.T.astype(f32), kv_send))
-    whole = lax.all_gather(wide, TENSOR, axis=0, tiled=True)
+    met = met.reshape(8, 2, 4, 8, ch)
     out = call(
         embed_kernel,
         "embed",

time: 173 us -> 168 us (0.971)
  local copies, waits for them, and re-layouts: 14.1 us -> 7.59 us
  Pallas kernels: 17.9 us -> 19.7 us
    unnamed x38 -> x34, local copies, waits for them, and re-layouts: 14.1 us -> 7.58 us
    pallas_call x10 -> x11, Pallas kernels: 17.9 us -> 19.7 us  [call(): pl.pallas_call(kernel, out_shape=out, in_specs=[SMEM] * scalars + [ANY] *...]
  transfers between devices with their start and end apart: 16 -> 16, of which waited for: 8 -> 9; matrix products, arithmetic and copies ran while one was open for 0% -> 0% of each run, Pallas kernels for 4% -> 7%
where the time goes in v5:
time: 168 us; the launch traced here: 167 us
  blocking collectives  50.6 us (30%)
  starting transfers between devices  45 us (27%)
  waiting for transfers between devices  29.4 us (18%)
  Pallas kernels  19.7 us (12%)
  between operations  13.7 us (8%)
  local copies, waits for them, and re-layouts  7.59 us (5%)
    ppermute x14, starting transfers between devices, permute(): return lax.ppermute(value, AXES, pairs)  45 us
    ppermute x14, waiting for transfers between devices, permute(): return lax.ppermute(value, AXES, pairs)  28.5 us
    all_to_all x1, blocking collectives, local(): met = lax.all_to_all(total.reshape(64, 8, ch), rest, 0, 0, tiled=True)  22.8 us
    pallas_call x11, Pallas kernels, call(): pl.pallas_call(kernel, out_shape=out, in_specs=[SMEM] * scalars + [ANY] *...  19.7 us
    all_to_all x1, blocking collectives, local(): met = lax.all_to_all(spread, ('xhi', 'xlo', 'zlo'), 0, 0, tiled=True)  14.9 us
    all_to_all x1, blocking collectives, local(): met = lax.all_to_all(total, 'y', 0, 0, tiled=True)  13 us
    unnamed x34, local copies, waits for them, and re-layouts  7.58 us
  transfers between devices with their start and end apart: 16, of which 9 were waited for; matrix products, arithmetic and copies ran while one was open for 0% of the time, Pallas kernels for 7%

profile of v5, /device:TPU:1, one launch (start us, length us, event | category | flops | bytes accessed | tf_op | source)
XLA Modules:
  0.0 166.8 jit_solution(7324553314676085389)
XLA Ops:
  6.5 3.9 %collective-permute-start = (bf16[256,512]{1,0:T(8,128)(2,1)}, bf16[256,512]{1,0:T(8,128)(2,1)S(1)}, u32[]{:S(2)}, u32[]{:S(2)}) collective-permute-start(bf16[256,512]{1,0:T(8,128)(2,1)} %bitcast.18), channel_id=1, source_target_pairs={{0,128},{1,129},{64,192},{65,193},{2,130},{3,131},{66,194},{67,195... | collective-permute-start | bytes 786440 | tf_op jit(solution)/shard_map/ppermute | solution.py:30
  10.5 1.0 copy-done.4
  11.5 0.9 copy-done.7
  14.4 0.9 copy-done.5
  16.3 0.9 copy-done.6
  17.3 14.9 %all_to_all.15.met_ref = bf16[8,64,384]{2,1,0:T(8,128)(2,1)S(1)} all-to-all(bf16[8,64,384]{2,1,0:T(8,128)(2,1)S(1)} %spread_weight.1), channel_id=1, replica_groups=mesh['xhi'=2,'xlo'=2,'zlo'=2,'y'=8,'zhi'=4,'core'=2] {'xhi','xlo','zlo'}, dimensions={0} | all-to-all | bytes 786432 | tf_op jit(solution)/shard_map/all_to_all | solution.py:335
  32.2 5.0 %collective-permute-start.1 = (bf16[4,64,384]{2,1,0:T(8,128)(2,1)S(1)}, bf16[4,64,384]{2,1,0:T(8,128)(2,1)S(1)}, u32[]{:S(2)}, u32[]{:S(2)}) collective-permute-start(bf16[4,64,384]{2,1,0:T(8,128)(2,1)S(1)} %get-tuple-element.27), channel_id=1, source_target_pairs={{0,1},{1,0},{64,65},{65,64},{2,3},{3,2},{66,67},{67,66},{4,5},{5,4... | collective-permute-start | bytes 589832 | tf_op jit(solution)/shard_map/ppermute | solution.py:30
  37.2 1.0 collective-permute-done.1
  38.3 3.0 %collective-permute-start.5 = (bf16[2,4,64,384]{3,2,1,0:T(8,128)(2,1)S(1)}, bf16[2,4,64,384]{3,2,1,0:T(8,128)(2,1)S(1)}, u32[]{:S(2)}, u32[]{:S(2)}) collective-permute-start(bf16[2,4,64,384]{3,2,1,0:T(8,128)(2,1)S(1)} %pad_maximum_fusion.refs_0_), channel_id=1, source_target_pairs={{0,8},{1,9},{64,72},{65,73},{2,10},{3,11},{66,74},{67,75},{4,12},{... | collective-permute-start | bytes 1179656 | tf_op jit(solution)/shard_map/ppermute | solution.py:30
  41.3 3.8 %collective-permute-start.2 = (bf16[2,4,64,384]{3,2,1,0:T(8,128)(2,1)S(1)}, bf16[2,4,64,384]{3,2,1,0:T(8,128)(2,1)S(1)}, u32[]{:S(2)}, u32[]{:S(2)}) collective-permute-start(bf16[2,4,64,384]{3,2,1,0:T(8,128)(2,1)S(1)} %pad_maximum_fusion.refs_0_), channel_id=1, source_target_pairs={{0,56},{1,57},{64,120},{65,121},{2,58},{3,59},{66,122},{67,123},{4... | collective-permute-start | bytes 1179656 | tf_op jit(solution)/shard_map/ppermute | solution.py:30
  45.2 7.3 %collective-permute-done.5.refs_6_ = bf16[2,4,64,384]{3,2,1,0:T(8,128)(2,1)S(1)} collective-permute-done((bf16[2,4,64,384]{3,2,1,0:T(8,128)(2,1)S(1)}, bf16[2,4,64,384]{3,2,1,0:T(8,128)(2,1)S(1)}, u32[]{:S(2)}, u32[]{:S(2)}) %collective-permute-start.5) | collective-permute-done | bytes 393248 | tf_op jit(solution)/shard_map/ppermute | solution.py:30
  52.5 1.9 %collective-permute-start.6 = (bf16[2,4,64,384]{3,2,1,0:T(8,128)(2,1)S(1)}, bf16[2,4,64,384]{3,2,1,0:T(8,128)(2,1)S(1)}, u32[]{:S(2)}, u32[]{:S(2)}) collective-permute-start(bf16[2,4,64,384]{3,2,1,0:T(8,128)(2,1)S(1)} %collective-permute-done.5.refs_6_), channel_id=1, source_target_pairs={{0,8},{1,9},{64,72},{65,73},{2,10},{3,11},{66,74},{67,75},{4,12},{... | collective-permute-start | bytes 1179656 | tf_op jit(solution)/shard_map/ppermute | solution.py:30
  54.4 4.6 %collective-permute-start.3 = (bf16[2,4,64,384]{3,2,1,0:T(8,128)(2,1)S(1)}, bf16[2,4,64,384]{3,2,1,0:T(8,128)(2,1)S(1)}, u32[]{:S(2)}, u32[]{:S(2)}) collective-permute-start(bf16[2,4,64,384]{3,2,1,0:T(8,128)(2,1)S(1)} %collective-permute-done.2.refs_1_), channel_id=1, source_target_pairs={{0,56},{1,57},{64,120},{65,121},{2,58},{3,59},{66,122},{67,123},{4... | collective-permute-start | bytes 1179656 | tf_op jit(solution)/shard_map/ppermute | solution.py:30
  59.0 6.5 %collective-permute-done.6.refs_5_ = bf16[2,4,64,384]{3,2,1,0:T(8,128)(2,1)S(1)} collective-permute-done((bf16[2,4,64,384]{3,2,1,0:T(8,128)(2,1)S(1)}, bf16[2,4,64,384]{3,2,1,0:T(8,128)(2,1)S(1)}, u32[]{:S(2)}, u32[]{:S(2)}) %collective-permute-start.6) | collective-permute-done | bytes 393248 | tf_op jit(solution)/shard_map/ppermute | solution.py:30
  65.6 1.9 %collective-permute-start.7 = (bf16[2,4,64,384]{3,2,1,0:T(8,128)(2,1)S(1)}, bf16[2,4,64,384]{3,2,1,0:T(8,128)(2,1)S(1)}, u32[]{:S(2)}, u32[]{:S(2)}) collective-permute-start(bf16[2,4,64,384]{3,2,1,0:T(8,128)(2,1)S(1)} %collective-permute-done.6.refs_5_), channel_id=1, source_target_pairs={{0,8},{1,9},{64,72},{65,73},{2,10},{3,11},{66,74},{67,75},{4,12},{... | collective-permute-start | bytes 1179656 | tf_op jit(solution)/shard_map/ppermute | solution.py:30
  67.5 4.6 %collective-permute-start.4 = (bf16[2,4,64,384]{3,2,1,0:T(8,128)(2,1)S(1)}, bf16[2,4,64,384]{3,2,1,0:T(8,128)(2,1)}, u32[]{:S(2)}, u32[]{:S(2)}) collective-permute-start(bf16[2,4,64,384]{3,2,1,0:T(8,128)(2,1)S(1)} %collective-permute-done.3.refs_2_), channel_id=1, source_target_pairs={{0,56},{1,57},{64,120},{65,121},{2,58},{3,59},{66,122},{67,123},{4... | collective-permute-start | bytes 1179656 | tf_op jit(solution)/shard_map/ppermute | solution.py:30
  72.1 5.7 %collective-permute-done.7.refs_4_ = bf16[2,4,64,384]{3,2,1,0:T(8,128)(2,1)S(1)} collective-permute-done((bf16[2,4,64,384]{3,2,1,0:T(8,128)(2,1)S(1)}, bf16[2,4,64,384]{3,2,1,0:T(8,128)(2,1)S(1)}, u32[]{:S(2)}, u32[]{:S(2)}) %collective-permute-start.7) | collective-permute-done | bytes 393248 | tf_op jit(solution)/shard_map/ppermute | solution.py:30
  77.8 1.9 %collective-permute-start.8 = (bf16[2,4,64,384]{3,2,1,0:T(8,128)(2,1)S(1)}, bf16[2,4,64,384]{3,2,1,0:T(8,128)(2,1)S(1)}, u32[]{:S(2)}, u32[]{:S(2)}) collective-permute-start(bf16[2,4,64,384]{3,2,1,0:T(8,128)(2,1)S(1)} %collective-permute-done.7.refs_4_), channel_id=1, source_target_pairs={{0,8},{1,9},{64,72},{65,73},{2,10},{3,11},{66,74},{67,75},{4,12},{... | collective-permute-start | bytes 1179656 | tf_op jit(solution)/shard_map/ppermute | solution.py:30
  79.7 4.3 %collective-permute-start.9 = (bf16[32,384]{1,0:T(8,128)(2,1)S(1)}, bf16[32,384]{1,0:T(8,128)(2,1)S(1)}, u32[]{:S(2)}, u32[]{:S(2)}) collective-permute-start(bf16[32,384]{1,0:T(8,128)(2,1)S(1)} %get-tuple-element.36.up), channel_id=1, source_target_pairs={{0,1},{1,0},{64,65},{65,64},{2,3},{3,2},{66,67},{67,66},{4,5},{5,4... | collective-permute-start | bytes 73736 | tf_op jit(solution)/shard_map/ppermute | solution.py:30
  85.0 3.6 %pack_weights.1.packed = bf16[3,2048,256]{2,1,0:T(8,128)(2,1)} custom-call(bf16[2,4,64,384]{3,2,1,0:T(8,128)(2,1)} %copy-done.10, bf16[2,4,64,384]{3,2,1,0:T(8,128)(2,1)} %copy-done.12, bf16[2,4,64,384]{3,2,1,0:T(8,128)(2,1)} %copy-done.14, bf16[2,4,64,384]{3,2,1,0:T(8,128)(2,1)} %collective-permute-done.4.refs_3_, bf16[2,4,64,384]{3,2,1,0:T(8,128)(2,1)} %copy-done.15, ...), custom_call_target="tpu_custom_call" | custom-call | tf_op jit(solution)/shard_map/pack_weights/pallas_call | solution.py:291
  89.1 1.9 %copy-done = bf16[3,2048,256]{2,1,0:T(8,128)(2,1)S(1)} copy-done((bf16[3,2048,256]{2,1,0:T(8,128)(2,1)S(1)}, bf16[3,2048,256]{2,1,0:T(8,128)(2,1)}, u32[]{:S(2)}) %copy-start) | copy-done | bytes 3145752
  91.0 6.3 %project.1 = (f32[4,256,256]{2,1,0:T(8,128)S(1)}, bf16[4,256,256]{2,1,0:T(8,128)(2,1)S(1)}, f32[4,256,128]{2,1,0:T(8,128)S(1)}, bf16[4,256,128]{2,1,0:T(8,128)(2,1)S(1)}) custom-call(bf16[8,544,512]{2,1,0:T(8,128)(2,1)S(1)} %bitcast.14, bf16[3,2048,256]{2,1,0:T(8,128)(2,1)S(1)} %copy-done, bf16[2,4,64,384]{3,2,1,0:T(8,128)(2,1)S(1)} %collective-permute-done.8.last, ...), custom_call_target="tpu_custom_call" | custom-call | tf_op jit(solution)/shard_map/project/pallas_call | solution.py:291
  97.4 5.2 %collective-permute-start.10 = (bf16[4,256,256]{2,1,0:T(8,128)(2,1)S(1)}, bf16[4,256,256]{2,1,0:T(8,128)(2,1)S(1)}, u32[]{:S(2)}, u32[]{:S(2)}) collective-permute-start(bf16[4,256,256]{2,1,0:T(8,128)(2,1)S(1)} %get-tuple-element.38), channel_id=1, source_target_pairs={{0,1},{1,0},{64,65},{65,64},{2,3},{3,2},{66,67},{67,66},{4,5},{5,4... | collective-permute-start | bytes 1572872 | tf_op jit(solution)/shard_map/ppermute | solution.py:30
  104.2 2.3 %collective-permute-start.11 = (bf16[4,256,128]{2,1,0:T(8,128)(2,1)S(1)}, bf16[4,256,128]{2,1,0:T(8,128)(2,1)S(1)}, u32[]{:S(2)}, u32[]{:S(2)}) collective-permute-start(bf16[4,256,128]{2,1,0:T(8,128)(2,1)S(1)} %get-tuple-element.41), channel_id=1, source_target_pairs={{0,1},{1,0},{64,65},{65,64},{2,3},{3,2},{66,67},{67,66},{4,5},{5,4... | collective-permute-start | bytes 786440 | tf_op jit(solution)/shard_map/ppermute | solution.py:30
  106.5 1.9 %collective-permute-start.12 = (bf16[4,2,128,128]{3,2,1,0:T(8,128)(2,1)S(1)}, bf16[4,2,128,128]{3,2,1,0:T(8,128)(2,1)S(1)}, u32[]{:S(2)}, u32[]{:S(2)}) collective-permute-start(bf16[4,2,128,128]{3,2,1,0:T(8,128)(2,1)S(1)} %combine_kv.1.kv_ref), channel_id=1, source_target_pairs={{0,8},{1,9},{64,72},{65,73},{2,10},{3,11},{66,74},{67,75},{4,12},{... | collective-permute-start | bytes 786440 | tf_op jit(solution)/shard_map/ppermute | solution.py:30
  109.2 2.5 %conv_own.1.part_ref = f32[4,2,128,128]{3,2,1,0:T(8,128)S(1)} custom-call(bf16[4,2,128,128]{3,2,1,0:T(8,128)(2,1)S(1)} %combine_kv.1.kv_ref, bf16[512,128]{1,0:T(8,128)(2,1)S(1)} %copy-done.3), custom_call_target="tpu_custom_call" | custom-call | tf_op jit(solution)/shard_map/conv_own/pallas_call | solution.py:291
  111.7 5.7 %collective-permute-done.12.prev_ref = bf16[4,2,128,128]{3,2,1,0:T(8,128)(2,1)S(1)} collective-permute-done((bf16[4,2,128,128]{3,2,1,0:T(8,128)(2,1)S(1)}, bf16[4,2,128,128]{3,2,1,0:T(8,128)(2,1)S(1)}, u32[]{:S(2)}, u32[]{:S(2)}) %collective-permute-start.12) | collective-permute-done | bytes 262176 | tf_op jit(solution)/shard_map/ppermute | solution.py:30
  117.4 4.2 %gate_pool.1 = bf16[8,64,128]{2,1,0:T(8,128)(2,1)S(1)} custom-call(s32[2,32]{1,0:T(2,128)S(1)} %copy-done.8, f32[4,2,128,128]{3,2,1,0:T(8,128)S(1)} %conv_own.1.part_ref, f32[4,256,128]{2,1,0:T(8,128)S(1)} %get-tuple-element.40.own_ref, bf16[4,256,128]{2,1,0:T(8,128)(2,1)S(1)} %collective-permute-done.11.met_ref, ...), custom_call_target="tpu_custom_call" | custom-call | tf_op jit(solution)/shard_map/gate_pool/pallas_call | solution.py:291
  121.6 13.0 %all_to_all.16.met_ref = bf16[8,64,128]{2,1,0:T(8,128)(2,1)S(1)} all-to-all(bf16[8,64,128]{2,1,0:T(8,128)(2,1)S(1)} %gate_pool.1), channel_id=1, replica_groups=mesh['xhi'=2,'xlo'=2,'zlo'=2,'y'=8,'zhi'=4,'core'=2] {'y'}, dimensions={0} | all-to-all | bytes 262144 | tf_op jit(solution)/shard_map/all_to_all | solution.py:402
  134.6 22.8 %all_to_all.17 = bf16[64,8,128]{2,1,0:T(8,128)(2,1)S(1)} all-to-all(bf16[64,8,128]{2,1,0:T(8,128)(2,1)S(1)} %bitcast.15), channel_id=1, replica_groups=mesh['xhi'=2,'xlo'=2,'zlo'=2,'y'=8,'zhi'=4,'core'=2] {'zhi','core','xhi'..., dimensions={0} | all-to-all | bytes 262144 | tf_op jit(solution)/shard_map/all_to_all | solution.py:405
  157.4 1.2 copy-done.2
  158.6 1.4 embed.1
  (53 shorter events, 6.9 us)
Async XLA Ops:
  6.5 78.3 %all-gather.6.cloned.1.call-start = ((), (), s32[]{:S(2)}) async-start(), calls=%async_computation.4 | async-start | bytes 5013504 | tf_op jit(solution)/shard_map/all_gather | solution.py:326
  6.5 7.9 %collective-permute-start = (bf16[256,512]{1,0:T(8,128)(2,1)}, bf16[256,512]{1,0:T(8,128)(2,1)S(1)}, u32[]{:S(2)}, u32[]{:S(2)}) collective-permute-start(bf16[256,512]{1,0:T(8,128)(2,1)} %bitcast.18), channel_id=1, source_target_pairs={{0,128},{1,129},{64,192},{65,193},{2,130},{3,131},{66,194},{67,195... | collective-permute-start | bytes 786440 | tf_op jit(solution)/shard_map/ppermute | solution.py:30
  10.5 1.0 copy-start.4
  11.5 0.9 copy-start.7
  14.4 1.0 copy-start.5
  16.3 141.1 %all-gather.4.cloned.1.call-start = ((), (), s32[]{:S(2)}) async-start(), calls=%async_computation.3 | async-start | bytes 1179648 | tf_op jit(solution)/shard_map/all_gather | solution.py:377
  16.3 0.9 copy-start.6
  32.2 6.0 %collective-permute-start.1 = (bf16[4,64,384]{2,1,0:T(8,128)(2,1)S(1)}, bf16[4,64,384]{2,1,0:T(8,128)(2,1)S(1)}, u32[]{:S(2)}, u32[]{:S(2)}) collective-permute-start(bf16[4,64,384]{2,1,0:T(8,128)(2,1)S(1)} %get-tuple-element.27), channel_id=1, source_target_pairs={{0,1},{1,0},{64,65},{65,64},{2,3},{3,2},{66,67},{67,66},{4,5},{5,4... | collective-permute-start | bytes 589832 | tf_op jit(solution)/shard_map/ppermute | solution.py:30
  38.3 46.6 %copy-start.10 = (bf16[2,4,64,384]{3,2,1,0:T(8,128)(2,1)}, bf16[2,4,64,384]{3,2,1,0:T(8,128)(2,1)S(1)}, u32[]{:S(2)}) copy-start(bf16[2,4,64,384]{3,2,1,0:T(8,128)(2,1)S(1)} %pad_maximum_fusion.refs_0_) | copy-start | bytes 1179652
  38.3 14.2 %collective-permute-start.5 = (bf16[2,4,64,384]{3,2,1,0:T(8,128)(2,1)S(1)}, bf16[2,4,64,384]{3,2,1,0:T(8,128)(2,1)S(1)}, u32[]{:S(2)}, u32[]{:S(2)}) collective-permute-start(bf16[2,4,64,384]{3,2,1,0:T(8,128)(2,1)S(1)} %pad_maximum_fusion.refs_0_), channel_id=1, source_target_pairs={{0,8},{1,9},{64,72},{65,73},{2,10},{3,11},{66,74},{67,75},{4,12},{... | collective-permute-start | bytes 1179656 | tf_op jit(solution)/shard_map/ppermute | solution.py:30
  41.3 13.1 %collective-permute-start.2 = (bf16[2,4,64,384]{3,2,1,0:T(8,128)(2,1)S(1)}, bf16[2,4,64,384]{3,2,1,0:T(8,128)(2,1)S(1)}, u32[]{:S(2)}, u32[]{:S(2)}) collective-permute-start(bf16[2,4,64,384]{3,2,1,0:T(8,128)(2,1)S(1)} %pad_maximum_fusion.refs_0_), channel_id=1, source_target_pairs={{0,56},{1,57},{64,120},{65,121},{2,58},{3,59},{66,122},{67,123},{4... | collective-permute-start | bytes 1179656 | tf_op jit(solution)/shard_map/ppermute | solution.py:30
  52.5 32.4 %copy-start.11 = (bf16[2,4,64,384]{3,2,1,0:T(8,128)(2,1)}, bf16[2,4,64,384]{3,2,1,0:T(8,128)(2,1)S(1)}, u32[]{:S(2)}) copy-start(bf16[2,4,64,384]{3,2,1,0:T(8,128)(2,1)S(1)} %collective-permute-done.5.refs_6_) | copy-start | bytes 1179652
  52.5 13.1 %collective-permute-start.6 = (bf16[2,4,64,384]{3,2,1,0:T(8,128)(2,1)S(1)}, bf16[2,4,64,384]{3,2,1,0:T(8,128)(2,1)S(1)}, u32[]{:S(2)}, u32[]{:S(2)}) collective-permute-start(bf16[2,4,64,384]{3,2,1,0:T(8,128)(2,1)S(1)} %collective-permute-done.5.refs_6_), channel_id=1, source_target_pairs={{0,8},{1,9},{64,72},{65,73},{2,10},{3,11},{66,74},{67,75},{4,12},{... | collective-permute-start | bytes 1179656 | tf_op jit(solution)/shard_map/ppermute | solution.py:30
  54.4 30.4 %copy-start.12 = (bf16[2,4,64,384]{3,2,1,0:T(8,128)(2,1)}, bf16[2,4,64,384]{3,2,1,0:T(8,128)(2,1)S(1)}, u32[]{:S(2)}) copy-start(bf16[2,4,64,384]{3,2,1,0:T(8,128)(2,1)S(1)} %collective-permute-done.2.refs_1_) | copy-start | bytes 1179652
  54.4 13.0 %collective-permute-start.3 = (bf16[2,4,64,384]{3,2,1,0:T(8,128)(2,1)S(1)}, bf16[2,4,64,384]{3,2,1,0:T(8,128)(2,1)S(1)}, u32[]{:S(2)}, u32[]{:S(2)}) collective-permute-start(bf16[2,4,64,384]{3,2,1,0:T(8,128)(2,1)S(1)} %collective-permute-done.2.refs_1_), channel_id=1, source_target_pairs={{0,56},{1,57},{64,120},{65,121},{2,58},{3,59},{66,122},{67,123},{4... | collective-permute-start | bytes 1179656 | tf_op jit(solution)/shard_map/ppermute | solution.py:30
  65.6 19.3 %copy-start.13 = (bf16[2,4,64,384]{3,2,1,0:T(8,128)(2,1)}, bf16[2,4,64,384]{3,2,1,0:T(8,128)(2,1)S(1)}, u32[]{:S(2)}) copy-start(bf16[2,4,64,384]{3,2,1,0:T(8,128)(2,1)S(1)} %collective-permute-done.6.refs_5_) | copy-start | bytes 1179652
  65.6 12.2 %collective-permute-start.7 = (bf16[2,4,64,384]{3,2,1,0:T(8,128)(2,1)S(1)}, bf16[2,4,64,384]{3,2,1,0:T(8,128)(2,1)S(1)}, u32[]{:S(2)}, u32[]{:S(2)}) collective-permute-start(bf16[2,4,64,384]{3,2,1,0:T(8,128)(2,1)S(1)} %collective-permute-done.6.refs_5_), channel_id=1, source_target_pairs={{0,8},{1,9},{64,72},{65,73},{2,10},{3,11},{66,74},{67,75},{4,12},{... | collective-permute-start | bytes 1179656 | tf_op jit(solution)/shard_map/ppermute | solution.py:30
  67.5 17.4 %copy-start.14 = (bf16[2,4,64,384]{3,2,1,0:T(8,128)(2,1)}, bf16[2,4,64,384]{3,2,1,0:T(8,128)(2,1)S(1)}, u32[]{:S(2)}) copy-start(bf16[2,4,64,384]{3,2,1,0:T(8,128)(2,1)S(1)} %collective-permute-done.3.refs_2_) | copy-start | bytes 1179652
  67.5 16.5 %collective-permute-start.4 = (bf16[2,4,64,384]{3,2,1,0:T(8,128)(2,1)S(1)}, bf16[2,4,64,384]{3,2,1,0:T(8,128)(2,1)}, u32[]{:S(2)}, u32[]{:S(2)}) collective-permute-start(bf16[2,4,64,384]{3,2,1,0:T(8,128)(2,1)S(1)} %collective-permute-done.3.refs_2_), channel_id=1, source_target_pairs={{0,56},{1,57},{64,120},{65,121},{2,58},{3,59},{66,122},{67,123},{4... | collective-permute-start | bytes 1179656 | tf_op jit(solution)/shard_map/ppermute | solution.py:30
  77.8 7.1 %copy-start.15 = (bf16[2,4,64,384]{3,2,1,0:T(8,128)(2,1)}, bf16[2,4,64,384]{3,2,1,0:T(8,128)(2,1)S(1)}, u32[]{:S(2)}) copy-start(bf16[2,4,64,384]{3,2,1,0:T(8,128)(2,1)S(1)} %collective-permute-done.7.refs_4_) | copy-start | bytes 1179652
  77.8 11.3 %collective-permute-start.8 = (bf16[2,4,64,384]{3,2,1,0:T(8,128)(2,1)S(1)}, bf16[2,4,64,384]{3,2,1,0:T(8,128)(2,1)S(1)}, u32[]{:S(2)}, u32[]{:S(2)}) collective-permute-start(bf16[2,4,64,384]{3,2,1,0:T(8,128)(2,1)S(1)} %collective-permute-done.7.refs_4_), channel_id=1, source_target_pairs={{0,8},{1,9},{64,72},{65,73},{2,10},{3,11},{66,74},{67,75},{4,12},{... | collective-permute-start | bytes 1179656 | tf_op jit(solution)/shard_map/ppermute | solution.py:30
  79.7 8.8 %collective-permute-start.9 = (bf16[32,384]{1,0:T(8,128)(2,1)S(1)}, bf16[32,384]{1,0:T(8,128)(2,1)S(1)}, u32[]{:S(2)}, u32[]{:S(2)}) collective-permute-start(bf16[32,384]{1,0:T(8,128)(2,1)S(1)} %get-tuple-element.36.up), channel_id=1, source_target_pairs={{0,1},{1,0},{64,65},{65,64},{2,3},{3,2},{66,67},{67,66},{4,5},{5,4... | collective-permute-start | bytes 73736 | tf_op jit(solution)/shard_map/ppermute | solution.py:30
  84.9 4.3 %copy-start.1 = (bf16[4352,512]{1,0:T(8,128)(2,1)S(1)}, bf16[4352,512]{1,0:T(8,128)(2,1)}, u32[]{:S(2)}) copy-start(bf16[4352,512]{1,0:T(8,128)(2,1)} %all-gather.6.cloned.1.call-done) | copy-start | bytes 13369348
  84.9 17.7 %copy-start.16 = (bf16[512,64]{0,1:T(8,128)(2,1)S(1)}, bf16[512,64]{0,1:T(8,128)(2,1)}, u32[]{:S(2)}) copy-start(bf16[512,64]{0,1:T(8,128)(2,1)} %param.15) | copy-start | bytes 196612
  84.9 24.2 %copy-start.3 = (bf16[512,128]{1,0:T(8,128)(2,1)S(1)}, bf16[512,128]{1,0:T(8,128)(2,1)}, u32[]{:S(2)}) copy-start(bf16[512,128]{1,0:T(8,128)(2,1)} %filters_ref.3) | copy-start | bytes 393220
  84.9 32.5 %copy-start.8 = (s32[2,32]{1,0:T(2,128)S(1)}, s32[2,32]{1,0:T(2,128)}, u32[]{:S(2)}) copy-start(s32[2,32]{1,0:T(2,128)} %lengths.3) | copy-start | bytes 772
  89.1 1.9 %copy-start = (bf16[3,2048,256]{2,1,0:T(8,128)(2,1)S(1)}, bf16[3,2048,256]{2,1,0:T(8,128)(2,1)}, u32[]{:S(2)}) copy-start(bf16[3,2048,256]{2,1,0:T(8,128)(2,1)} %pack_weights.1.packed) | copy-start | bytes 9437188
  97.4 6.7 %collective-permute-start.10 = (bf16[4,256,256]{2,1,0:T(8,128)(2,1)S(1)}, bf16[4,256,256]{2,1,0:T(8,128)(2,1)S(1)}, u32[]{:S(2)}, u32[]{:S(2)}) collective-permute-start(bf16[4,256,256]{2,1,0:T(8,128)(2,1)S(1)} %get-tuple-element.38), channel_id=1, source_target_pairs={{0,1},{1,0},{64,65},{65,64},{2,3},{3,2},{66,67},{67,66},{4,5},{5,4... | collective-permute-start | bytes 1572872 | tf_op jit(solution)/shard_map/ppermute | solution.py:30
  104.2 7.4 %collective-permute-start.11 = (bf16[4,256,128]{2,1,0:T(8,128)(2,1)S(1)}, bf16[4,256,128]{2,1,0:T(8,128)(2,1)S(1)}, u32[]{:S(2)}, u32[]{:S(2)}) collective-permute-start(bf16[4,256,128]{2,1,0:T(8,128)(2,1)S(1)} %get-tuple-element.41), channel_id=1, source_target_pairs={{0,1},{1,0},{64,65},{65,64},{2,3},{3,2},{66,67},{67,66},{4,5},{5,4... | collective-permute-start | bytes 786440 | tf_op jit(solution)/shard_map/ppermute | solution.py:30
  106.5 10.9 %collective-permute-start.12 = (bf16[4,2,128,128]{3,2,1,0:T(8,128)(2,1)S(1)}, bf16[4,2,128,128]{3,2,1,0:T(8,128)(2,1)S(1)}, u32[]{:S(2)}, u32[]{:S(2)}) collective-permute-start(bf16[4,2,128,128]{3,2,1,0:T(8,128)(2,1)S(1)} %combine_kv.1.kv_ref), channel_id=1, source_target_pairs={{0,8},{1,9},{64,72},{65,73},{2,10},{3,11},{66,74},{67,75},{4,12},{... | collective-permute-start | bytes 786440 | tf_op jit(solution)/shard_map/ppermute | solution.py:30
  108.5 3.2 %collective-permute-start.13 = (bf16[2,128,128]{2,1,0:T(8,128)(2,1)S(1)}, bf16[2,128,128]{2,1,0:T(8,128)(2,1)S(1)}, u32[]{:S(2)}, u32[]{:S(2)}) collective-permute-start(bf16[2,128,128]{2,1,0:T(8,128)(2,1)S(1)} %slice_bitcast_fusion), channel_id=1, source_target_pairs={{56,256},{57,257},{120,320},{121,321},{58,258},{59,259},{122,322},... | collective-permute-start | bytes 196616 | tf_op jit(solution)/shard_map/ppermute | solution.py:30
  157.4 1.2 copy-start.2
  (1 other events, 0.7 us)
Sparse Core Ops, SparseCore 0:
  16.4 68.4 all-gather.5
  104.4 33.7 all-gather.3

commit v6 on v5

--- a/solution.py
+++ b/solution.py
@@ -85,23 +85,26 @@
         place_rows(out_ref, held.at[i], lax.rem(position()[3] + dist, NY))
 
 
-def project_kernel(tokens, packed, last, up, up_other, kv_own, kv_send, q_own, q_send, weight):
+def low_kernel(tokens, low_ref):
+    _, half, ranks = low_ref.shape
+    row = lax.broadcasted_iota(jnp.int32, (half, ranks), 0)
+    column = lax.broadcasted_iota(jnp.int32, (half, ranks), 1)
+    mine = (row >= half // 2) == (column >= ranks // 2)
+    for quarter in range(4):
+        down = jnp.concatenate([tokens[z, 2 * half :, :] for z in range(quarter % 2, NZ, 2)], axis=1)
+        low = nt_dot(rows_of(tokens, quarter, half), down)
+        low_ref[quarter] = jnp.where(mine, adapter_scale * low, 0.0).astype(low_ref.dtype)
+
+
+def project_kernel(tokens, packed, last, low_ref, up, up_other, kv_own, kv_send, q_own, q_send, weight):
     weight[...] = packed[...]
     place_rows(weight, last, lax.rem(position()[3] + NY // 2, NY))
     half = kv_own.shape[1]
     ch = up.shape[1] // 3
-    ranks = up.shape[0]
-    row = lax.broadcasted_iota(jnp.int32, (half, ranks), 0)
-    column = lax.broadcasted_iota(jnp.int32, (half, ranks), 1)
-    mine = (row >= half // 2) == (column >= ranks // 2)
     q_up = jnp.concatenate([up[:, :ch], up_other[:, :ch]], axis=1)
-    lows = {}
     for quarter in (0, 2, 1, 3):
-        z_lo = quarter % 2
-        down = jnp.concatenate([tokens[z, 2 * half :, :] for z in range(z_lo, NZ, 2)], axis=1)
         a = rows_of(tokens, quarter, half)
-        low = jnp.where(mine, adapter_scale * nt_dot(a, down), 0.0).astype(jnp.bfloat16)
-        lows[quarter] = low
+        low = low_ref[quarter]
         for side in range(2):
             part = jnp.dot(a, weight[side], preferred_element_type=jnp.float32)
             ups = (up if side == 0 else up_other)[:, ch:]
@@ -112,7 +115,7 @@
                 kv_send[quarter] = part.astype(kv_send.dtype)
     for quarter in range(4):
         part = jnp.dot(rows_of(tokens, quarter, half), weight[2], preferred_element_type=jnp.float32)
-        part += jnp.dot(lows[quarter], q_up, preferred_element_type=jnp.float32)
+        part += jnp.dot(low_ref[quarter], q_up, preferred_element_type=jnp.float32)
         q_own[quarter] = part[:, :ch]
         q_send[quarter] = part[:, ch:].astype(q_send.dtype)
 
@@ -198,52 +201,75 @@
     lax.fori_loop(0, 8, block, 0)
 
 
-def gate_kernel(lengths, part_ref, own_ref, met_ref, prev_ref, wrap_ref, filters_ref, out_ref, ext, sums, taps, edges):
-    x_hi, _, _, y, _, _ = position()
-    rows, ch = part_ref.shape[2], part_ref.shape[3]
-    groups = rows // 8
-    count = out_ref.shape[1]
+def fill_edges(lengths, edges):
     each = lengths.shape[1] // 8
-    fill_taps(filters_ref, taps)
     for seg in range(2):
         start = jnp.int32(0)
         for window in range(lengths.shape[1]):
             at = (window // each) * 2 * each + seg * each + window % each
             end = start + lengths[seg, window]
-            edges[0, at : at + 1, :] = jnp.full((1, rows), start, jnp.int32)
-            edges[1, at : at + 1, :] = jnp.full((1, rows), end, jnp.int32)
+            edges[0, at : at + 1, :] = jnp.full((1, edges.shape[2]), start, jnp.int32)
+            edges[1, at : at + 1, :] = jnp.full((1, edges.shape[2]), end, jnp.int32)
             start = end
-    sums[...] = jnp.zeros((count, ch), jnp.float32)
+
+
+def gate_block(quarter, seg, before, part_ref, own_ref, met_ref, taps, edges, ext, sums):
+    x_hi, _, _, y, _, _ = position()
+    rows, ch = part_ref.shape[2], part_ref.shape[3]
+    groups = rows // 8
+    count = sums.shape[0]
     row = lax.broadcasted_iota(jnp.int32, (count, rows), 0)
     column = lax.broadcasted_iota(jnp.int32, (count, rows), 1)
-    row_seg = lax.rem(row // each, 2)
+    row_seg = lax.rem(row // 4, 2)
+    ext[0:8, :] = jnp.zeros((8, ch), jnp.float32)
+    ext[8 : 8 + rows, :] = before.astype(jnp.float32)
+    ext[8 + rows :, :] = jnp.zeros((8, ch), jnp.float32)
+    total = [part_ref[quarter, seg, 8 * g : 8 * g + 8, :] for g in range(groups)]
+    for r in range(8):
+        shifted = [ext[8 * g + 8 - r : 8 * g + 16 - r, :] for g in range(groups + (1 if r else 0))]
+        for s in range(groups):
+            tap = spread_taps(taps, 8 * s + r, ch)
+            for g in range(groups):
+                if groups + g - s < len(shifted):
+                    total[g] = total[g] + tap * shifted[groups + g - s]
+    at_rows = pl.ds(pl.multiple_of(seg * rows, rows), rows)
+    q = own_ref[quarter, at_rows, :] + met_ref[quarter, at_rows, :].astype(jnp.float32)
+    gated = (q * jnp.concatenate(total, axis=0)).astype(jnp.bfloat16)
+    place = ((x_hi * 4 + quarter) * NY + y) * rows + column
+    inside = (place >= edges[0]) & (place < edges[1]) & (row_seg == seg)
+    member = inside.astype(jnp.float32).astype(jnp.bfloat16)
+    sums[...] += jnp.dot(member, gated, preferred_element_type=jnp.float32)
+
+
+def gate_most_kernel(lengths, part_ref, own_ref, met_ref, prev_ref, filters_ref, sums, ext, taps, edges):
+    fill_taps(filters_ref, taps)
+    fill_edges(lengths, edges)
+    sums[...] = jnp.zeros(sums.shape, jnp.float32)
+    y = position()[3]
 
     def block(n, carry):
         quarter, seg = n // 2, lax.rem(n, 2)
-        at = jnp.where(y > 0, quarter, jnp.maximum(quarter - 1, 0))
-        before = prev_ref[at, seg].astype(jnp.float32)
-        wrapped = wrap_ref[seg].astype(jnp.float32)
-        ext[0:8, :] = jnp.zeros((8, ch), jnp.float32)
-        ext[8 : 8 + rows, :] = jnp.where((y == 0) & (quarter == 0), wrapped, before)
-        ext[8 + rows :, :] = jnp.zeros((8, ch), jnp.float32)
-        total = [part_ref[quarter, seg, 8 * g : 8 * g + 8, :] for g in range(groups)]
-        for r in range(8):
-            shifted = [ext[8 * g + 8 - r : 8 * g + 16 - r, :] for g in range(groups + (1 if r else 0))]
-            for s in range(groups):
-                tap = spread_taps(taps, 8 * s + r, ch)
-                for g in range(groups):
-                    if groups + g - s < len(shifted):
-                        total[g] = total[g] + tap * shifted[groups + g - s]
-        at_rows = pl.ds(pl.multiple_of(seg * rows, rows), rows)
-        q = own_ref[quarter, at_rows, :] + met_ref[quarter, at_rows, :].astype(jnp.float32)
-        gated = (q * jnp.concatenate(total, axis=0)).astype(jnp.bfloat16)
-        place = ((x_hi * 4 + quarter) * NY + y) * rows + column
-        inside = (place >= edges[0]) & (place < edges[1]) & (row_seg == seg)
-        member = inside.astype(jnp.float32).astype(jnp.bfloat16)
-        sums[...] += jnp.dot(member, gated, preferred_element_type=jnp.float32)
+        before = prev_ref[jnp.where(y > 0, quarter, quarter - 1), seg]
+        gate_block(quarter, seg, before, part_ref, own_ref, met_ref, taps, edges, ext, sums)
         return carry
 
-    lax.fori_loop(0, 8, block, 0)
+    lax.fori_loop(2, 8, block, 0)
+
+
+def gate_first_kernel(
+    lengths, most_ref, part_ref, own_ref, met_ref, prev_ref, wrap_ref, filters_ref, out_ref, ext, taps, edges, sums
+):
+    fill_taps(filters_ref, taps)
+    fill_edges(lengths, edges)
+    sums[...] = most_ref[...]
+    y = position()[3]
+
+    def block(seg, carry):
+        before = jnp.where(y > 0, prev_ref[0, seg].astype(jnp.float32), wrap_ref[seg].astype(jnp.float32))
+        gate_block(0, seg, before, part_ref, own_ref, met_ref, taps, edges, ext, sums)
+        return carry
+
+    lax.fori_loop(0, 2, block, 0)
     for copy in range(out_ref.shape[0]):
         out_ref[copy] = sums[...].astype(out_ref.dtype)
 
@@ -320,17 +346,18 @@
     )
     own = tokens.reshape(half, depth)
     other = x_pair_swap(own)
-    piece = call(
-        join_kernel, "join_rows", jax.ShapeDtypeStruct((2 * half + ranks, depth), bf16), (own, other, down)
-    )
-    gathered = lax.all_gather(piece, ("zhi", "zlo"), axis=0, tiled=False)
-
     spread = call(
         spread_kernel,
         "spread_weight",
         jax.ShapeDtypeStruct((8, w_rows, 3 * ch), bf16),
         (in_weight.transpose(1, 0, 2),),
     )
+    spread, other = lax.optimization_barrier((spread, other))
+    piece = call(
+        join_kernel, "join_rows", jax.ShapeDtypeStruct((2 * half + ranks, depth), bf16), (own, other, down)
+    )
+    gathered = lax.all_gather(piece, ("zhi", "zlo"), axis=0, tiled=False)
+
     spread, piece = lax.optimization_barrier((spread, piece))
     met = lax.all_to_all(spread, ("xhi", "xlo", "zlo"), 0, 0, tiled=True)
     split = jax.ShapeDtypeStruct((4, w_rows, 3 * ch), bf16)
@@ -345,7 +372,6 @@
     cut = (4, half)
     features = w_rows * NY * 4
     early = [weight[d] for d in range(NY) if d != NY // 2]
-    gathered, *early = lax.optimization_barrier((gathered, *early))
     packed = call(
         pack_kernel,
         "pack_weights",
@@ -355,6 +381,7 @@
         vmem=56,
         where=NY - 1,
     )
+    low = call(low_kernel, "low_rank", jax.ShapeDtypeStruct((*cut, ranks), bf16), (gathered,))
     kv_own, kv_send, q_own, q_send = call(
         project_kernel,
         "project",
@@ -364,7 +391,7 @@
             jax.ShapeDtypeStruct((*cut, ch), f32),
             jax.ShapeDtypeStruct((*cut, ch), bf16),
         ),
-        (gathered, packed, weight[NY // 2], up, up_other),
+        (gathered, packed, weight[NY // 2], low, up, up_other),
         [pltpu.VMEM(packed.shape, bf16)],
     )
     kv = call(
@@ -377,7 +404,6 @@
     whole = lax.all_gather(wide, TENSOR, axis=0, tiled=True)
     prev = permute(kv, lambda x, y, z, c: (x, y + 1, z, c))
     wrap = permute(kv[3], lambda x, y, z, c: (x + 2, 0, z, c), lambda x, y, z, c: x < 2 and y == NY - 1)
-    q_met = core_swap(q_send)
     part = call(
         conv_own_kernel,
         "conv_own",
@@ -385,17 +411,27 @@
         (kv, filters),
         [pltpu.VMEM((8 + rows, ch), f32), pltpu.VMEM((filters.shape[1], ch), f32)],
     )
+    part, q_send = lax.optimization_barrier((part, q_send))
+    q_met = core_swap(q_send)
+    gate_scratch = [
+        pltpu.VMEM((16 + rows, ch), f32),
+        pltpu.VMEM((filters.shape[1], ch), f32),
+        pltpu.VMEM((2, count, rows), jnp.int32),
+    ]
+    most = call(
+        gate_most_kernel,
+        "gate_most",
+        jax.ShapeDtypeStruct((count, ch), f32),
+        (window_lengths, part, q_own, q_met, prev, filters),
+        gate_scratch,
+        scalars=True,
+    )
     total = call(
-        gate_kernel,
-        "gate_pool",
+        gate_first_kernel,
+        "gate_first",
         jax.ShapeDtypeStruct((NY, count, ch), bf16),
-        (window_lengths, part, q_own, q_met, prev, wrap, filters),
-        [
-            pltpu.VMEM((16 + rows, ch), f32),
-            pltpu.VMEM((count, ch), f32),
-            pltpu.VMEM((filters.shape[1], ch), f32),
-            pltpu.VMEM((2, count, rows), jnp.int32),
-        ],
+        (window_lengths, most, part, q_own, q_met, prev, wrap, filters),
+        [*gate_scratch, pltpu.VMEM((count, ch), f32)],
         scalars=True,
     )
 

time: 168 us -> 164 us (0.976)
  local copies, waits for them, and re-layouts: 7.59 us -> 11.6 us
  starting transfers between devices: 45 us -> 41.5 us
  waiting for transfers between devices: 29.4 us -> 26.1 us
    unnamed x34 -> x38, local copies, waits for them, and re-layouts: 7.58 us -> 11.6 us
    ppermute x14, starting transfers between devices: 45 us -> 41.4 us  [permute(): return lax.ppermute(value, AXES, pairs)]
    ppermute x14, waiting for transfers between devices: 28.5 us -> 26.1 us  [permute(): return lax.ppermute(value, AXES, pairs)]
    pallas_call x11 -> x13, Pallas kernels: 19.7 us -> 19.2 us  [call(): pl.pallas_call(kernel, out_shape=out, in_specs=[SMEM] * scalars + [ANY] *...]
  transfers between devices with their start and end apart: 16 -> 16, of which waited for: 9 -> 7; matrix products, arithmetic and copies ran while one was open for 0% -> 0% of each run, Pallas kernels for 7% -> 8%
where the time goes in v6:
time: 164 us; the launch traced here: 163 us
  blocking collectives  50.2 us (31%)
  starting transfers between devices  41.5 us (25%)
  waiting for transfers between devices  26.1 us (16%)
  Pallas kernels  19.2 us (12%)
  between operations  13.8 us (8%)
  local copies, waits for them, and re-layouts  11.6 us (7%)
    ppermute x14, starting transfers between devices, permute(): return lax.ppermute(value, AXES, pairs)  41.4 us
    ppermute x14, waiting for transfers between devices, permute(): return lax.ppermute(value, AXES, pairs)  26.1 us
    all_to_all x1, blocking collectives, local(): met = lax.all_to_all(total.reshape(64, 8, ch), rest, 0, 0, tiled=True)  22.5 us
    pallas_call x13, Pallas kernels, call(): pl.pallas_call(kernel, out_shape=out, in_specs=[SMEM] * scalars + [ANY] *...  19.2 us
    all_to_all x1, blocking collectives, local(): met = lax.all_to_all(spread, ('xhi', 'xlo', 'zlo'), 0, 0, tiled=True)  14.6 us
    all_to_all x1, blocking collectives, local(): met = lax.all_to_all(total, 'y', 0, 0, tiled=True)  13.2 us
    unnamed x38, local copies, waits for them, and re-layouts  11.6 us
  transfers between devices with their start and end apart: 16, of which 7 were waited for; matrix products, arithmetic and copies ran while one was open for 0% of the time, Pallas kernels for 8%

profile of v6, /device:TPU:1, one launch (start us, length us, event | category | flops | bytes accessed | tf_op | source)
XLA Modules:
  0.0 163.2 jit_solution(7162177834542424847)
XLA Ops:
  6.5 3.9 %collective-permute-start = (bf16[256,512]{1,0:T(8,128)(2,1)}, bf16[256,512]{1,0:T(8,128)(2,1)S(1)}, u32[]{:S(2)}, u32[]{:S(2)}) collective-permute-start(bf16[256,512]{1,0:T(8,128)(2,1)} %bitcast.19), channel_id=1, source_target_pairs={{0,128},{1,129},{64,192},{65,193},{2,130},{3,131},{66,194},{67,195... | collective-permute-start | bytes 786440 | tf_op jit(solution)/shard_map/ppermute | solution.py:30
  16.7 14.6 %all_to_all.15.met_ref = bf16[8,64,384]{2,1,0:T(8,128)(2,1)S(1)} all-to-all(bf16[8,64,384]{2,1,0:T(8,128)(2,1)S(1)} %spread_weight.1), channel_id=1, replica_groups=mesh['xhi'=2,'xlo'=2,'zlo'=2,'y'=8,'zhi'=4,'core'=2] {'xhi','xlo','zlo'}, dimensions={0} | all-to-all | bytes 786432 | tf_op jit(solution)/shard_map/all_to_all | solution.py:362
  31.3 5.0 %collective-permute-start.1 = (bf16[4,64,384]{2,1,0:T(8,128)(2,1)S(1)}, bf16[4,64,384]{2,1,0:T(8,128)(2,1)S(1)}, u32[]{:S(2)}, u32[]{:S(2)}) collective-permute-start(bf16[4,64,384]{2,1,0:T(8,128)(2,1)S(1)} %get-tuple-element.25), channel_id=1, source_target_pairs={{0,1},{1,0},{64,65},{65,64},{2,3},{3,2},{66,67},{67,66},{4,5},{5,4... | collective-permute-start | bytes 589832 | tf_op jit(solution)/shard_map/ppermute | solution.py:30
  36.3 1.0 collective-permute-done.1
  37.4 3.0 %collective-permute-start.5 = (bf16[2,4,64,384]{3,2,1,0:T(8,128)(2,1)S(1)}, bf16[2,4,64,384]{3,2,1,0:T(8,128)(2,1)S(1)}, u32[]{:S(2)}, u32[]{:S(2)}) collective-permute-start(bf16[2,4,64,384]{3,2,1,0:T(8,128)(2,1)S(1)} %pad_maximum_fusion.refs_0_), channel_id=1, source_target_pairs={{0,8},{1,9},{64,72},{65,73},{2,10},{3,11},{66,74},{67,75},{4,12},{... | collective-permute-start | bytes 1179656 | tf_op jit(solution)/shard_map/ppermute | solution.py:30
  40.4 3.8 %collective-permute-start.2 = (bf16[2,4,64,384]{3,2,1,0:T(8,128)(2,1)S(1)}, bf16[2,4,64,384]{3,2,1,0:T(8,128)(2,1)S(1)}, u32[]{:S(2)}, u32[]{:S(2)}) collective-permute-start(bf16[2,4,64,384]{3,2,1,0:T(8,128)(2,1)S(1)} %pad_maximum_fusion.refs_0_), channel_id=1, source_target_pairs={{0,56},{1,57},{64,120},{65,121},{2,58},{3,59},{66,122},{67,123},{4... | collective-permute-start | bytes 1179656 | tf_op jit(solution)/shard_map/ppermute | solution.py:30
  44.2 7.3 %collective-permute-done.5.refs_6_ = bf16[2,4,64,384]{3,2,1,0:T(8,128)(2,1)S(1)} collective-permute-done((bf16[2,4,64,384]{3,2,1,0:T(8,128)(2,1)S(1)}, bf16[2,4,64,384]{3,2,1,0:T(8,128)(2,1)S(1)}, u32[]{:S(2)}, u32[]{:S(2)}) %collective-permute-start.5) | collective-permute-done | bytes 393248 | tf_op jit(solution)/shard_map/ppermute | solution.py:30
  51.6 1.9 %collective-permute-start.6 = (bf16[2,4,64,384]{3,2,1,0:T(8,128)(2,1)S(1)}, bf16[2,4,64,384]{3,2,1,0:T(8,128)(2,1)S(1)}, u32[]{:S(2)}, u32[]{:S(2)}) collective-permute-start(bf16[2,4,64,384]{3,2,1,0:T(8,128)(2,1)S(1)} %collective-permute-done.5.refs_6_), channel_id=1, source_target_pairs={{0,8},{1,9},{64,72},{65,73},{2,10},{3,11},{66,74},{67,75},{4,12},{... | collective-permute-start | bytes 1179656 | tf_op jit(solution)/shard_map/ppermute | solution.py:30
  53.5 4.6 %collective-permute-start.3 = (bf16[2,4,64,384]{3,2,1,0:T(8,128)(2,1)S(1)}, bf16[2,4,64,384]{3,2,1,0:T(8,128)(2,1)S(1)}, u32[]{:S(2)}, u32[]{:S(2)}) collective-permute-start(bf16[2,4,64,384]{3,2,1,0:T(8,128)(2,1)S(1)} %collective-permute-done.2.refs_1_), channel_id=1, source_target_pairs={{0,56},{1,57},{64,120},{65,121},{2,58},{3,59},{66,122},{67,123},{4... | collective-permute-start | bytes 1179656 | tf_op jit(solution)/shard_map/ppermute | solution.py:30
  58.1 6.5 %collective-permute-done.6.refs_5_ = bf16[2,4,64,384]{3,2,1,0:T(8,128)(2,1)S(1)} collective-permute-done((bf16[2,4,64,384]{3,2,1,0:T(8,128)(2,1)S(1)}, bf16[2,4,64,384]{3,2,1,0:T(8,128)(2,1)S(1)}, u32[]{:S(2)}, u32[]{:S(2)}) %collective-permute-start.6) | collective-permute-done | bytes 393248 | tf_op jit(solution)/shard_map/ppermute | solution.py:30
  64.6 1.9 %collective-permute-start.7 = (bf16[2,4,64,384]{3,2,1,0:T(8,128)(2,1)S(1)}, bf16[2,4,64,384]{3,2,1,0:T(8,128)(2,1)S(1)}, u32[]{:S(2)}, u32[]{:S(2)}) collective-permute-start(bf16[2,4,64,384]{3,2,1,0:T(8,128)(2,1)S(1)} %collective-permute-done.6.refs_5_), channel_id=1, source_target_pairs={{0,8},{1,9},{64,72},{65,73},{2,10},{3,11},{66,74},{67,75},{4,12},{... | collective-permute-start | bytes 1179656 | tf_op jit(solution)/shard_map/ppermute | solution.py:30
  66.6 4.6 %collective-permute-start.4 = (bf16[2,4,64,384]{3,2,1,0:T(8,128)(2,1)S(1)}, bf16[2,4,64,384]{3,2,1,0:T(8,128)(2,1)S(1)}, u32[]{:S(2)}, u32[]{:S(2)}) collective-permute-start(bf16[2,4,64,384]{3,2,1,0:T(8,128)(2,1)S(1)} %collective-permute-done.3.refs_2_), channel_id=1, source_target_pairs={{0,56},{1,57},{64,120},{65,121},{2,58},{3,59},{66,122},{67,123},{4... | collective-permute-start | bytes 1179656 | tf_op jit(solution)/shard_map/ppermute | solution.py:30
  71.2 5.7 %collective-permute-done.7.refs_4_ = bf16[2,4,64,384]{3,2,1,0:T(8,128)(2,1)S(1)} collective-permute-done((bf16[2,4,64,384]{3,2,1,0:T(8,128)(2,1)S(1)}, bf16[2,4,64,384]{3,2,1,0:T(8,128)(2,1)S(1)}, u32[]{:S(2)}, u32[]{:S(2)}) %collective-permute-start.7) | collective-permute-done | bytes 393248 | tf_op jit(solution)/shard_map/ppermute | solution.py:30
  76.9 1.9 %collective-permute-start.8 = (bf16[2,4,64,384]{3,2,1,0:T(8,128)(2,1)S(1)}, bf16[2,4,64,384]{3,2,1,0:T(8,128)(2,1)S(1)}, u32[]{:S(2)}, u32[]{:S(2)}) collective-permute-start(bf16[2,4,64,384]{3,2,1,0:T(8,128)(2,1)S(1)} %collective-permute-done.7.refs_4_), channel_id=1, source_target_pairs={{0,8},{1,9},{64,72},{65,73},{2,10},{3,11},{66,74},{67,75},{4,12},{... | collective-permute-start | bytes 1179656 | tf_op jit(solution)/shard_map/ppermute | solution.py:30
  78.8 4.3 %collective-permute-start.9 = (bf16[32,384]{1,0:T(8,128)(2,1)S(1)}, bf16[32,384]{1,0:T(8,128)(2,1)S(1)}, u32[]{:S(2)}, u32[]{:S(2)}) collective-permute-start(bf16[32,384]{1,0:T(8,128)(2,1)S(1)} %get-tuple-element.26.up), channel_id=1, source_target_pairs={{0,1},{1,0},{64,65},{65,64},{2,3},{3,2},{66,67},{67,66},{4,5},{5,4... | collective-permute-start | bytes 73736 | tf_op jit(solution)/shard_map/ppermute | solution.py:30
  83.9 3.5 %pack_weights.1.packed = bf16[3,2048,256]{2,1,0:T(8,128)(2,1)} custom-call(bf16[2,4,64,384]{3,2,1,0:T(8,128)(2,1)} %copy-done.11, bf16[2,4,64,384]{3,2,1,0:T(8,128)(2,1)} %copy-done.13, bf16[2,4,64,384]{3,2,1,0:T(8,128)(2,1)} %copy-done.16, bf16[2,4,64,384]{3,2,1,0:T(8,128)(2,1)} %copy-done.17, bf16[2,4,64,384]{3,2,1,0:T(8,128)(2,1)} %copy-done.15, ...), custom_call_target="tpu_custom_call" | custom-call | tf_op jit(solution)/shard_map/pack_weights/pallas_call | solution.py:317
  87.4 2.3 %copy-done = bf16[4352,512]{1,0:T(8,128)(2,1)S(1)} copy-done((bf16[4352,512]{1,0:T(8,128)(2,1)S(1)}, bf16[4352,512]{1,0:T(8,128)(2,1)}, u32[]{:S(2)}) %copy-start) | copy-done | bytes 4456472
  89.7 1.2 low_rank.1.low_ref
  91.9 1.9 %copy-done.2 = bf16[3,2048,256]{2,1,0:T(8,128)(2,1)S(1)} copy-done((bf16[3,2048,256]{2,1,0:T(8,128)(2,1)S(1)}, bf16[3,2048,256]{2,1,0:T(8,128)(2,1)}, u32[]{:S(2)}) %copy-start.2) | copy-done | bytes 3145752
  93.8 4.0 %project.1 = (f32[4,256,256]{2,1,0:T(8,128)S(1)}, bf16[4,256,256]{2,1,0:T(8,128)(2,1)S(1)}, f32[4,256,128]{2,1,0:T(8,128)S(1)}, bf16[4,256,128]{2,1,0:T(8,128)(2,1)S(1)}) custom-call(bf16[8,544,512]{2,1,0:T(8,128)(2,1)S(1)} %bitcast.15, bf16[3,2048,256]{2,1,0:T(8,128)(2,1)S(1)} %copy-done.2, bf16[2,4,64,384]{3,2,1,0:T(8,128)(2,1)S(1)} %collective-permute-done.8.last, ...), custom_call_target="tpu_custom_call" | custom-call | tf_op jit(solution)/shard_map/project/pallas_call | solution.py:317
  97.8 1.9 %collective-permute-start.10 = (bf16[4,256,256]{2,1,0:T(8,128)(2,1)S(1)}, bf16[4,256,256]{2,1,0:T(8,128)(2,1)S(1)}, u32[]{:S(2)}, u32[]{:S(2)}) collective-permute-start(bf16[4,256,256]{2,1,0:T(8,128)(2,1)S(1)} %get-tuple-element.28), channel_id=1, source_target_pairs={{0,1},{1,0},{64,65},{65,64},{2,3},{3,2},{66,67},{67,66},{4,5},{5,4... | collective-permute-start | bytes 1572872 | tf_op jit(solution)/shard_map/ppermute | solution.py:30
  100.4 1.2 collective-permute-done.10.met_ref
  101.8 1.9 %collective-permute-start.12 = (bf16[4,2,128,128]{3,2,1,0:T(8,128)(2,1)S(1)}, bf16[4,2,128,128]{3,2,1,0:T(8,128)(2,1)S(1)}, u32[]{:S(2)}, u32[]{:S(2)}) collective-permute-start(bf16[4,2,128,128]{3,2,1,0:T(8,128)(2,1)S(1)} %combine_kv.1.kv_ref), channel_id=1, source_target_pairs={{0,8},{1,9},{64,72},{65,73},{2,10},{3,11},{66,74},{67,75},{4,12},{... | collective-permute-start | bytes 786440 | tf_op jit(solution)/shard_map/ppermute | solution.py:30
  103.7 2.5 %conv_own.1.part_ref = f32[4,2,128,128]{3,2,1,0:T(8,128)S(1)} custom-call(bf16[4,2,128,128]{3,2,1,0:T(8,128)(2,1)S(1)} %combine_kv.1.kv_ref, bf16[512,128]{1,0:T(8,128)(2,1)S(1)} %copy-done.3), custom_call_target="tpu_custom_call" | custom-call | tf_op jit(solution)/shard_map/conv_own/pallas_call | solution.py:317
  106.2 2.0 %collective-permute-start.11 = (bf16[4,256,128]{2,1,0:T(8,128)(2,1)S(1)}, bf16[4,256,128]{2,1,0:T(8,128)(2,1)S(1)}, u32[]{:S(2)}, u32[]{:S(2)}) collective-permute-start(bf16[4,256,128]{2,1,0:T(8,128)(2,1)S(1)} %get-tuple-element.33), channel_id=1, source_target_pairs={{0,1},{1,0},{64,65},{65,64},{2,3},{3,2},{66,67},{67,66},{4,5},{5,4... | collective-permute-start | bytes 786440 | tf_op jit(solution)/shard_map/ppermute | solution.py:30
  109.6 3.5 %collective-permute-done.12.prev_ref = bf16[4,2,128,128]{3,2,1,0:T(8,128)(2,1)S(1)} collective-permute-done((bf16[4,2,128,128]{3,2,1,0:T(8,128)(2,1)S(1)}, bf16[4,2,128,128]{3,2,1,0:T(8,128)(2,1)S(1)}, u32[]{:S(2)}, u32[]{:S(2)}) %collective-permute-start.12) | collective-permute-done | bytes 262176 | tf_op jit(solution)/shard_map/ppermute | solution.py:30
  113.2 3.3 %gate_most.1.most_ref = f32[64,128]{1,0:T(8,128)S(1)} custom-call(s32[2,32]{1,0:T(2,128)S(1)} %copy-done.9, f32[4,2,128,128]{3,2,1,0:T(8,128)S(1)} %conv_own.1.part_ref, f32[4,256,128]{2,1,0:T(8,128)S(1)} %get-tuple-element.32.own_ref, bf16[4,256,128]{2,1,0:T(8,128)(2,1)S(1)} %collective-permute-done.11.met_ref, ...), custom_call_target="tpu_custom_call" | custom-call | tf_op jit(solution)/shard_map/gate_most/pallas_call | solution.py:317
  116.4 1.5 gate_first.1
  118.0 13.2 %all_to_all.16.met_ref = bf16[8,64,128]{2,1,0:T(8,128)(2,1)S(1)} all-to-all(bf16[8,64,128]{2,1,0:T(8,128)(2,1)S(1)} %gate_first.1), channel_id=1, replica_groups=mesh['xhi'=2,'xlo'=2,'zlo'=2,'y'=8,'zhi'=4,'core'=2] {'y'}, dimensions={0} | all-to-all | bytes 262144 | tf_op jit(solution)/shard_map/all_to_all | solution.py:438
  131.2 22.5 %all_to_all.17 = bf16[64,8,128]{2,1,0:T(8,128)(2,1)S(1)} all-to-all(bf16[64,8,128]{2,1,0:T(8,128)(2,1)S(1)} %bitcast.16), channel_id=1, replica_groups=mesh['xhi'=2,'xlo'=2,'zlo'=2,'y'=8,'zhi'=4,'core'=2] {'zhi','core','xhi'..., dimensions={0} | all-to-all | bytes 262144 | tf_op jit(solution)/shard_map/all_to_all | solution.py:441
  153.7 1.2 copy-done.4
  154.9 1.4 embed.1
  (59 shorter events, 10.2 us)
Async XLA Ops:
  6.5 80.9 %all-gather.6.cloned.1.call-start = ((), (), s32[]{:S(2)}) async-start(), calls=%async_computation.4 | async-start | bytes 5013504 | tf_op jit(solution)/shard_map/all_gather | solution.py:359
  6.5 8.2 %collective-permute-start = (bf16[256,512]{1,0:T(8,128)(2,1)}, bf16[256,512]{1,0:T(8,128)(2,1)S(1)}, u32[]{:S(2)}, u32[]{:S(2)}) collective-permute-start(bf16[256,512]{1,0:T(8,128)(2,1)} %bitcast.19), channel_id=1, source_target_pairs={{0,128},{1,129},{64,192},{65,193},{2,130},{3,131},{66,194},{67,195... | collective-permute-start | bytes 786440 | tf_op jit(solution)/shard_map/ppermute | solution.py:30
  10.5 0.9 copy-start.7
  11.5 1.0 copy-start.5
  14.7 1.0 copy-start.6
  16.6 137.1 %all-gather.4.cloned.1.call-start = ((), (), s32[]{:S(2)}) async-start(), calls=%async_computation.3 | async-start | bytes 1179648 | tf_op jit(solution)/shard_map/all_gather | solution.py:404
  31.3 6.0 %collective-permute-start.1 = (bf16[4,64,384]{2,1,0:T(8,128)(2,1)S(1)}, bf16[4,64,384]{2,1,0:T(8,128)(2,1)S(1)}, u32[]{:S(2)}, u32[]{:S(2)}) collective-permute-start(bf16[4,64,384]{2,1,0:T(8,128)(2,1)S(1)} %get-tuple-element.25), channel_id=1, source_target_pairs={{0,1},{1,0},{64,65},{65,64},{2,3},{3,2},{66,67},{67,66},{4,5},{5,4... | collective-permute-start | bytes 589832 | tf_op jit(solution)/shard_map/ppermute | solution.py:30
  37.4 45.7 %copy-start.11 = (bf16[2,4,64,384]{3,2,1,0:T(8,128)(2,1)}, bf16[2,4,64,384]{3,2,1,0:T(8,128)(2,1)S(1)}, u32[]{:S(2)}) copy-start(bf16[2,4,64,384]{3,2,1,0:T(8,128)(2,1)S(1)} %pad_maximum_fusion.refs_0_) | copy-start | bytes 1179652
  37.4 14.2 %collective-permute-start.5 = (bf16[2,4,64,384]{3,2,1,0:T(8,128)(2,1)S(1)}, bf16[2,4,64,384]{3,2,1,0:T(8,128)(2,1)S(1)}, u32[]{:S(2)}, u32[]{:S(2)}) collective-permute-start(bf16[2,4,64,384]{3,2,1,0:T(8,128)(2,1)S(1)} %pad_maximum_fusion.refs_0_), channel_id=1, source_target_pairs={{0,8},{1,9},{64,72},{65,73},{2,10},{3,11},{66,74},{67,75},{4,12},{... | collective-permute-start | bytes 1179656 | tf_op jit(solution)/shard_map/ppermute | solution.py:30
  40.4 13.1 %collective-permute-start.2 = (bf16[2,4,64,384]{3,2,1,0:T(8,128)(2,1)S(1)}, bf16[2,4,64,384]{3,2,1,0:T(8,128)(2,1)S(1)}, u32[]{:S(2)}, u32[]{:S(2)}) collective-permute-start(bf16[2,4,64,384]{3,2,1,0:T(8,128)(2,1)S(1)} %pad_maximum_fusion.refs_0_), channel_id=1, source_target_pairs={{0,56},{1,57},{64,120},{65,121},{2,58},{3,59},{66,122},{67,123},{4... | collective-permute-start | bytes 1179656 | tf_op jit(solution)/shard_map/ppermute | solution.py:30
  51.6 31.5 %copy-start.12 = (bf16[2,4,64,384]{3,2,1,0:T(8,128)(2,1)}, bf16[2,4,64,384]{3,2,1,0:T(8,128)(2,1)S(1)}, u32[]{:S(2)}) copy-start(bf16[2,4,64,384]{3,2,1,0:T(8,128)(2,1)S(1)} %collective-permute-done.5.refs_6_) | copy-start | bytes 1179652
  51.6 13.1 %collective-permute-start.6 = (bf16[2,4,64,384]{3,2,1,0:T(8,128)(2,1)S(1)}, bf16[2,4,64,384]{3,2,1,0:T(8,128)(2,1)S(1)}, u32[]{:S(2)}, u32[]{:S(2)}) collective-permute-start(bf16[2,4,64,384]{3,2,1,0:T(8,128)(2,1)S(1)} %collective-permute-done.5.refs_6_), channel_id=1, source_target_pairs={{0,8},{1,9},{64,72},{65,73},{2,10},{3,11},{66,74},{67,75},{4,12},{... | collective-permute-start | bytes 1179656 | tf_op jit(solution)/shard_map/ppermute | solution.py:30
  53.5 29.6 %copy-start.13 = (bf16[2,4,64,384]{3,2,1,0:T(8,128)(2,1)}, bf16[2,4,64,384]{3,2,1,0:T(8,128)(2,1)S(1)}, u32[]{:S(2)}) copy-start(bf16[2,4,64,384]{3,2,1,0:T(8,128)(2,1)S(1)} %collective-permute-done.2.refs_1_) | copy-start | bytes 1179652
  53.5 13.0 %collective-permute-start.3 = (bf16[2,4,64,384]{3,2,1,0:T(8,128)(2,1)S(1)}, bf16[2,4,64,384]{3,2,1,0:T(8,128)(2,1)S(1)}, u32[]{:S(2)}, u32[]{:S(2)}) collective-permute-start(bf16[2,4,64,384]{3,2,1,0:T(8,128)(2,1)S(1)} %collective-permute-done.2.refs_1_), channel_id=1, source_target_pairs={{0,56},{1,57},{64,120},{65,121},{2,58},{3,59},{66,122},{67,123},{4... | collective-permute-start | bytes 1179656 | tf_op jit(solution)/shard_map/ppermute | solution.py:30
  64.6 18.5 %copy-start.14 = (bf16[2,4,64,384]{3,2,1,0:T(8,128)(2,1)}, bf16[2,4,64,384]{3,2,1,0:T(8,128)(2,1)S(1)}, u32[]{:S(2)}) copy-start(bf16[2,4,64,384]{3,2,1,0:T(8,128)(2,1)S(1)} %collective-permute-done.6.refs_5_) | copy-start | bytes 1179652
  64.6 12.2 %collective-permute-start.7 = (bf16[2,4,64,384]{3,2,1,0:T(8,128)(2,1)S(1)}, bf16[2,4,64,384]{3,2,1,0:T(8,128)(2,1)S(1)}, u32[]{:S(2)}, u32[]{:S(2)}) collective-permute-start(bf16[2,4,64,384]{3,2,1,0:T(8,128)(2,1)S(1)} %collective-permute-done.6.refs_5_), channel_id=1, source_target_pairs={{0,8},{1,9},{64,72},{65,73},{2,10},{3,11},{66,74},{67,75},{4,12},{... | collective-permute-start | bytes 1179656 | tf_op jit(solution)/shard_map/ppermute | solution.py:30
  66.6 16.6 %copy-start.16 = (bf16[2,4,64,384]{3,2,1,0:T(8,128)(2,1)}, bf16[2,4,64,384]{3,2,1,0:T(8,128)(2,1)S(1)}, u32[]{:S(2)}) copy-start(bf16[2,4,64,384]{3,2,1,0:T(8,128)(2,1)S(1)} %collective-permute-done.3.refs_2_) | copy-start | bytes 1179652
  66.6 16.5 %collective-permute-start.4 = (bf16[2,4,64,384]{3,2,1,0:T(8,128)(2,1)S(1)}, bf16[2,4,64,384]{3,2,1,0:T(8,128)(2,1)S(1)}, u32[]{:S(2)}, u32[]{:S(2)}) collective-permute-start(bf16[2,4,64,384]{3,2,1,0:T(8,128)(2,1)S(1)} %collective-permute-done.3.refs_2_), channel_id=1, source_target_pairs={{0,56},{1,57},{64,120},{65,121},{2,58},{3,59},{66,122},{67,123},{4... | collective-permute-start | bytes 1179656 | tf_op jit(solution)/shard_map/ppermute | solution.py:30
  76.9 6.3 %copy-start.15 = (bf16[2,4,64,384]{3,2,1,0:T(8,128)(2,1)}, bf16[2,4,64,384]{3,2,1,0:T(8,128)(2,1)S(1)}, u32[]{:S(2)}) copy-start(bf16[2,4,64,384]{3,2,1,0:T(8,128)(2,1)S(1)} %collective-permute-done.7.refs_4_) | copy-start | bytes 1179652
  76.9 14.0 %collective-permute-start.8 = (bf16[2,4,64,384]{3,2,1,0:T(8,128)(2,1)S(1)}, bf16[2,4,64,384]{3,2,1,0:T(8,128)(2,1)S(1)}, u32[]{:S(2)}, u32[]{:S(2)}) collective-permute-start(bf16[2,4,64,384]{3,2,1,0:T(8,128)(2,1)S(1)} %collective-permute-done.7.refs_4_), channel_id=1, source_target_pairs={{0,8},{1,9},{64,72},{65,73},{2,10},{3,11},{66,74},{67,75},{4,12},{... | collective-permute-start | bytes 1179656 | tf_op jit(solution)/shard_map/ppermute | solution.py:30
  78.8 12.1 %collective-permute-start.9 = (bf16[32,384]{1,0:T(8,128)(2,1)S(1)}, bf16[32,384]{1,0:T(8,128)(2,1)S(1)}, u32[]{:S(2)}, u32[]{:S(2)}) collective-permute-start(bf16[32,384]{1,0:T(8,128)(2,1)S(1)} %get-tuple-element.26.up), channel_id=1, source_target_pairs={{0,1},{1,0},{64,65},{65,64},{2,3},{3,2},{66,67},{67,66},{4,5},{5,4... | collective-permute-start | bytes 73736 | tf_op jit(solution)/shard_map/ppermute | solution.py:30
  87.4 2.3 %copy-start = (bf16[4352,512]{1,0:T(8,128)(2,1)S(1)}, bf16[4352,512]{1,0:T(8,128)(2,1)}, u32[]{:S(2)}) copy-start(bf16[4352,512]{1,0:T(8,128)(2,1)} %all-gather.6.cloned.1.call-done) | copy-start | bytes 13369348
  89.7 2.3 %copy-start.1 = (bf16[4352,512]{1,0:T(8,128)(2,1)S(1)}, bf16[4352,512]{1,0:T(8,128)(2,1)}, u32[]{:S(2)}) copy-start(bf16[4352,512]{1,0:T(8,128)(2,1)} %all-gather.6.cloned.1.call-done) | copy-start | bytes 13369348
  89.7 10.1 %copy-start.18 = (bf16[512,64]{0,1:T(8,128)(2,1)S(1)}, bf16[512,64]{0,1:T(8,128)(2,1)}, u32[]{:S(2)}) copy-start(bf16[512,64]{0,1:T(8,128)(2,1)} %param.15) | copy-start | bytes 196612
  89.7 14.0 %copy-start.3 = (bf16[512,128]{1,0:T(8,128)(2,1)S(1)}, bf16[512,128]{1,0:T(8,128)(2,1)}, u32[]{:S(2)}) copy-start(bf16[512,128]{1,0:T(8,128)(2,1)} %filters_ref.5) | copy-start | bytes 393220
  89.7 23.5 %copy-start.9 = (s32[2,32]{1,0:T(2,128)S(1)}, s32[2,32]{1,0:T(2,128)}, u32[]{:S(2)}) copy-start(s32[2,32]{1,0:T(2,128)} %lengths.5) | copy-start | bytes 772
  91.9 1.9 %copy-start.2 = (bf16[3,2048,256]{2,1,0:T(8,128)(2,1)S(1)}, bf16[3,2048,256]{2,1,0:T(8,128)(2,1)}, u32[]{:S(2)}) copy-start(bf16[3,2048,256]{2,1,0:T(8,128)(2,1)} %pack_weights.1.packed) | copy-start | bytes 9437188
  97.8 3.8 %collective-permute-start.10 = (bf16[4,256,256]{2,1,0:T(8,128)(2,1)S(1)}, bf16[4,256,256]{2,1,0:T(8,128)(2,1)S(1)}, u32[]{:S(2)}, u32[]{:S(2)}) collective-permute-start(bf16[4,256,256]{2,1,0:T(8,128)(2,1)S(1)} %get-tuple-element.28), channel_id=1, source_target_pairs={{0,1},{1,0},{64,65},{65,64},{2,3},{3,2},{66,67},{67,66},{4,5},{5,4... | collective-permute-start | bytes 1572872 | tf_op jit(solution)/shard_map/ppermute | solution.py:30
  101.8 11.4 %collective-permute-start.12 = (bf16[4,2,128,128]{3,2,1,0:T(8,128)(2,1)S(1)}, bf16[4,2,128,128]{3,2,1,0:T(8,128)(2,1)S(1)}, u32[]{:S(2)}, u32[]{:S(2)}) collective-permute-start(bf16[4,2,128,128]{3,2,1,0:T(8,128)(2,1)S(1)} %combine_kv.1.kv_ref), channel_id=1, source_target_pairs={{0,8},{1,9},{64,72},{65,73},{2,10},{3,11},{66,74},{67,75},{4,12},{... | collective-permute-start | bytes 786440 | tf_op jit(solution)/shard_map/ppermute | solution.py:30
  106.2 3.4 %collective-permute-start.11 = (bf16[4,256,128]{2,1,0:T(8,128)(2,1)S(1)}, bf16[4,256,128]{2,1,0:T(8,128)(2,1)S(1)}, u32[]{:S(2)}, u32[]{:S(2)}) collective-permute-start(bf16[4,256,128]{2,1,0:T(8,128)(2,1)S(1)} %get-tuple-element.33), channel_id=1, source_target_pairs={{0,1},{1,0},{64,65},{65,64},{2,3},{3,2},{66,67},{67,66},{4,5},{5,4... | collective-permute-start | bytes 786440 | tf_op jit(solution)/shard_map/ppermute | solution.py:30
  108.3 8.2 %collective-permute-start.13 = (bf16[2,128,128]{2,1,0:T(8,128)(2,1)S(1)}, bf16[2,128,128]{2,1,0:T(8,128)(2,1)S(1)}, u32[]{:S(2)}, u32[]{:S(2)}) collective-permute-start(bf16[2,128,128]{2,1,0:T(8,128)(2,1)S(1)} %slice_bitcast_fusion), channel_id=1, source_target_pairs={{56,256},{57,257},{120,320},{121,321},{58,258},{59,259},{122,322},... | collective-permute-start | bytes 196616 | tf_op jit(solution)/shard_map/ppermute | solution.py:30
  153.7 1.2 copy-start.4
  (3 other events, 2.3 us)
Sparse Core Ops, SparseCore 0:
  16.8 68.1 all-gather.5
  101.9 34.3 all-gather.3

commit v7 on v6

--- a/solution.py
+++ b/solution.py
@@ -85,7 +85,7 @@
         place_rows(out_ref, held.at[i], lax.rem(position()[3] + dist, NY))
 
 
-def low_kernel(tokens, low_ref):
+def low_kernel(tokens, packed, low_ref):
     _, half, ranks = low_ref.shape
     row = lax.broadcasted_iota(jnp.int32, (half, ranks), 0)
     column = lax.broadcasted_iota(jnp.int32, (half, ranks), 1)
@@ -381,7 +381,7 @@
         vmem=56,
         where=NY - 1,
     )
-    low = call(low_kernel, "low_rank", jax.ShapeDtypeStruct((*cut, ranks), bf16), (gathered,))
+    low = call(low_kernel, "low_rank", jax.ShapeDtypeStruct((*cut, ranks), bf16), (gathered, packed))
     kv_own, kv_send, q_own, q_send = call(
         project_kernel,
         "project",

time: 164 us -> 164 us (level)
  no operation moved by 1% of the time
where the time goes in v7:
time: 164 us; the launch traced here: 163 us
  blocking collectives  50.2 us (31%)
  starting transfers between devices  41.5 us (25%)
  waiting for transfers between devices  26.1 us (16%)
  Pallas kernels  19.2 us (12%)
  between operations  13.8 us (8%)
  local copies, waits for them, and re-layouts  11.2 us (7%)
    ppermute x14, starting transfers between devices, permute(): return lax.ppermute(value, AXES, pairs)  41.4 us
    ppermute x14, waiting for transfers between devices, permute(): return lax.ppermute(value, AXES, pairs)  26.1 us
    all_to_all x1, blocking collectives, local(): met = lax.all_to_all(total.reshape(64, 8, ch), rest, 0, 0, tiled=True)  22.5 us
    pallas_call x13, Pallas kernels, call(): pl.pallas_call(kernel, out_shape=out, in_specs=[SMEM] * scalars + [ANY] *...  19.2 us
    all_to_all x1, blocking collectives, local(): met = lax.all_to_all(spread, ('xhi', 'xlo', 'zlo'), 0, 0, tiled=True)  14.6 us
    all_to_all x1, blocking collectives, local(): met = lax.all_to_all(total, 'y', 0, 0, tiled=True)  13.2 us
    unnamed x38, local copies, waits for them, and re-layouts  11.2 us
  transfers between devices with their start and end apart: 16, of which 7 were waited for; matrix products, arithmetic and copies ran while one was open for 0% of the time, Pallas kernels for 8%

profile of v7, /device:TPU:1, one launch (start us, length us, event | category | flops | bytes accessed | tf_op | source)
XLA Modules:
  0.0 162.8 jit_solution(9138743439674504388)
XLA Ops:
  6.5 3.9 %collective-permute-start = (bf16[256,512]{1,0:T(8,128)(2,1)}, bf16[256,512]{1,0:T(8,128)(2,1)S(1)}, u32[]{:S(2)}, u32[]{:S(2)}) collective-permute-start(bf16[256,512]{1,0:T(8,128)(2,1)} %bitcast.19), channel_id=1, source_target_pairs={{0,128},{1,129},{64,192},{65,193},{2,130},{3,131},{66,194},{67,195... | collective-permute-start | bytes 786440 | tf_op jit(solution)/shard_map/ppermute | solution.py:30
  16.7 14.6 %all_to_all.15.met_ref = bf16[8,64,384]{2,1,0:T(8,128)(2,1)S(1)} all-to-all(bf16[8,64,384]{2,1,0:T(8,128)(2,1)S(1)} %spread_weight.1), channel_id=1, replica_groups=mesh['xhi'=2,'xlo'=2,'zlo'=2,'y'=8,'zhi'=4,'core'=2] {'xhi','xlo','zlo'}, dimensions={0} | all-to-all | bytes 786432 | tf_op jit(solution)/shard_map/all_to_all | solution.py:362
  31.3 5.0 %collective-permute-start.1 = (bf16[4,64,384]{2,1,0:T(8,128)(2,1)S(1)}, bf16[4,64,384]{2,1,0:T(8,128)(2,1)S(1)}, u32[]{:S(2)}, u32[]{:S(2)}) collective-permute-start(bf16[4,64,384]{2,1,0:T(8,128)(2,1)S(1)} %get-tuple-element.25), channel_id=1, source_target_pairs={{0,1},{1,0},{64,65},{65,64},{2,3},{3,2},{66,67},{67,66},{4,5},{5,4... | collective-permute-start | bytes 589832 | tf_op jit(solution)/shard_map/ppermute | solution.py:30
  36.3 1.0 collective-permute-done.1
  37.4 3.0 %collective-permute-start.5 = (bf16[2,4,64,384]{3,2,1,0:T(8,128)(2,1)S(1)}, bf16[2,4,64,384]{3,2,1,0:T(8,128)(2,1)S(1)}, u32[]{:S(2)}, u32[]{:S(2)}) collective-permute-start(bf16[2,4,64,384]{3,2,1,0:T(8,128)(2,1)S(1)} %pad_maximum_fusion.refs_0_), channel_id=1, source_target_pairs={{0,8},{1,9},{64,72},{65,73},{2,10},{3,11},{66,74},{67,75},{4,12},{... | collective-permute-start | bytes 1179656 | tf_op jit(solution)/shard_map/ppermute | solution.py:30
  40.4 3.8 %collective-permute-start.2 = (bf16[2,4,64,384]{3,2,1,0:T(8,128)(2,1)S(1)}, bf16[2,4,64,384]{3,2,1,0:T(8,128)(2,1)S(1)}, u32[]{:S(2)}, u32[]{:S(2)}) collective-permute-start(bf16[2,4,64,384]{3,2,1,0:T(8,128)(2,1)S(1)} %pad_maximum_fusion.refs_0_), channel_id=1, source_target_pairs={{0,56},{1,57},{64,120},{65,121},{2,58},{3,59},{66,122},{67,123},{4... | collective-permute-start | bytes 1179656 | tf_op jit(solution)/shard_map/ppermute | solution.py:30
  44.2 7.3 %collective-permute-done.5.refs_6_ = bf16[2,4,64,384]{3,2,1,0:T(8,128)(2,1)S(1)} collective-permute-done((bf16[2,4,64,384]{3,2,1,0:T(8,128)(2,1)S(1)}, bf16[2,4,64,384]{3,2,1,0:T(8,128)(2,1)S(1)}, u32[]{:S(2)}, u32[]{:S(2)}) %collective-permute-start.5) | collective-permute-done | bytes 393248 | tf_op jit(solution)/shard_map/ppermute | solution.py:30
  51.6 1.9 %collective-permute-start.6 = (bf16[2,4,64,384]{3,2,1,0:T(8,128)(2,1)S(1)}, bf16[2,4,64,384]{3,2,1,0:T(8,128)(2,1)S(1)}, u32[]{:S(2)}, u32[]{:S(2)}) collective-permute-start(bf16[2,4,64,384]{3,2,1,0:T(8,128)(2,1)S(1)} %collective-permute-done.5.refs_6_), channel_id=1, source_target_pairs={{0,8},{1,9},{64,72},{65,73},{2,10},{3,11},{66,74},{67,75},{4,12},{... | collective-permute-start | bytes 1179656 | tf_op jit(solution)/shard_map/ppermute | solution.py:30
  53.5 4.6 %collective-permute-start.3 = (bf16[2,4,64,384]{3,2,1,0:T(8,128)(2,1)S(1)}, bf16[2,4,64,384]{3,2,1,0:T(8,128)(2,1)S(1)}, u32[]{:S(2)}, u32[]{:S(2)}) collective-permute-start(bf16[2,4,64,384]{3,2,1,0:T(8,128)(2,1)S(1)} %collective-permute-done.2.refs_1_), channel_id=1, source_target_pairs={{0,56},{1,57},{64,120},{65,121},{2,58},{3,59},{66,122},{67,123},{4... | collective-permute-start | bytes 1179656 | tf_op jit(solution)/shard_map/ppermute | solution.py:30
  58.1 6.5 %collective-permute-done.6.refs_5_ = bf16[2,4,64,384]{3,2,1,0:T(8,128)(2,1)S(1)} collective-permute-done((bf16[2,4,64,384]{3,2,1,0:T(8,128)(2,1)S(1)}, bf16[2,4,64,384]{3,2,1,0:T(8,128)(2,1)S(1)}, u32[]{:S(2)}, u32[]{:S(2)}) %collective-permute-start.6) | collective-permute-done | bytes 393248 | tf_op jit(solution)/shard_map/ppermute | solution.py:30
  64.6 1.9 %collective-permute-start.7 = (bf16[2,4,64,384]{3,2,1,0:T(8,128)(2,1)S(1)}, bf16[2,4,64,384]{3,2,1,0:T(8,128)(2,1)S(1)}, u32[]{:S(2)}, u32[]{:S(2)}) collective-permute-start(bf16[2,4,64,384]{3,2,1,0:T(8,128)(2,1)S(1)} %collective-permute-done.6.refs_5_), channel_id=1, source_target_pairs={{0,8},{1,9},{64,72},{65,73},{2,10},{3,11},{66,74},{67,75},{4,12},{... | collective-permute-start | bytes 1179656 | tf_op jit(solution)/shard_map/ppermute | solution.py:30
  66.6 4.6 %collective-permute-start.4 = (bf16[2,4,64,384]{3,2,1,0:T(8,128)(2,1)S(1)}, bf16[2,4,64,384]{3,2,1,0:T(8,128)(2,1)S(1)}, u32[]{:S(2)}, u32[]{:S(2)}) collective-permute-start(bf16[2,4,64,384]{3,2,1,0:T(8,128)(2,1)S(1)} %collective-permute-done.3.refs_2_), channel_id=1, source_target_pairs={{0,56},{1,57},{64,120},{65,121},{2,58},{3,59},{66,122},{67,123},{4... | collective-permute-start | bytes 1179656 | tf_op jit(solution)/shard_map/ppermute | solution.py:30
  71.2 5.7 %collective-permute-done.7.refs_4_ = bf16[2,4,64,384]{3,2,1,0:T(8,128)(2,1)S(1)} collective-permute-done((bf16[2,4,64,384]{3,2,1,0:T(8,128)(2,1)S(1)}, bf16[2,4,64,384]{3,2,1,0:T(8,128)(2,1)S(1)}, u32[]{:S(2)}, u32[]{:S(2)}) %collective-permute-start.7) | collective-permute-done | bytes 393248 | tf_op jit(solution)/shard_map/ppermute | solution.py:30
  76.9 1.9 %collective-permute-start.8 = (bf16[2,4,64,384]{3,2,1,0:T(8,128)(2,1)S(1)}, bf16[2,4,64,384]{3,2,1,0:T(8,128)(2,1)S(1)}, u32[]{:S(2)}, u32[]{:S(2)}) collective-permute-start(bf16[2,4,64,384]{3,2,1,0:T(8,128)(2,1)S(1)} %collective-permute-done.7.refs_4_), channel_id=1, source_target_pairs={{0,8},{1,9},{64,72},{65,73},{2,10},{3,11},{66,74},{67,75},{4,12},{... | collective-permute-start | bytes 1179656 | tf_op jit(solution)/shard_map/ppermute | solution.py:30
  78.8 4.3 %collective-permute-start.9 = (bf16[32,384]{1,0:T(8,128)(2,1)S(1)}, bf16[32,384]{1,0:T(8,128)(2,1)S(1)}, u32[]{:S(2)}, u32[]{:S(2)}) collective-permute-start(bf16[32,384]{1,0:T(8,128)(2,1)S(1)} %get-tuple-element.26.up), channel_id=1, source_target_pairs={{0,1},{1,0},{64,65},{65,64},{2,3},{3,2},{66,67},{67,66},{4,5},{5,4... | collective-permute-start | bytes 73736 | tf_op jit(solution)/shard_map/ppermute | solution.py:30
  83.9 3.5 %pack_weights.1.packed = bf16[3,2048,256]{2,1,0:T(8,128)(2,1)} custom-call(bf16[2,4,64,384]{3,2,1,0:T(8,128)(2,1)} %copy-done.11, bf16[2,4,64,384]{3,2,1,0:T(8,128)(2,1)} %copy-done.13, bf16[2,4,64,384]{3,2,1,0:T(8,128)(2,1)} %copy-done.16, bf16[2,4,64,384]{3,2,1,0:T(8,128)(2,1)} %copy-done.17, bf16[2,4,64,384]{3,2,1,0:T(8,128)(2,1)} %copy-done.15, ...), custom_call_target="tpu_custom_call" | custom-call | tf_op jit(solution)/shard_map/pack_weights/pallas_call | solution.py:317
  87.4 1.9 %copy-done = bf16[3,2048,256]{2,1,0:T(8,128)(2,1)S(1)} copy-done((bf16[3,2048,256]{2,1,0:T(8,128)(2,1)S(1)}, bf16[3,2048,256]{2,1,0:T(8,128)(2,1)}, u32[]{:S(2)}) %copy-start) | copy-done | bytes 3145752
  89.3 2.3 %copy-done.2 = bf16[4352,512]{1,0:T(8,128)(2,1)S(1)} copy-done((bf16[4352,512]{1,0:T(8,128)(2,1)S(1)}, bf16[4352,512]{1,0:T(8,128)(2,1)}, u32[]{:S(2)}) %copy-start.2) | copy-done | bytes 4456472
  91.6 1.2 low_rank.1.low_ref
  93.5 4.0 %project.1 = (f32[4,256,256]{2,1,0:T(8,128)S(1)}, bf16[4,256,256]{2,1,0:T(8,128)(2,1)S(1)}, f32[4,256,128]{2,1,0:T(8,128)S(1)}, bf16[4,256,128]{2,1,0:T(8,128)(2,1)S(1)}) custom-call(bf16[8,544,512]{2,1,0:T(8,128)(2,1)S(1)} %bitcast.15, bf16[3,2048,256]{2,1,0:T(8,128)(2,1)S(1)} %copy-done.1, bf16[2,4,64,384]{3,2,1,0:T(8,128)(2,1)S(1)} %collective-permute-done.8.last, ...), custom_call_target="tpu_custom_call" | custom-call | tf_op jit(solution)/shard_map/project/pallas_call | solution.py:317
  97.5 1.9 %collective-permute-start.10 = (bf16[4,256,256]{2,1,0:T(8,128)(2,1)S(1)}, bf16[4,256,256]{2,1,0:T(8,128)(2,1)S(1)}, u32[]{:S(2)}, u32[]{:S(2)}) collective-permute-start(bf16[4,256,256]{2,1,0:T(8,128)(2,1)S(1)} %get-tuple-element.28), channel_id=1, source_target_pairs={{0,1},{1,0},{64,65},{65,64},{2,3},{3,2},{66,67},{67,66},{4,5},{5,4... | collective-permute-start | bytes 1572872 | tf_op jit(solution)/shard_map/ppermute | solution.py:30
  100.1 1.2 collective-permute-done.10.met_ref
  101.4 1.9 %collective-permute-start.12 = (bf16[4,2,128,128]{3,2,1,0:T(8,128)(2,1)S(1)}, bf16[4,2,128,128]{3,2,1,0:T(8,128)(2,1)S(1)}, u32[]{:S(2)}, u32[]{:S(2)}) collective-permute-start(bf16[4,2,128,128]{3,2,1,0:T(8,128)(2,1)S(1)} %combine_kv.1.kv_ref), channel_id=1, source_target_pairs={{0,8},{1,9},{64,72},{65,73},{2,10},{3,11},{66,74},{67,75},{4,12},{... | collective-permute-start | bytes 786440 | tf_op jit(solution)/shard_map/ppermute | solution.py:30
  103.3 2.5 %conv_own.1.part_ref = f32[4,2,128,128]{3,2,1,0:T(8,128)S(1)} custom-call(bf16[4,2,128,128]{3,2,1,0:T(8,128)(2,1)S(1)} %combine_kv.1.kv_ref, bf16[512,128]{1,0:T(8,128)(2,1)S(1)} %copy-done.3), custom_call_target="tpu_custom_call" | custom-call | tf_op jit(solution)/shard_map/conv_own/pallas_call | solution.py:317
  105.8 2.0 %collective-permute-start.11 = (bf16[4,256,128]{2,1,0:T(8,128)(2,1)S(1)}, bf16[4,256,128]{2,1,0:T(8,128)(2,1)S(1)}, u32[]{:S(2)}, u32[]{:S(2)}) collective-permute-start(bf16[4,256,128]{2,1,0:T(8,128)(2,1)S(1)} %get-tuple-element.33), channel_id=1, source_target_pairs={{0,1},{1,0},{64,65},{65,64},{2,3},{3,2},{66,67},{67,66},{4,5},{5,4... | collective-permute-start | bytes 786440 | tf_op jit(solution)/shard_map/ppermute | solution.py:30
  109.3 3.5 %collective-permute-done.12.prev_ref = bf16[4,2,128,128]{3,2,1,0:T(8,128)(2,1)S(1)} collective-permute-done((bf16[4,2,128,128]{3,2,1,0:T(8,128)(2,1)S(1)}, bf16[4,2,128,128]{3,2,1,0:T(8,128)(2,1)S(1)}, u32[]{:S(2)}, u32[]{:S(2)}) %collective-permute-start.12) | collective-permute-done | bytes 262176 | tf_op jit(solution)/shard_map/ppermute | solution.py:30
  112.8 3.3 %gate_most.1.most_ref = f32[64,128]{1,0:T(8,128)S(1)} custom-call(s32[2,32]{1,0:T(2,128)S(1)} %copy-done.9, f32[4,2,128,128]{3,2,1,0:T(8,128)S(1)} %conv_own.1.part_ref, f32[4,256,128]{2,1,0:T(8,128)S(1)} %get-tuple-element.32.own_ref, bf16[4,256,128]{2,1,0:T(8,128)(2,1)S(1)} %collective-permute-done.11.met_ref, ...), custom_call_target="tpu_custom_call" | custom-call | tf_op jit(solution)/shard_map/gate_most/pallas_call | solution.py:317
  116.1 1.5 gate_first.1
  117.6 13.2 %all_to_all.16.met_ref = bf16[8,64,128]{2,1,0:T(8,128)(2,1)S(1)} all-to-all(bf16[8,64,128]{2,1,0:T(8,128)(2,1)S(1)} %gate_first.1), channel_id=1, replica_groups=mesh['xhi'=2,'xlo'=2,'zlo'=2,'y'=8,'zhi'=4,'core'=2] {'y'}, dimensions={0} | all-to-all | bytes 262144 | tf_op jit(solution)/shard_map/all_to_all | solution.py:438
  130.8 22.5 %all_to_all.17 = bf16[64,8,128]{2,1,0:T(8,128)(2,1)S(1)} all-to-all(bf16[64,8,128]{2,1,0:T(8,128)(2,1)S(1)} %bitcast.16), channel_id=1, replica_groups=mesh['xhi'=2,'xlo'=2,'zlo'=2,'y'=8,'zhi'=4,'core'=2] {'zhi','core','xhi'..., dimensions={0} | all-to-all | bytes 262144 | tf_op jit(solution)/shard_map/all_to_all | solution.py:441
  153.3 1.2 copy-done.4
  154.5 1.4 embed.1
  (59 shorter events, 9.8 us)
Async XLA Ops:
  6.5 80.9 %all-gather.6.cloned.1.call-start = ((), (), s32[]{:S(2)}) async-start(), calls=%async_computation.4 | async-start | bytes 5013504 | tf_op jit(solution)/shard_map/all_gather | solution.py:359
  6.5 8.2 %collective-permute-start = (bf16[256,512]{1,0:T(8,128)(2,1)}, bf16[256,512]{1,0:T(8,128)(2,1)S(1)}, u32[]{:S(2)}, u32[]{:S(2)}) collective-permute-start(bf16[256,512]{1,0:T(8,128)(2,1)} %bitcast.19), channel_id=1, source_target_pairs={{0,128},{1,129},{64,192},{65,193},{2,130},{3,131},{66,194},{67,195... | collective-permute-start | bytes 786440 | tf_op jit(solution)/shard_map/ppermute | solution.py:30
  10.5 0.9 copy-start.7
  11.5 1.0 copy-start.5
  14.7 1.0 copy-start.6
  16.6 136.7 %all-gather.4.cloned.1.call-start = ((), (), s32[]{:S(2)}) async-start(), calls=%async_computation.3 | async-start | bytes 1179648 | tf_op jit(solution)/shard_map/all_gather | solution.py:404
  31.3 6.0 %collective-permute-start.1 = (bf16[4,64,384]{2,1,0:T(8,128)(2,1)S(1)}, bf16[4,64,384]{2,1,0:T(8,128)(2,1)S(1)}, u32[]{:S(2)}, u32[]{:S(2)}) collective-permute-start(bf16[4,64,384]{2,1,0:T(8,128)(2,1)S(1)} %get-tuple-element.25), channel_id=1, source_target_pairs={{0,1},{1,0},{64,65},{65,64},{2,3},{3,2},{66,67},{67,66},{4,5},{5,4... | collective-permute-start | bytes 589832 | tf_op jit(solution)/shard_map/ppermute | solution.py:30
  37.4 45.7 %copy-start.11 = (bf16[2,4,64,384]{3,2,1,0:T(8,128)(2,1)}, bf16[2,4,64,384]{3,2,1,0:T(8,128)(2,1)S(1)}, u32[]{:S(2)}) copy-start(bf16[2,4,64,384]{3,2,1,0:T(8,128)(2,1)S(1)} %pad_maximum_fusion.refs_0_) | copy-start | bytes 1179652
  37.4 14.2 %collective-permute-start.5 = (bf16[2,4,64,384]{3,2,1,0:T(8,128)(2,1)S(1)}, bf16[2,4,64,384]{3,2,1,0:T(8,128)(2,1)S(1)}, u32[]{:S(2)}, u32[]{:S(2)}) collective-permute-start(bf16[2,4,64,384]{3,2,1,0:T(8,128)(2,1)S(1)} %pad_maximum_fusion.refs_0_), channel_id=1, source_target_pairs={{0,8},{1,9},{64,72},{65,73},{2,10},{3,11},{66,74},{67,75},{4,12},{... | collective-permute-start | bytes 1179656 | tf_op jit(solution)/shard_map/ppermute | solution.py:30
  40.4 13.1 %collective-permute-start.2 = (bf16[2,4,64,384]{3,2,1,0:T(8,128)(2,1)S(1)}, bf16[2,4,64,384]{3,2,1,0:T(8,128)(2,1)S(1)}, u32[]{:S(2)}, u32[]{:S(2)}) collective-permute-start(bf16[2,4,64,384]{3,2,1,0:T(8,128)(2,1)S(1)} %pad_maximum_fusion.refs_0_), channel_id=1, source_target_pairs={{0,56},{1,57},{64,120},{65,121},{2,58},{3,59},{66,122},{67,123},{4... | collective-permute-start | bytes 1179656 | tf_op jit(solution)/shard_map/ppermute | solution.py:30
  51.6 31.5 %copy-start.12 = (bf16[2,4,64,384]{3,2,1,0:T(8,128)(2,1)}, bf16[2,4,64,384]{3,2,1,0:T(8,128)(2,1)S(1)}, u32[]{:S(2)}) copy-start(bf16[2,4,64,384]{3,2,1,0:T(8,128)(2,1)S(1)} %collective-permute-done.5.refs_6_) | copy-start | bytes 1179652
  51.6 13.1 %collective-permute-start.6 = (bf16[2,4,64,384]{3,2,1,0:T(8,128)(2,1)S(1)}, bf16[2,4,64,384]{3,2,1,0:T(8,128)(2,1)S(1)}, u32[]{:S(2)}, u32[]{:S(2)}) collective-permute-start(bf16[2,4,64,384]{3,2,1,0:T(8,128)(2,1)S(1)} %collective-permute-done.5.refs_6_), channel_id=1, source_target_pairs={{0,8},{1,9},{64,72},{65,73},{2,10},{3,11},{66,74},{67,75},{4,12},{... | collective-permute-start | bytes 1179656 | tf_op jit(solution)/shard_map/ppermute | solution.py:30
  53.5 29.6 %copy-start.13 = (bf16[2,4,64,384]{3,2,1,0:T(8,128)(2,1)}, bf16[2,4,64,384]{3,2,1,0:T(8,128)(2,1)S(1)}, u32[]{:S(2)}) copy-start(bf16[2,4,64,384]{3,2,1,0:T(8,128)(2,1)S(1)} %collective-permute-done.2.refs_1_) | copy-start | bytes 1179652
  53.5 13.0 %collective-permute-start.3 = (bf16[2,4,64,384]{3,2,1,0:T(8,128)(2,1)S(1)}, bf16[2,4,64,384]{3,2,1,0:T(8,128)(2,1)S(1)}, u32[]{:S(2)}, u32[]{:S(2)}) collective-permute-start(bf16[2,4,64,384]{3,2,1,0:T(8,128)(2,1)S(1)} %collective-permute-done.2.refs_1_), channel_id=1, source_target_pairs={{0,56},{1,57},{64,120},{65,121},{2,58},{3,59},{66,122},{67,123},{4... | collective-permute-start | bytes 1179656 | tf_op jit(solution)/shard_map/ppermute | solution.py:30
  64.6 18.5 %copy-start.14 = (bf16[2,4,64,384]{3,2,1,0:T(8,128)(2,1)}, bf16[2,4,64,384]{3,2,1,0:T(8,128)(2,1)S(1)}, u32[]{:S(2)}) copy-start(bf16[2,4,64,384]{3,2,1,0:T(8,128)(2,1)S(1)} %collective-permute-done.6.refs_5_) | copy-start | bytes 1179652
  64.6 12.2 %collective-permute-start.7 = (bf16[2,4,64,384]{3,2,1,0:T(8,128)(2,1)S(1)}, bf16[2,4,64,384]{3,2,1,0:T(8,128)(2,1)S(1)}, u32[]{:S(2)}, u32[]{:S(2)}) collective-permute-start(bf16[2,4,64,384]{3,2,1,0:T(8,128)(2,1)S(1)} %collective-permute-done.6.refs_5_), channel_id=1, source_target_pairs={{0,8},{1,9},{64,72},{65,73},{2,10},{3,11},{66,74},{67,75},{4,12},{... | collective-permute-start | bytes 1179656 | tf_op jit(solution)/shard_map/ppermute | solution.py:30
  66.6 16.6 %copy-start.16 = (bf16[2,4,64,384]{3,2,1,0:T(8,128)(2,1)}, bf16[2,4,64,384]{3,2,1,0:T(8,128)(2,1)S(1)}, u32[]{:S(2)}) copy-start(bf16[2,4,64,384]{3,2,1,0:T(8,128)(2,1)S(1)} %collective-permute-done.3.refs_2_) | copy-start | bytes 1179652
  66.6 16.5 %collective-permute-start.4 = (bf16[2,4,64,384]{3,2,1,0:T(8,128)(2,1)S(1)}, bf16[2,4,64,384]{3,2,1,0:T(8,128)(2,1)S(1)}, u32[]{:S(2)}, u32[]{:S(2)}) collective-permute-start(bf16[2,4,64,384]{3,2,1,0:T(8,128)(2,1)S(1)} %collective-permute-done.3.refs_2_), channel_id=1, source_target_pairs={{0,56},{1,57},{64,120},{65,121},{2,58},{3,59},{66,122},{67,123},{4... | collective-permute-start | bytes 1179656 | tf_op jit(solution)/shard_map/ppermute | solution.py:30
  76.9 6.3 %copy-start.15 = (bf16[2,4,64,384]{3,2,1,0:T(8,128)(2,1)}, bf16[2,4,64,384]{3,2,1,0:T(8,128)(2,1)S(1)}, u32[]{:S(2)}) copy-start(bf16[2,4,64,384]{3,2,1,0:T(8,128)(2,1)S(1)} %collective-permute-done.7.refs_4_) | copy-start | bytes 1179652
  76.9 15.9 %collective-permute-start.8 = (bf16[2,4,64,384]{3,2,1,0:T(8,128)(2,1)S(1)}, bf16[2,4,64,384]{3,2,1,0:T(8,128)(2,1)S(1)}, u32[]{:S(2)}, u32[]{:S(2)}) collective-permute-start(bf16[2,4,64,384]{3,2,1,0:T(8,128)(2,1)S(1)} %collective-permute-done.7.refs_4_), channel_id=1, source_target_pairs={{0,8},{1,9},{64,72},{65,73},{2,10},{3,11},{66,74},{67,75},{4,12},{... | collective-permute-start | bytes 1179656 | tf_op jit(solution)/shard_map/ppermute | solution.py:30
  78.8 14.0 %collective-permute-start.9 = (bf16[32,384]{1,0:T(8,128)(2,1)S(1)}, bf16[32,384]{1,0:T(8,128)(2,1)S(1)}, u32[]{:S(2)}, u32[]{:S(2)}) collective-permute-start(bf16[32,384]{1,0:T(8,128)(2,1)S(1)} %get-tuple-element.26.up), channel_id=1, source_target_pairs={{0,1},{1,0},{64,65},{65,64},{2,3},{3,2},{66,67},{67,66},{4,5},{5,4... | collective-permute-start | bytes 73736 | tf_op jit(solution)/shard_map/ppermute | solution.py:30
  87.4 1.9 %copy-start = (bf16[3,2048,256]{2,1,0:T(8,128)(2,1)S(1)}, bf16[3,2048,256]{2,1,0:T(8,128)(2,1)}, u32[]{:S(2)}) copy-start(bf16[3,2048,256]{2,1,0:T(8,128)(2,1)} %pack_weights.1.packed) | copy-start | bytes 9437188
  89.3 2.3 %copy-start.2 = (bf16[4352,512]{1,0:T(8,128)(2,1)S(1)}, bf16[4352,512]{1,0:T(8,128)(2,1)}, u32[]{:S(2)}) copy-start(bf16[4352,512]{1,0:T(8,128)(2,1)} %all-gather.6.cloned.1.call-done) | copy-start | bytes 13369348
  91.6 1.9 %copy-start.1 = (bf16[3,2048,256]{2,1,0:T(8,128)(2,1)S(1)}, bf16[3,2048,256]{2,1,0:T(8,128)(2,1)}, u32[]{:S(2)}) copy-start(bf16[3,2048,256]{2,1,0:T(8,128)(2,1)} %pack_weights.1.packed) | copy-start | bytes 9437188
  92.8 6.6 %copy-start.18 = (bf16[512,64]{0,1:T(8,128)(2,1)S(1)}, bf16[512,64]{0,1:T(8,128)(2,1)}, u32[]{:S(2)}) copy-start(bf16[512,64]{0,1:T(8,128)(2,1)} %param.15) | copy-start | bytes 196612
  92.8 10.5 %copy-start.3 = (bf16[512,128]{1,0:T(8,128)(2,1)S(1)}, bf16[512,128]{1,0:T(8,128)(2,1)}, u32[]{:S(2)}) copy-start(bf16[512,128]{1,0:T(8,128)(2,1)} %filters_ref.5) | copy-start | bytes 393220
  92.8 20.0 %copy-start.9 = (s32[2,32]{1,0:T(2,128)S(1)}, s32[2,32]{1,0:T(2,128)}, u32[]{:S(2)}) copy-start(s32[2,32]{1,0:T(2,128)} %lengths.5) | copy-start | bytes 772
  97.5 3.8 %collective-permute-start.10 = (bf16[4,256,256]{2,1,0:T(8,128)(2,1)S(1)}, bf16[4,256,256]{2,1,0:T(8,128)(2,1)S(1)}, u32[]{:S(2)}, u32[]{:S(2)}) collective-permute-start(bf16[4,256,256]{2,1,0:T(8,128)(2,1)S(1)} %get-tuple-element.28), channel_id=1, source_target_pairs={{0,1},{1,0},{64,65},{65,64},{2,3},{3,2},{66,67},{67,66},{4,5},{5,4... | collective-permute-start | bytes 1572872 | tf_op jit(solution)/shard_map/ppermute | solution.py:30
  101.4 11.4 %collective-permute-start.12 = (bf16[4,2,128,128]{3,2,1,0:T(8,128)(2,1)S(1)}, bf16[4,2,128,128]{3,2,1,0:T(8,128)(2,1)S(1)}, u32[]{:S(2)}, u32[]{:S(2)}) collective-permute-start(bf16[4,2,128,128]{3,2,1,0:T(8,128)(2,1)S(1)} %combine_kv.1.kv_ref), channel_id=1, source_target_pairs={{0,8},{1,9},{64,72},{65,73},{2,10},{3,11},{66,74},{67,75},{4,12},{... | collective-permute-start | bytes 786440 | tf_op jit(solution)/shard_map/ppermute | solution.py:30
  105.8 3.4 %collective-permute-start.11 = (bf16[4,256,128]{2,1,0:T(8,128)(2,1)S(1)}, bf16[4,256,128]{2,1,0:T(8,128)(2,1)S(1)}, u32[]{:S(2)}, u32[]{:S(2)}) collective-permute-start(bf16[4,256,128]{2,1,0:T(8,128)(2,1)S(1)} %get-tuple-element.33), channel_id=1, source_target_pairs={{0,1},{1,0},{64,65},{65,64},{2,3},{3,2},{66,67},{67,66},{4,5},{5,4... | collective-permute-start | bytes 786440 | tf_op jit(solution)/shard_map/ppermute | solution.py:30
  107.9 8.2 %collective-permute-start.13 = (bf16[2,128,128]{2,1,0:T(8,128)(2,1)S(1)}, bf16[2,128,128]{2,1,0:T(8,128)(2,1)S(1)}, u32[]{:S(2)}, u32[]{:S(2)}) collective-permute-start(bf16[2,128,128]{2,1,0:T(8,128)(2,1)S(1)} %slice_bitcast_fusion), channel_id=1, source_target_pairs={{56,256},{57,257},{120,320},{121,321},{58,258},{59,259},{122,322},... | collective-permute-start | bytes 196616 | tf_op jit(solution)/shard_map/ppermute | solution.py:30
  153.3 1.2 copy-start.4
  (3 other events, 2.3 us)
Sparse Core Ops, SparseCore 0:
  16.8 68.1 all-gather.5
  101.5 34.3 all-gather.3

commit v8 on v6

--- a/solution.py
+++ b/solution.py
@@ -158,7 +158,8 @@
         given_ref[block] = met_ref[2 * block + 1 - core]
 
 
-def spread_kernel(weight_ref, out_ref):
+def spread_kernel(weight_ref, own_ref, out_ref, rows_ref):
+    rows_ref[...] = own_ref[...]
     ch = out_ref.shape[2] // 3
     for quarter in range(4):
         for stream in range(3):
@@ -346,15 +347,15 @@
     )
     own = tokens.reshape(half, depth)
     other = x_pair_swap(own)
-    spread = call(
+    spread, own_rows = call(
         spread_kernel,
         "spread_weight",
-        jax.ShapeDtypeStruct((8, w_rows, 3 * ch), bf16),
-        (in_weight.transpose(1, 0, 2),),
-    )
-    spread, other = lax.optimization_barrier((spread, other))
+        (jax.ShapeDtypeStruct((8, w_rows, 3 * ch), bf16), jax.ShapeDtypeStruct(own.shape, bf16)),
+        (in_weight.transpose(1, 0, 2), own),
+    )
+    spread, own_rows, other = lax.optimization_barrier((spread, own_rows, other))
     piece = call(
-        join_kernel, "join_rows", jax.ShapeDtypeStruct((2 * half + ranks, depth), bf16), (own, other, down)
+        join_kernel, "join_rows", jax.ShapeDtypeStruct((2 * half + ranks, depth), bf16), (own_rows, other, down)
     )
     gathered = lax.all_gather(piece, ("zhi", "zlo"), axis=0, tiled=False)
 

time: 164 us -> 163 us (level)
  no operation moved by 1% of the time
where the time goes in v8:
time: 163 us; the launch traced here: 162 us
  blocking collectives  49.3 us (30%)
  starting transfers between devices  41.5 us (25%)
  waiting for transfers between devices  26.1 us (16%)
  Pallas kernels  19.3 us (12%)
  between operations  13.8 us (8%)
  local copies, waits for them, and re-layouts  11.6 us (7%)
    ppermute x14, starting transfers between devices, permute(): return lax.ppermute(value, AXES, pairs)  41.4 us
    ppermute x14, waiting for transfers between devices, permute(): return lax.ppermute(value, AXES, pairs)  26.1 us
    all_to_all x1, blocking collectives, local(): met = lax.all_to_all(total.reshape(64, 8, ch), rest, 0, 0, tiled=True)  22.5 us
    pallas_call x13, Pallas kernels, call(): pl.pallas_call(kernel, out_shape=out, in_specs=[SMEM] * scalars + [ANY] *...  19.3 us
    all_to_all x1, blocking collectives, local(): met = lax.all_to_all(spread, ('xhi', 'xlo', 'zlo'), 0, 0, tiled=True)  13.6 us
    all_to_all x1, blocking collectives, local(): met = lax.all_to_all(total, 'y', 0, 0, tiled=True)  13.2 us
    unnamed x38, local copies, waits for them, and re-layouts  11.6 us
  transfers between devices with their start and end apart: 16, of which 7 were waited for; matrix products, arithmetic and copies ran while one was open for 0% of the time, Pallas kernels for 8%

profile of v8, /device:TPU:1, one launch (start us, length us, event | category | flops | bytes accessed | tf_op | source)
XLA Modules:
  0.0 162.2 jit_solution(6634446398881186401)
XLA Ops:
  6.5 3.9 %collective-permute-start = (bf16[256,512]{1,0:T(8,128)(2,1)}, bf16[256,512]{1,0:T(8,128)(2,1)S(1)}, u32[]{:S(2)}, u32[]{:S(2)}) collective-permute-start(bf16[256,512]{1,0:T(8,128)(2,1)} %bitcast.19), channel_id=1, source_target_pairs={{0,128},{1,129},{64,192},{65,193},{2,130},{3,131},{66,194},{67,195... | collective-permute-start | bytes 786440 | tf_op jit(solution)/shard_map/ppermute | solution.py:30
  16.7 13.6 %all_to_all.15.met_ref = bf16[8,64,384]{2,1,0:T(8,128)(2,1)S(1)} all-to-all(bf16[8,64,384]{2,1,0:T(8,128)(2,1)S(1)} %get-tuple-element.29), channel_id=1, replica_groups=mesh['xhi'=2,'xlo'=2,'zlo'=2,'y'=8,'zhi'=4,'core'=2] {'xhi','xlo','zlo'}, dimensions={0} | all-to-all | bytes 786432 | tf_op jit(solution)/shard_map/all_to_all | solution.py:363
  30.4 5.0 %collective-permute-start.1 = (bf16[4,64,384]{2,1,0:T(8,128)(2,1)S(1)}, bf16[4,64,384]{2,1,0:T(8,128)(2,1)S(1)}, u32[]{:S(2)}, u32[]{:S(2)}) collective-permute-start(bf16[4,64,384]{2,1,0:T(8,128)(2,1)S(1)} %get-tuple-element.31), channel_id=1, source_target_pairs={{0,1},{1,0},{64,65},{65,64},{2,3},{3,2},{66,67},{67,66},{4,5},{5,4... | collective-permute-start | bytes 589832 | tf_op jit(solution)/shard_map/ppermute | solution.py:30
  35.3 1.0 collective-permute-done.1
  36.4 3.0 %collective-permute-start.5 = (bf16[2,4,64,384]{3,2,1,0:T(8,128)(2,1)S(1)}, bf16[2,4,64,384]{3,2,1,0:T(8,128)(2,1)S(1)}, u32[]{:S(2)}, u32[]{:S(2)}) collective-permute-start(bf16[2,4,64,384]{3,2,1,0:T(8,128)(2,1)S(1)} %pad_maximum_fusion.refs_0_), channel_id=1, source_target_pairs={{0,8},{1,9},{64,72},{65,73},{2,10},{3,11},{66,74},{67,75},{4,12},{... | collective-permute-start | bytes 1179656 | tf_op jit(solution)/shard_map/ppermute | solution.py:30
  39.5 3.8 %collective-permute-start.2 = (bf16[2,4,64,384]{3,2,1,0:T(8,128)(2,1)S(1)}, bf16[2,4,64,384]{3,2,1,0:T(8,128)(2,1)S(1)}, u32[]{:S(2)}, u32[]{:S(2)}) collective-permute-start(bf16[2,4,64,384]{3,2,1,0:T(8,128)(2,1)S(1)} %pad_maximum_fusion.refs_0_), channel_id=1, source_target_pairs={{0,56},{1,57},{64,120},{65,121},{2,58},{3,59},{66,122},{67,123},{4... | collective-permute-start | bytes 1179656 | tf_op jit(solution)/shard_map/ppermute | solution.py:30
  43.3 7.3 %collective-permute-done.5.refs_6_ = bf16[2,4,64,384]{3,2,1,0:T(8,128)(2,1)S(1)} collective-permute-done((bf16[2,4,64,384]{3,2,1,0:T(8,128)(2,1)S(1)}, bf16[2,4,64,384]{3,2,1,0:T(8,128)(2,1)S(1)}, u32[]{:S(2)}, u32[]{:S(2)}) %collective-permute-start.5) | collective-permute-done | bytes 393248 | tf_op jit(solution)/shard_map/ppermute | solution.py:30
  50.6 1.9 %collective-permute-start.6 = (bf16[2,4,64,384]{3,2,1,0:T(8,128)(2,1)S(1)}, bf16[2,4,64,384]{3,2,1,0:T(8,128)(2,1)S(1)}, u32[]{:S(2)}, u32[]{:S(2)}) collective-permute-start(bf16[2,4,64,384]{3,2,1,0:T(8,128)(2,1)S(1)} %collective-permute-done.5.refs_6_), channel_id=1, source_target_pairs={{0,8},{1,9},{64,72},{65,73},{2,10},{3,11},{66,74},{67,75},{4,12},{... | collective-permute-start | bytes 1179656 | tf_op jit(solution)/shard_map/ppermute | solution.py:30
  52.6 4.6 %collective-permute-start.3 = (bf16[2,4,64,384]{3,2,1,0:T(8,128)(2,1)S(1)}, bf16[2,4,64,384]{3,2,1,0:T(8,128)(2,1)S(1)}, u32[]{:S(2)}, u32[]{:S(2)}) collective-permute-start(bf16[2,4,64,384]{3,2,1,0:T(8,128)(2,1)S(1)} %collective-permute-done.2.refs_1_), channel_id=1, source_target_pairs={{0,56},{1,57},{64,120},{65,121},{2,58},{3,59},{66,122},{67,123},{4... | collective-permute-start | bytes 1179656 | tf_op jit(solution)/shard_map/ppermute | solution.py:30
  57.2 6.5 %collective-permute-done.6.refs_5_ = bf16[2,4,64,384]{3,2,1,0:T(8,128)(2,1)S(1)} collective-permute-done((bf16[2,4,64,384]{3,2,1,0:T(8,128)(2,1)S(1)}, bf16[2,4,64,384]{3,2,1,0:T(8,128)(2,1)S(1)}, u32[]{:S(2)}, u32[]{:S(2)}) %collective-permute-start.6) | collective-permute-done | bytes 393248 | tf_op jit(solution)/shard_map/ppermute | solution.py:30
  63.7 1.9 %collective-permute-start.7 = (bf16[2,4,64,384]{3,2,1,0:T(8,128)(2,1)S(1)}, bf16[2,4,64,384]{3,2,1,0:T(8,128)(2,1)S(1)}, u32[]{:S(2)}, u32[]{:S(2)}) collective-permute-start(bf16[2,4,64,384]{3,2,1,0:T(8,128)(2,1)S(1)} %collective-permute-done.6.refs_5_), channel_id=1, source_target_pairs={{0,8},{1,9},{64,72},{65,73},{2,10},{3,11},{66,74},{67,75},{4,12},{... | collective-permute-start | bytes 1179656 | tf_op jit(solution)/shard_map/ppermute | solution.py:30
  65.6 4.6 %collective-permute-start.4 = (bf16[2,4,64,384]{3,2,1,0:T(8,128)(2,1)S(1)}, bf16[2,4,64,384]{3,2,1,0:T(8,128)(2,1)S(1)}, u32[]{:S(2)}, u32[]{:S(2)}) collective-permute-start(bf16[2,4,64,384]{3,2,1,0:T(8,128)(2,1)S(1)} %collective-permute-done.3.refs_2_), channel_id=1, source_target_pairs={{0,56},{1,57},{64,120},{65,121},{2,58},{3,59},{66,122},{67,123},{4... | collective-permute-start | bytes 1179656 | tf_op jit(solution)/shard_map/ppermute | solution.py:30
  70.2 5.7 %collective-permute-done.7.refs_4_ = bf16[2,4,64,384]{3,2,1,0:T(8,128)(2,1)S(1)} collective-permute-done((bf16[2,4,64,384]{3,2,1,0:T(8,128)(2,1)S(1)}, bf16[2,4,64,384]{3,2,1,0:T(8,128)(2,1)S(1)}, u32[]{:S(2)}, u32[]{:S(2)}) %collective-permute-start.7) | collective-permute-done | bytes 393248 | tf_op jit(solution)/shard_map/ppermute | solution.py:30
  76.0 1.9 %collective-permute-start.8 = (bf16[2,4,64,384]{3,2,1,0:T(8,128)(2,1)S(1)}, bf16[2,4,64,384]{3,2,1,0:T(8,128)(2,1)S(1)}, u32[]{:S(2)}, u32[]{:S(2)}) collective-permute-start(bf16[2,4,64,384]{3,2,1,0:T(8,128)(2,1)S(1)} %collective-permute-done.7.refs_4_), channel_id=1, source_target_pairs={{0,8},{1,9},{64,72},{65,73},{2,10},{3,11},{66,74},{67,75},{4,12},{... | collective-permute-start | bytes 1179656 | tf_op jit(solution)/shard_map/ppermute | solution.py:30
  77.9 4.3 %collective-permute-start.9 = (bf16[32,384]{1,0:T(8,128)(2,1)S(1)}, bf16[32,384]{1,0:T(8,128)(2,1)S(1)}, u32[]{:S(2)}, u32[]{:S(2)}) collective-permute-start(bf16[32,384]{1,0:T(8,128)(2,1)S(1)} %get-tuple-element.32.up), channel_id=1, source_target_pairs={{0,1},{1,0},{64,65},{65,64},{2,3},{3,2},{66,67},{67,66},{4,5},{5,4... | collective-permute-start | bytes 73736 | tf_op jit(solution)/shard_map/ppermute | solution.py:30
  83.0 3.4 %pack_weights.1.packed = bf16[3,2048,256]{2,1,0:T(8,128)(2,1)} custom-call(bf16[2,4,64,384]{3,2,1,0:T(8,128)(2,1)} %copy-done.11, bf16[2,4,64,384]{3,2,1,0:T(8,128)(2,1)} %copy-done.13, bf16[2,4,64,384]{3,2,1,0:T(8,128)(2,1)} %copy-done.16, bf16[2,4,64,384]{3,2,1,0:T(8,128)(2,1)} %copy-done.17, bf16[2,4,64,384]{3,2,1,0:T(8,128)(2,1)} %copy-done.15, ...), custom_call_target="tpu_custom_call" | custom-call | tf_op jit(solution)/shard_map/pack_weights/pallas_call | solution.py:318
  86.5 2.3 %copy-done = bf16[4352,512]{1,0:T(8,128)(2,1)S(1)} copy-done((bf16[4352,512]{1,0:T(8,128)(2,1)S(1)}, bf16[4352,512]{1,0:T(8,128)(2,1)}, u32[]{:S(2)}) %copy-start) | copy-done | bytes 4456472
  88.7 1.2 low_rank.1.low_ref
  91.0 1.9 %copy-done.2 = bf16[3,2048,256]{2,1,0:T(8,128)(2,1)S(1)} copy-done((bf16[3,2048,256]{2,1,0:T(8,128)(2,1)S(1)}, bf16[3,2048,256]{2,1,0:T(8,128)(2,1)}, u32[]{:S(2)}) %copy-start.2) | copy-done | bytes 3145752
  92.9 4.0 %project.1 = (f32[4,256,256]{2,1,0:T(8,128)S(1)}, bf16[4,256,256]{2,1,0:T(8,128)(2,1)S(1)}, f32[4,256,128]{2,1,0:T(8,128)S(1)}, bf16[4,256,128]{2,1,0:T(8,128)(2,1)S(1)}) custom-call(bf16[8,544,512]{2,1,0:T(8,128)(2,1)S(1)} %bitcast.15, bf16[3,2048,256]{2,1,0:T(8,128)(2,1)S(1)} %copy-done.2, bf16[2,4,64,384]{3,2,1,0:T(8,128)(2,1)S(1)} %collective-permute-done.8.last, ...), custom_call_target="tpu_custom_call" | custom-call | tf_op jit(solution)/shard_map/project/pallas_call | solution.py:318
  96.9 1.9 %collective-permute-start.10 = (bf16[4,256,256]{2,1,0:T(8,128)(2,1)S(1)}, bf16[4,256,256]{2,1,0:T(8,128)(2,1)S(1)}, u32[]{:S(2)}, u32[]{:S(2)}) collective-permute-start(bf16[4,256,256]{2,1,0:T(8,128)(2,1)S(1)} %get-tuple-element.34), channel_id=1, source_target_pairs={{0,1},{1,0},{64,65},{65,64},{2,3},{3,2},{66,67},{67,66},{4,5},{5,4... | collective-permute-start | bytes 1572872 | tf_op jit(solution)/shard_map/ppermute | solution.py:30
  99.5 1.2 collective-permute-done.10.met_ref
  100.8 1.9 %collective-permute-start.12 = (bf16[4,2,128,128]{3,2,1,0:T(8,128)(2,1)S(1)}, bf16[4,2,128,128]{3,2,1,0:T(8,128)(2,1)S(1)}, u32[]{:S(2)}, u32[]{:S(2)}) collective-permute-start(bf16[4,2,128,128]{3,2,1,0:T(8,128)(2,1)S(1)} %combine_kv.1.kv_ref), channel_id=1, source_target_pairs={{0,8},{1,9},{64,72},{65,73},{2,10},{3,11},{66,74},{67,75},{4,12},{... | collective-permute-start | bytes 786440 | tf_op jit(solution)/shard_map/ppermute | solution.py:30
  102.8 2.5 %conv_own.1.part_ref = f32[4,2,128,128]{3,2,1,0:T(8,128)S(1)} custom-call(bf16[4,2,128,128]{3,2,1,0:T(8,128)(2,1)S(1)} %combine_kv.1.kv_ref, bf16[512,128]{1,0:T(8,128)(2,1)S(1)} %copy-done.3), custom_call_target="tpu_custom_call" | custom-call | tf_op jit(solution)/shard_map/conv_own/pallas_call | solution.py:318
  105.3 2.0 %collective-permute-start.11 = (bf16[4,256,128]{2,1,0:T(8,128)(2,1)S(1)}, bf16[4,256,128]{2,1,0:T(8,128)(2,1)S(1)}, u32[]{:S(2)}, u32[]{:S(2)}) collective-permute-start(bf16[4,256,128]{2,1,0:T(8,128)(2,1)S(1)} %get-tuple-element.39), channel_id=1, source_target_pairs={{0,1},{1,0},{64,65},{65,64},{2,3},{3,2},{66,67},{67,66},{4,5},{5,4... | collective-permute-start | bytes 786440 | tf_op jit(solution)/shard_map/ppermute | solution.py:30
  108.7 3.5 %collective-permute-done.12.prev_ref = bf16[4,2,128,128]{3,2,1,0:T(8,128)(2,1)S(1)} collective-permute-done((bf16[4,2,128,128]{3,2,1,0:T(8,128)(2,1)S(1)}, bf16[4,2,128,128]{3,2,1,0:T(8,128)(2,1)S(1)}, u32[]{:S(2)}, u32[]{:S(2)}) %collective-permute-start.12) | collective-permute-done | bytes 262176 | tf_op jit(solution)/shard_map/ppermute | solution.py:30
  112.2 3.3 %gate_most.1.most_ref = f32[64,128]{1,0:T(8,128)S(1)} custom-call(s32[2,32]{1,0:T(2,128)S(1)} %copy-done.9, f32[4,2,128,128]{3,2,1,0:T(8,128)S(1)} %conv_own.1.part_ref, f32[4,256,128]{2,1,0:T(8,128)S(1)} %get-tuple-element.38.own_ref, bf16[4,256,128]{2,1,0:T(8,128)(2,1)S(1)} %collective-permute-done.11.met_ref, ...), custom_call_target="tpu_custom_call" | custom-call | tf_op jit(solution)/shard_map/gate_most/pallas_call | solution.py:318
  115.5 1.5 gate_first.1
  117.1 13.2 %all_to_all.16.met_ref = bf16[8,64,128]{2,1,0:T(8,128)(2,1)S(1)} all-to-all(bf16[8,64,128]{2,1,0:T(8,128)(2,1)S(1)} %gate_first.1), channel_id=1, replica_groups=mesh['xhi'=2,'xlo'=2,'zlo'=2,'y'=8,'zhi'=4,'core'=2] {'y'}, dimensions={0} | all-to-all | bytes 262144 | tf_op jit(solution)/shard_map/all_to_all | solution.py:439
  130.3 22.5 %all_to_all.17 = bf16[64,8,128]{2,1,0:T(8,128)(2,1)S(1)} all-to-all(bf16[64,8,128]{2,1,0:T(8,128)(2,1)S(1)} %bitcast.16), channel_id=1, replica_groups=mesh['xhi'=2,'xlo'=2,'zlo'=2,'y'=8,'zhi'=4,'core'=2] {'zhi','core','xhi'..., dimensions={0} | all-to-all | bytes 262144 | tf_op jit(solution)/shard_map/all_to_all | solution.py:442
  152.7 1.2 copy-done.4
  154.0 1.4 embed.1
  (59 shorter events, 10.2 us)
Async XLA Ops:
  6.5 79.9 %all-gather.6.cloned.1.call-start = ((), (), s32[]{:S(2)}) async-start(), calls=%async_computation.4 | async-start | bytes 5013504 | tf_op jit(solution)/shard_map/all_gather | solution.py:360
  6.5 9.2 %collective-permute-start = (bf16[256,512]{1,0:T(8,128)(2,1)}, bf16[256,512]{1,0:T(8,128)(2,1)S(1)}, u32[]{:S(2)}, u32[]{:S(2)}) collective-permute-start(bf16[256,512]{1,0:T(8,128)(2,1)} %bitcast.19), channel_id=1, source_target_pairs={{0,128},{1,129},{64,192},{65,193},{2,130},{3,131},{66,194},{67,195... | collective-permute-start | bytes 786440 | tf_op jit(solution)/shard_map/ppermute | solution.py:30
  10.5 1.0 copy-start.6
  11.4 0.9 copy-start.7
  12.4 1.0 copy-start.5
  16.7 136.1 %all-gather.4.cloned.1.call-start = ((), (), s32[]{:S(2)}) async-start(), calls=%async_computation.3 | async-start | bytes 1179648 | tf_op jit(solution)/shard_map/all_gather | solution.py:405
  30.4 6.0 %collective-permute-start.1 = (bf16[4,64,384]{2,1,0:T(8,128)(2,1)S(1)}, bf16[4,64,384]{2,1,0:T(8,128)(2,1)S(1)}, u32[]{:S(2)}, u32[]{:S(2)}) collective-permute-start(bf16[4,64,384]{2,1,0:T(8,128)(2,1)S(1)} %get-tuple-element.31), channel_id=1, source_target_pairs={{0,1},{1,0},{64,65},{65,64},{2,3},{3,2},{66,67},{67,66},{4,5},{5,4... | collective-permute-start | bytes 589832 | tf_op jit(solution)/shard_map/ppermute | solution.py:30
  36.4 45.7 %copy-start.11 = (bf16[2,4,64,384]{3,2,1,0:T(8,128)(2,1)}, bf16[2,4,64,384]{3,2,1,0:T(8,128)(2,1)S(1)}, u32[]{:S(2)}) copy-start(bf16[2,4,64,384]{3,2,1,0:T(8,128)(2,1)S(1)} %pad_maximum_fusion.refs_0_) | copy-start | bytes 1179652
  36.4 14.2 %collective-permute-start.5 = (bf16[2,4,64,384]{3,2,1,0:T(8,128)(2,1)S(1)}, bf16[2,4,64,384]{3,2,1,0:T(8,128)(2,1)S(1)}, u32[]{:S(2)}, u32[]{:S(2)}) collective-permute-start(bf16[2,4,64,384]{3,2,1,0:T(8,128)(2,1)S(1)} %pad_maximum_fusion.refs_0_), channel_id=1, source_target_pairs={{0,8},{1,9},{64,72},{65,73},{2,10},{3,11},{66,74},{67,75},{4,12},{... | collective-permute-start | bytes 1179656 | tf_op jit(solution)/shard_map/ppermute | solution.py:30
  39.5 13.1 %collective-permute-start.2 = (bf16[2,4,64,384]{3,2,1,0:T(8,128)(2,1)S(1)}, bf16[2,4,64,384]{3,2,1,0:T(8,128)(2,1)S(1)}, u32[]{:S(2)}, u32[]{:S(2)}) collective-permute-start(bf16[2,4,64,384]{3,2,1,0:T(8,128)(2,1)S(1)} %pad_maximum_fusion.refs_0_), channel_id=1, source_target_pairs={{0,56},{1,57},{64,120},{65,121},{2,58},{3,59},{66,122},{67,123},{4... | collective-permute-start | bytes 1179656 | tf_op jit(solution)/shard_map/ppermute | solution.py:30
  50.6 31.5 %copy-start.12 = (bf16[2,4,64,384]{3,2,1,0:T(8,128)(2,1)}, bf16[2,4,64,384]{3,2,1,0:T(8,128)(2,1)S(1)}, u32[]{:S(2)}) copy-start(bf16[2,4,64,384]{3,2,1,0:T(8,128)(2,1)S(1)} %collective-permute-done.5.refs_6_) | copy-start | bytes 1179652
  50.6 13.1 %collective-permute-start.6 = (bf16[2,4,64,384]{3,2,1,0:T(8,128)(2,1)S(1)}, bf16[2,4,64,384]{3,2,1,0:T(8,128)(2,1)S(1)}, u32[]{:S(2)}, u32[]{:S(2)}) collective-permute-start(bf16[2,4,64,384]{3,2,1,0:T(8,128)(2,1)S(1)} %collective-permute-done.5.refs_6_), channel_id=1, source_target_pairs={{0,8},{1,9},{64,72},{65,73},{2,10},{3,11},{66,74},{67,75},{4,12},{... | collective-permute-start | bytes 1179656 | tf_op jit(solution)/shard_map/ppermute | solution.py:30
  52.6 29.6 %copy-start.13 = (bf16[2,4,64,384]{3,2,1,0:T(8,128)(2,1)}, bf16[2,4,64,384]{3,2,1,0:T(8,128)(2,1)S(1)}, u32[]{:S(2)}) copy-start(bf16[2,4,64,384]{3,2,1,0:T(8,128)(2,1)S(1)} %collective-permute-done.2.refs_1_) | copy-start | bytes 1179652
  52.6 13.0 %collective-permute-start.3 = (bf16[2,4,64,384]{3,2,1,0:T(8,128)(2,1)S(1)}, bf16[2,4,64,384]{3,2,1,0:T(8,128)(2,1)S(1)}, u32[]{:S(2)}, u32[]{:S(2)}) collective-permute-start(bf16[2,4,64,384]{3,2,1,0:T(8,128)(2,1)S(1)} %collective-permute-done.2.refs_1_), channel_id=1, source_target_pairs={{0,56},{1,57},{64,120},{65,121},{2,58},{3,59},{66,122},{67,123},{4... | collective-permute-start | bytes 1179656 | tf_op jit(solution)/shard_map/ppermute | solution.py:30
  63.7 18.5 %copy-start.14 = (bf16[2,4,64,384]{3,2,1,0:T(8,128)(2,1)}, bf16[2,4,64,384]{3,2,1,0:T(8,128)(2,1)S(1)}, u32[]{:S(2)}) copy-start(bf16[2,4,64,384]{3,2,1,0:T(8,128)(2,1)S(1)} %collective-permute-done.6.refs_5_) | copy-start | bytes 1179652
  63.7 12.2 %collective-permute-start.7 = (bf16[2,4,64,384]{3,2,1,0:T(8,128)(2,1)S(1)}, bf16[2,4,64,384]{3,2,1,0:T(8,128)(2,1)S(1)}, u32[]{:S(2)}, u32[]{:S(2)}) collective-permute-start(bf16[2,4,64,384]{3,2,1,0:T(8,128)(2,1)S(1)} %collective-permute-done.6.refs_5_), channel_id=1, source_target_pairs={{0,8},{1,9},{64,72},{65,73},{2,10},{3,11},{66,74},{67,75},{4,12},{... | collective-permute-start | bytes 1179656 | tf_op jit(solution)/shard_map/ppermute | solution.py:30
  65.6 16.6 %copy-start.16 = (bf16[2,4,64,384]{3,2,1,0:T(8,128)(2,1)}, bf16[2,4,64,384]{3,2,1,0:T(8,128)(2,1)S(1)}, u32[]{:S(2)}) copy-start(bf16[2,4,64,384]{3,2,1,0:T(8,128)(2,1)S(1)} %collective-permute-done.3.refs_2_) | copy-start | bytes 1179652
  65.6 16.5 %collective-permute-start.4 = (bf16[2,4,64,384]{3,2,1,0:T(8,128)(2,1)S(1)}, bf16[2,4,64,384]{3,2,1,0:T(8,128)(2,1)S(1)}, u32[]{:S(2)}, u32[]{:S(2)}) collective-permute-start(bf16[2,4,64,384]{3,2,1,0:T(8,128)(2,1)S(1)} %collective-permute-done.3.refs_2_), channel_id=1, source_target_pairs={{0,56},{1,57},{64,120},{65,121},{2,58},{3,59},{66,122},{67,123},{4... | collective-permute-start | bytes 1179656 | tf_op jit(solution)/shard_map/ppermute | solution.py:30
  76.0 6.3 %copy-start.15 = (bf16[2,4,64,384]{3,2,1,0:T(8,128)(2,1)}, bf16[2,4,64,384]{3,2,1,0:T(8,128)(2,1)S(1)}, u32[]{:S(2)}) copy-start(bf16[2,4,64,384]{3,2,1,0:T(8,128)(2,1)S(1)} %collective-permute-done.7.refs_4_) | copy-start | bytes 1179652
  76.0 14.0 %collective-permute-start.8 = (bf16[2,4,64,384]{3,2,1,0:T(8,128)(2,1)S(1)}, bf16[2,4,64,384]{3,2,1,0:T(8,128)(2,1)S(1)}, u32[]{:S(2)}, u32[]{:S(2)}) collective-permute-start(bf16[2,4,64,384]{3,2,1,0:T(8,128)(2,1)S(1)} %collective-permute-done.7.refs_4_), channel_id=1, source_target_pairs={{0,8},{1,9},{64,72},{65,73},{2,10},{3,11},{66,74},{67,75},{4,12},{... | collective-permute-start | bytes 1179656 | tf_op jit(solution)/shard_map/ppermute | solution.py:30
  77.9 12.1 %collective-permute-start.9 = (bf16[32,384]{1,0:T(8,128)(2,1)S(1)}, bf16[32,384]{1,0:T(8,128)(2,1)S(1)}, u32[]{:S(2)}, u32[]{:S(2)}) collective-permute-start(bf16[32,384]{1,0:T(8,128)(2,1)S(1)} %get-tuple-element.32.up), channel_id=1, source_target_pairs={{0,1},{1,0},{64,65},{65,64},{2,3},{3,2},{66,67},{67,66},{4,5},{5,4... | collective-permute-start | bytes 73736 | tf_op jit(solution)/shard_map/ppermute | solution.py:30
  86.5 2.3 %copy-start = (bf16[4352,512]{1,0:T(8,128)(2,1)S(1)}, bf16[4352,512]{1,0:T(8,128)(2,1)}, u32[]{:S(2)}) copy-start(bf16[4352,512]{1,0:T(8,128)(2,1)} %all-gather.6.cloned.1.call-done) | copy-start | bytes 13369348
  88.7 2.3 %copy-start.1 = (bf16[4352,512]{1,0:T(8,128)(2,1)S(1)}, bf16[4352,512]{1,0:T(8,128)(2,1)}, u32[]{:S(2)}) copy-start(bf16[4352,512]{1,0:T(8,128)(2,1)} %all-gather.6.cloned.1.call-done) | copy-start | bytes 13369348
  88.7 10.1 %copy-start.18 = (bf16[512,64]{0,1:T(8,128)(2,1)S(1)}, bf16[512,64]{0,1:T(8,128)(2,1)}, u32[]{:S(2)}) copy-start(bf16[512,64]{0,1:T(8,128)(2,1)} %param.15) | copy-start | bytes 196612
  88.7 14.0 %copy-start.3 = (bf16[512,128]{1,0:T(8,128)(2,1)S(1)}, bf16[512,128]{1,0:T(8,128)(2,1)}, u32[]{:S(2)}) copy-start(bf16[512,128]{1,0:T(8,128)(2,1)} %filters_ref.5) | copy-start | bytes 393220
  88.7 23.5 %copy-start.9 = (s32[2,32]{1,0:T(2,128)S(1)}, s32[2,32]{1,0:T(2,128)}, u32[]{:S(2)}) copy-start(s32[2,32]{1,0:T(2,128)} %lengths.5) | copy-start | bytes 772
  91.0 1.9 %copy-start.2 = (bf16[3,2048,256]{2,1,0:T(8,128)(2,1)S(1)}, bf16[3,2048,256]{2,1,0:T(8,128)(2,1)}, u32[]{:S(2)}) copy-start(bf16[3,2048,256]{2,1,0:T(8,128)(2,1)} %pack_weights.1.packed) | copy-start | bytes 9437188
  96.9 3.8 %collective-permute-start.10 = (bf16[4,256,256]{2,1,0:T(8,128)(2,1)S(1)}, bf16[4,256,256]{2,1,0:T(8,128)(2,1)S(1)}, u32[]{:S(2)}, u32[]{:S(2)}) collective-permute-start(bf16[4,256,256]{2,1,0:T(8,128)(2,1)S(1)} %get-tuple-element.34), channel_id=1, source_target_pairs={{0,1},{1,0},{64,65},{65,64},{2,3},{3,2},{66,67},{67,66},{4,5},{5,4... | collective-permute-start | bytes 1572872 | tf_op jit(solution)/shard_map/ppermute | solution.py:30
  100.8 11.4 %collective-permute-start.12 = (bf16[4,2,128,128]{3,2,1,0:T(8,128)(2,1)S(1)}, bf16[4,2,128,128]{3,2,1,0:T(8,128)(2,1)S(1)}, u32[]{:S(2)}, u32[]{:S(2)}) collective-permute-start(bf16[4,2,128,128]{3,2,1,0:T(8,128)(2,1)S(1)} %combine_kv.1.kv_ref), channel_id=1, source_target_pairs={{0,8},{1,9},{64,72},{65,73},{2,10},{3,11},{66,74},{67,75},{4,12},{... | collective-permute-start | bytes 786440 | tf_op jit(solution)/shard_map/ppermute | solution.py:30
  105.3 3.4 %collective-permute-start.11 = (bf16[4,256,128]{2,1,0:T(8,128)(2,1)S(1)}, bf16[4,256,128]{2,1,0:T(8,128)(2,1)S(1)}, u32[]{:S(2)}, u32[]{:S(2)}) collective-permute-start(bf16[4,256,128]{2,1,0:T(8,128)(2,1)S(1)} %get-tuple-element.39), channel_id=1, source_target_pairs={{0,1},{1,0},{64,65},{65,64},{2,3},{3,2},{66,67},{67,66},{4,5},{5,4... | collective-permute-start | bytes 786440 | tf_op jit(solution)/shard_map/ppermute | solution.py:30
  107.3 8.2 %collective-permute-start.13 = (bf16[2,128,128]{2,1,0:T(8,128)(2,1)S(1)}, bf16[2,128,128]{2,1,0:T(8,128)(2,1)S(1)}, u32[]{:S(2)}, u32[]{:S(2)}) collective-permute-start(bf16[2,128,128]{2,1,0:T(8,128)(2,1)S(1)} %slice_bitcast_fusion), channel_id=1, source_target_pairs={{56,256},{57,257},{120,320},{121,321},{58,258},{59,259},{122,322},... | collective-permute-start | bytes 196616 | tf_op jit(solution)/shard_map/ppermute | solution.py:30
  152.7 1.2 copy-start.4
  (3 other events, 2.3 us)
Sparse Core Ops, SparseCore 0:
  16.8 67.1 all-gather.5
  100.9 34.3 all-gather.3
